TPU v7x, 32 devices: a whole 2x2x4 slice. The times are simulated.
32 devices in a mesh: seq: 8 (over y, x, core), tp: 4 (over z).
Axes of the slice: x: 2, y: 2, z: 4, core: 2. Of those that a mesh axis runs over, the one named last changes fastest.
Arguments:
- tokens: bfloat16 [4096, 5376], P(('seq', 'tp')), may hold values from -180 to 180
- in_gain: float32 [5376], replicated, may hold values from 0.5 to 1.5
- raw_queries: bfloat16 [4096, 2048], P('seq', 'tp'), may hold values from -6 to 6
- w_key: bfloat16 [5376, 1024], P(None, 'tp'), may hold values from -0.078125 to 0.078125
- w_value: bfloat16 [5376, 1024], P(None, 'tp'), may hold values from -0.078125 to 0.078125
- q_gain: float32 [128], replicated, may hold values from 0.5 to 1.5
- k_gain: float32 [128], replicated, may hold values from 0.5 to 1.5
- doc_lengths: int32 [4], replicated, may hold values from 1 to 2048, as said below
- out_grad: bfloat16 [4096, 2048], P('seq', 'tp'), may hold values from -60 to 60
Outputs:
- grad_x: bfloat16 [4096, 5376], P(('seq', 'tp'))
- grad_queries: bfloat16 [4096, 2048], P('seq', 'tp')
- grad_wk: float32 [5376, 1024], P('seq', 'tp')
- grad_wv: float32 [5376, 1024], P('seq', 'tp')
Inputs may be any that keep to these rules, and one draw needn't show every extreme that they name: `doc_lengths`: the 4 lengths sum to 4096; the last rollout is the longest, exactly 2048 tokens.
All inputs are finite; a program needn't handle non-finite values.
Results may differ from a plain program's by a relative error of at most 0.014.
Values may be sent and summed in bfloat16 or wider, within the bound.
No kernel may reach another device: no remote copies, remote signals or barrier semaphores. Data moves between devices by JAX's collectives and lax.ppermute only.
A program may use at most 128 MiB of HBM per device.

v0:
```python
import jax
import jax.numpy as jnp
from jax import lax
from jax.sharding import PartitionSpec as P

WINDOW = 1024


EPSILON = 1e-06
QUERY_SCALE = 168.0 ** (-0.5)
ROPE_BASE = 10000.0


def from_behind(array, axis, by):
    size = lax.axis_size(axis)
    pairs = [(i, i + by) for i in range(size) if 0 <= i + by < size]
    return lax.ppermute(array, axis, pairs)


def doc_begin(doc_lengths, positions):
    endings = jnp.cumsum(doc_lengths, dtype=jnp.int32)
    starts = endings - doc_lengths
    inside = starts[None, :] <= positions[:, None]
    return jnp.max(jnp.where(inside, starts[None, :], jnp.zeros_like(starts)[None, :]), axis=1)


def input_norm(values, gain):
    return values * lax.rsqrt(jnp.mean(values * values, axis=1, keepdims=True) + EPSILON) * gain


def head_norm(values, gain):
    return values * lax.rsqrt(jnp.mean(values * values, axis=-1, keepdims=True) + EPSILON) * gain


def rotate(values, positions):
    half_size = values.shape[-1] // 2
    powers = jnp.arange(half_size, dtype=jnp.float32) * (2.0 / values.shape[-1])
    frequency = ROPE_BASE ** (-powers)
    angles = positions.astype(jnp.float32)[:, None] * frequency[None, :]
    cosine = jnp.cos(angles)[:, None, :]
    sine = jnp.sin(angles)[:, None, :]
    first = values[..., :half_size]
    second = values[..., half_size:]
    return jnp.concatenate(
        [first * cosine - second * sine, second * cosine + first * sine], axis=-1
    )


def contract_last(left, right):
    return lax.dot_general(
        left, right, (((1,), (1,)), ((), ())), preferred_element_type=jnp.float32
    )


def contract_first(left, right):
    return lax.dot_general(
        left, right, (((0,), (0,)), ((), ())), preferred_element_type=jnp.float32
    )


def attend(queries, key_rows, value_rows, grads, lowest, positions, key_positions):
    scores = jnp.einsum("qkgd,skd->kgqs", queries, key_rows, preferred_element_type=jnp.float32)
    allowed = (key_positions[None, :] >= lowest[:, None]) & (
        key_positions[None, :] <= positions[:, None]
    )
    exps = jnp.where(allowed[None, None], jnp.exp(scores), jnp.zeros_like(scores))
    totals = jnp.sum(exps, axis=-1, keepdims=True)
    probs = exps / totals
    rounded = probs.astype(jnp.bfloat16)
    outputs = jnp.einsum("kgqs,skd->qkgd", rounded, value_rows, preferred_element_type=jnp.float32)
    deltas = jnp.sum(grads.astype(jnp.float32) * outputs, axis=-1)
    along = jnp.einsum("qkgd,skd->kgqs", grads, value_rows, preferred_element_type=jnp.float32)
    slopes = (probs * (along - jnp.transpose(deltas, (1, 2, 0))[..., None])).astype(jnp.bfloat16)
    query_grad = jnp.einsum("kgqs,skd->qkgd", slopes, key_rows, preferred_element_type=jnp.float32)
    key_grad = jnp.einsum("kgqs,qkgd->skd", slopes, queries, preferred_element_type=jnp.float32)
    value_grad = jnp.einsum("kgqs,qkgd->skd", rounded, grads, preferred_element_type=jnp.float32)
    return (query_grad, key_grad, value_grad)


def shards(tokens, in_gain, raw_queries, w_key, w_value, q_gain, k_gain, doc_lengths, out_grad):
    tp_count = lax.axis_size("tp")
    head_size = q_gain.shape[0]
    kv_heads = w_key.shape[1] // head_size
    group_size = raw_queries.shape[1] // w_key.shape[1]
    shard_rows = tokens.shape[0] * tp_count
    reach_count = (WINDOW - 2) // shard_rows + 1
    x_float = tokens.astype(jnp.float32)
    normed_rows = input_norm(x_float, in_gain).astype(jnp.bfloat16)
    gathered = lax.all_gather(normed_rows, "tp", axis=0, tiled=True)
    first_row = lax.axis_index("seq") * shard_rows
    positions = first_row + jnp.arange(shard_rows, dtype=jnp.int32)
    begins = doc_begin(doc_lengths, positions)
    offsets = positions - begins
    lowest = jnp.maximum(begins, positions - (WINDOW - 1))
    queries = raw_queries.astype(jnp.float32).reshape(shard_rows, -1, head_size)
    keys_raw = jnp.dot(gathered, w_key, preferred_element_type=jnp.float32).reshape(
        shard_rows, -1, head_size
    )
    values_raw = jnp.dot(gathered, w_value, preferred_element_type=jnp.float32).reshape(
        shard_rows, -1, head_size
    )

    def query_map(values):
        return rotate(head_norm(values, q_gain), offsets) * QUERY_SCALE

    def key_map(values):
        return rotate(head_norm(values, k_gain), offsets)

    query_rot, query_back = jax.vjp(query_map, queries)
    key_rot, key_back = jax.vjp(key_map, keys_raw)
    query_rows = query_rot.astype(jnp.bfloat16).reshape(shard_rows, kv_heads, group_size, head_size)
    key_rows = key_rot.astype(jnp.bfloat16)
    value_rows = values_raw.astype(jnp.bfloat16)
    grad_rows = out_grad.reshape(shard_rows, kv_heads, group_size, head_size)
    rim_keys = []
    rim_values = []
    for distance in range(reach_count, 0, -1):
        far_keys, far_values = from_behind((key_rows, value_rows), "seq", distance)
        rim_keys.append(far_keys)
        rim_values.append(far_values)
    key_window = jnp.concatenate(rim_keys + [key_rows], axis=0)
    value_window = jnp.concatenate(rim_values + [value_rows], axis=0)
    key_positions = (
        first_row
        - reach_count * shard_rows
        + jnp.arange((reach_count + 1) * shard_rows, dtype=jnp.int32)
    )
    query_grad, key_grad_all, value_grad_all = attend(
        query_rows, key_window, value_window, grad_rows, lowest, positions, key_positions
    )
    own_start = reach_count * shard_rows
    carried = (key_grad_all[0:shard_rows], value_grad_all[0:shard_rows])
    arrived = carried
    for section_index in range(1, reach_count + 1):
        arrived = (
            from_behind(carried[0].astype(jnp.bfloat16), "seq", -1).astype(jnp.float32),
            from_behind(carried[1].astype(jnp.bfloat16), "seq", -1).astype(jnp.float32),
        )
        if section_index < reach_count:
            lower_row = section_index * shard_rows
            carried = (
                arrived[0] + key_grad_all[lower_row : lower_row + shard_rows],
                arrived[1] + value_grad_all[lower_row : lower_row + shard_rows],
            )
    key_grad = key_grad_all[own_start:] + arrived[0]
    value_grad = value_grad_all[own_start:] + arrived[1]
    query_grad = query_grad.reshape(shard_rows, kv_heads * group_size, head_size)
    grad_queries = query_back(query_grad)[0].reshape(shard_rows, -1).astype(jnp.bfloat16)
    grad_k = key_back(key_grad)[0].reshape(shard_rows, -1).astype(jnp.bfloat16)
    grad_v = value_grad.reshape(shard_rows, -1).astype(jnp.bfloat16)
    partial_sum = contract_last(grad_k, w_key) + contract_last(grad_v, w_value)
    normed_grad = lax.psum_scatter(
        partial_sum.astype(jnp.bfloat16), "tp", scatter_dimension=0, tiled=True
    ).astype(jnp.float32)

    def norm_map(values):
        return input_norm(values, in_gain)

    unused_rows, norm_back = jax.vjp(norm_map, x_float)
    grad_x = norm_back(normed_grad)[0].astype(jnp.bfloat16)
    grads_joined = jnp.concatenate([grad_k, grad_v], axis=1)
    weight_term = contract_first(gathered, grads_joined)
    summed = lax.psum_scatter(weight_term, "seq", scatter_dimension=0, tiled=True)
    kv_cols = w_key.shape[1]
    grad_wk = summed[:, :kv_cols]
    grad_wv = summed[:, kv_cols:]
    return (grad_x, grad_queries, grad_wk, grad_wv)


def solution(mesh):
    placed = (
        P(("seq", "tp"), None),
        P(),
        P("seq", "tp"),
        P(None, "tp"),
        P(None, "tp"),
        P(),
        P(),
        P(),
        P("seq", "tp"),
    )
    return jax.shard_map(
        shards,
        mesh=mesh,
        in_specs=placed,
        out_specs=(P(("seq", "tp"), None), P("seq", "tp"), P("seq", "tp"), P("seq", "tp")),
        check_vma=False,
    )
```

profile of v0, /device:TPU:0, one launch (start us, length us, event | category | flops | bytes accessed | tf_op | source)
XLA Modules:
  0.0 387.9 jit_solution(4661587953850697452)
XLA Ops:
  10.2 2.8 fusion.8
  24.1 2.8 fusion.13
  28.5 89.8 %all-gather.2.cloned.1.call-done = bf16[512,5376]{1,0:T(8,128)(2,1)} async-done(((bf16[128,5376]{1,0:T(8,128)(2,1)}), bf16[512,5376]{1,0:T(8,128)(2,1)}) %all-gather.2.cloned.1.call-update) | async-done | bytes 5505040 | tf_op jit(solution)/shard_map/all_gather | solution.py:89
  118.3 5.0 %multiply_reduce_fusion.3 = (f32[512,2]{0,1:T(2,128)S(1)}, f32[512,256]{0,1:T(8,128)}) fusion(bf16[512,5376]{1,0:T(8,128)(2,1)} %all-gather.2.cloned.1.call-done, bf16[5376,256]{1,0:T(8,128)(2,1)S(1)} %copy-done), kind=kOutput, calls=%fused_computation.64 | convolution fusion | flops 1409547264 | bytes 8785920 | tf_op jit(solution)/shard_map/dot_general | solution.py:96
  128.3 4.1 %collective-permute-start = (bf16[512,2,128]{2,0,1:T(8,128)(2,1)}, bf16[512,2,128]{2,0,1:T(8,128)(2,1)}, u32[]{:S(2)}, u32[]{:S(2)}) collective-permute-start(bf16[512,2,128]{2,0,1:T(8,128)(2,1)} %pad_maximum_fusion), channel_id=1, source_target_pairs={{0,8},{4,12},{8,16},{12,20},{16,24},{20,28},{1,9},{5,13},{9,17},{1... | collective-permute-start | bytes 786440 | tf_op jit(solution)/shard_map/ppermute | solution.py:17
  132.4 2.4 collective-permute-start.1
  134.8 4.9 %convolution_convert_fusion = bf16[512,256]{0,1:T(8,128)(2,1)} fusion(bf16[512,5376]{1,0:T(8,128)(2,1)} %all-gather.2.cloned.1.call-done, bf16[5376,256]{1,0:T(8,128)(2,1)S(1)} %copy-done.11), kind=kOutput, calls=%fused_computation.27 | convolution fusion | flops 1409417216 | bytes 8519680 | tf_op jit(solution)/shard_map/dot_general | solution.py:99
  141.4 2.4 collective-permute-start.2
  143.8 3.4 collective-permute-start.3
  147.3 5.0 %fusion.3 = (f32[2,2,512]{2,1,0:T(2,128)S(1)}, f32[2,1536,512,2]{2,1,3,0:T(8,128)S(1)}) fusion(pred[512,1536]{0,1:T(8,128)(4,1)} %compare_and_fusion, bf16[512,2,2,128]{3,0,2,1:T(8,128)(2,1)} %fusion.13, bf16[512,2,64]{2,0,1:T(8,128)(2,1)} %copy-done.19, bf16[512,2,64]{2,0,1:T(8,128)(2,1)} %copy-done.17, bf16[512,2,128]{2,0,1:T(8,128)(2,1)} %collective-permute-done.1, ...), kind=kOutput, calls=%fused_computation.5 | convolution fusion | flops 814741504 | bytes 14688256 | tf_op jit(solution)/shard_map/qkgd,skd->kgqs/dot_general | solution.py:62
  155.6 6.9 %fusion.1 = bf16[2,2,512,1536]{2,3,1,0:T(8,128)(2,1)} fusion(bf16[512,2,2,128]{0,3,2,1:T(8,128)(2,1)S(1)} %bitcast.94, f32[2,2,512]{2,1,0:T(2,128)S(1)} %bitcast.102, f32[2,2,512]{2,1,0:T(2,128)S(1)} %get-tuple-element.22, f32[2,1536,512,2]{2,1,3,0:T(8,128)S(1)} %get-tuple-element.23, pred[512,1536]{0,1:T(8,128)(4,1)S(1)} %copy-done.10, ...), kind=kOutput, calls=%fused_computation.2 | convolution fusion | flops 823394304 | bytes 20987904 | tf_op jit(solution)/shard_map/qkgd,skd->kgqs/dot_general | solution.py:72
  162.5 4.6 %convolution_bitcast_fusion = f32[1536,2,128]{2,0,1:T(8,128)S(1)} fusion(bf16[2,2,512,1536]{2,3,1,0:T(8,128)(2,1)} %fusion.1, bf16[512,2,2,128]{3,0,2,1:T(8,128)(2,1)S(1)} %copy-done.15), kind=kOutput, calls=%fused_computation.20 | convolution fusion | flops 805306368 | bytes 8388608 | tf_op jit(solution)/shard_map/kgqs,qkgd->skd/dot_general | solution.py:75
  168.4 2.1 convolution_bitcast_fusion.1
  184.8 4.1 %add_convert_fusion = bf16[512,5376]{1,0:T(8,128)(2,1)} fusion(f32[512,5376]{1,0:T(8,128)S(1)} %fusion.33, bf16[512,256]{0,1:T(8,128)(2,1)S(1)} %bitcast.89, bf16[5376,256]{1,0:T(8,128)(2,1)S(1)} %copy-done.12), kind=kOutput, calls=%fused_computation.6 | convolution fusion | flops 1414791168 | bytes 19529728 | tf_op jit(solution)/shard_map/dot_general | solution.py:50
  189.0 8.8 %fusion.18 = f32[5376,512]{1,0:T(8,128)} fusion(bf16[512,5376]{1,0:T(8,128)(2,1)} %all-gather.2.cloned.1.call-done, bf16[512,256]{0,1:T(8,128)(2,1)S(1)} %bitcast.90, bf16[512,256]{0,1:T(8,128)(2,1)S(1)} %bitcast.92), kind=kOutput, calls=%fused_computation.53 | convolution fusion | flops 2819620864 | bytes 17039360 | tf_op jit(solution)/shard_map/dot_general | solution.py:56
  199.0 4.4 %convolution_multiply_fusion = f32[2,128,2,512]{3,1,2,0:T(8,128)S(1)} fusion(bf16[2,2,512,1536]{2,3,1,0:T(8,128)(2,1)} %fusion.1, bf16[512,2,64]{2,0,1:T(8,128)(2,1)S(1)} %copy-done.20, bf16[512,2,64]{2,0,1:T(8,128)(2,1)S(1)} %copy-done.18, bf16[512,2,128]{2,0,1:T(8,128)(2,1)} %collective-permute-done.1, bf16[512,2,128]{2,0,1:T(8,128)(2,1)} %collective-permute-done), kind=kOutput, calls=%fused_computation.23 | convolution fusion | flops 808714240 | bytes 8126464 | tf_op jit(solution)/shard_map/kgqs,skd->qkgd/dot_general | solution.py:74
  204.4 2.4 copy.166
  206.8 2.4 copy.167
  209.1 2.3 multiply_add_fusion.1
  214.3 3.7 fusion.12
  218.9 71.8 %reduce-scatter.3.cloned.1.call-done = bf16[128,5376]{1,0:T(8,128)(2,1)} async-done(((bf16[512,5376]{1,0:T(8,128)(2,1)}), bf16[128,5376]{1,0:T(8,128)(2,1)}) %reduce-scatter.3.cloned.1.call-update) | async-done | bytes 1376272 | tf_op jit(solution)/shard_map/reduce_scatter | solution.py:152
  290.7 2.4 fusion.9
  295.1 83.8 %reduce-scatter.5.cloned.1.call-done = f32[672,512]{1,0:T(8,128)} async-done(((f32[5376,512]{1,0:T(8,128)}), f32[672,512]{1,0:T(8,128)}) %reduce-scatter.5.cloned.1.call-update) | async-done | bytes 1376272 | tf_op jit(solution)/shard_map/reduce_scatter | solution.py:163
  378.9 2.5 fusion.31
  (131 shorter events, 48.8 us)
Async XLA Ops:
  7.2 111.2 %copy-start = (bf16[5376,256]{1,0:T(8,128)(2,1)S(1)}, bf16[5376,256]{1,0:T(8,128)(2,1)}, u32[]{:S(2)}) copy-start(bf16[5376,256]{1,0:T(8,128)(2,1)} %param.12) | copy-start | bytes 8257540
  7.2 6.0 %copy-start.21 = (bf16[512,512]{1,0:T(8,128)(2,1)S(1)}, bf16[512,512]{1,0:T(8,128)(2,1)}, u32[]{:S(2)}) copy-start(bf16[512,512]{1,0:T(8,128)(2,1)} %param.11) | copy-start | bytes 1572868
  7.2 111.1 %all-gather.2.cloned.1.call-start = ((), (), s32[]{:S(2)}) async-start(), calls=%async_computation.2 | async-start | bytes 6881280 | tf_op jit(solution)/shard_map/all_gather | solution.py:89
  13.1 277.6 %reduce-scatter.3.cloned.1.call-start = ((), (), s32[]{:S(2)}) async-start(), calls=%async_computation.3 | async-start | bytes 6881280 | tf_op jit(solution)/shard_map/reduce_scatter | solution.py:152
  16.6 4.3 %copy-start.13 = (f32[512,4]{1,0:T(8,128)}, f32[512,4]{1,0:T(8,128)S(1)}, u32[]{:S(2)}) copy-start(f32[512,4]{1,0:T(8,128)S(1)} %copy.125) | copy-start | bytes 24580
  124.5 10.2 %copy-start.11 = (bf16[5376,256]{1,0:T(8,128)(2,1)S(1)}, bf16[5376,256]{1,0:T(8,128)(2,1)}, u32[]{:S(2)}) copy-start(bf16[5376,256]{1,0:T(8,128)(2,1)} %param.13) | copy-start | bytes 8257540
  128.3 18.9 %collective-permute-start = (bf16[512,2,128]{2,0,1:T(8,128)(2,1)}, bf16[512,2,128]{2,0,1:T(8,128)(2,1)}, u32[]{:S(2)}, u32[]{:S(2)}) collective-permute-start(bf16[512,2,128]{2,0,1:T(8,128)(2,1)} %pad_maximum_fusion), channel_id=1, source_target_pairs={{0,8},{4,12},{8,16},{12,20},{16,24},{20,28},{1,9},{5,13},{9,17},{1... | collective-permute-start | bytes 786440 | tf_op jit(solution)/shard_map/ppermute | solution.py:17
  132.4 14.8 %collective-permute-start.1 = (bf16[512,2,128]{2,0,1:T(8,128)(2,1)}, bf16[512,2,128]{2,0,1:T(8,128)(2,1)}, u32[]{:S(2)}, u32[]{:S(2)}) collective-permute-start(bf16[512,2,128]{2,0,1:T(8,128)(2,1)} %pad_maximum_fusion), channel_id=1, source_target_pairs={{0,4},{4,8},{8,12},{12,16},{16,20},{20,24},{24,28},{1,5},{5,9},{9,... | collective-permute-start | bytes 786440 | tf_op jit(solution)/shard_map/ppermute | solution.py:17
  141.4 10.9 %copy-start.10 = (pred[512,1536]{0,1:T(8,128)(4,1)S(1)}, pred[512,1536]{0,1:T(8,128)(4,1)}, u32[]{:S(2)}) copy-start(pred[512,1536]{0,1:T(8,128)(4,1)} %compare_and_fusion) | copy-start | bytes 2359300
  141.4 13.0 %collective-permute-start.2 = (bf16[512,2,128]{2,0,1:T(8,128)(2,1)}, bf16[512,2,128]{2,0,1:T(8,128)(2,1)S(1)}, u32[]{:S(2)}, u32[]{:S(2)}) collective-permute-start(bf16[512,2,128]{2,0,1:T(8,128)(2,1)} %copy.129), channel_id=1, source_target_pairs={{0,8},{4,12},{8,16},{12,20},{16,24},{20,28},{1,9},{5,13},{9,17},{1... | collective-permute-start | bytes 786440 | tf_op jit(solution)/shard_map/ppermute | solution.py:17
  143.8 10.7 %collective-permute-start.3 = (bf16[512,2,128]{2,0,1:T(8,128)(2,1)}, bf16[512,2,128]{2,0,1:T(8,128)(2,1)S(1)}, u32[]{:S(2)}, u32[]{:S(2)}) collective-permute-start(bf16[512,2,128]{2,0,1:T(8,128)(2,1)} %copy.129), channel_id=1, source_target_pairs={{0,4},{4,8},{8,12},{12,16},{16,20},{20,24},{24,28},{1,5},{5,9},{9,... | collective-permute-start | bytes 786440 | tf_op jit(solution)/shard_map/ppermute | solution.py:17
  155.6 6.9 %copy-start.15 = (bf16[512,2,2,128]{3,0,2,1:T(8,128)(2,1)S(1)}, bf16[512,2,2,128]{3,0,2,1:T(8,128)(2,1)}, u32[]{:S(2)}) copy-start(bf16[512,2,2,128]{3,0,2,1:T(8,128)(2,1)} %fusion.13) | copy-start | bytes 1572868
  167.1 4.9 %collective-permute-start.4 = (bf16[512,2,128]{2,0,1:T(8,128)(2,1)S(1)}, bf16[512,2,128]{2,0,1:T(8,128)(2,1)S(1)}, u32[]{:S(2)}, u32[]{:S(2)}) collective-permute-start(bf16[512,2,128]{2,0,1:T(8,128)(2,1)S(1)} %slice.83), channel_id=1, source_target_pairs={{4,0},{8,4},{12,8},{16,12},{20,16},{24,20},{28,24},{5,1},{9,5},{13... | collective-permute-start | bytes 786440 | tf_op jit(solution)/shard_map/ppermute | solution.py:17
  170.5 7.9 %copy-start.9 = (f32[1536,2,128]{0,2,1:T(8,128)}, f32[1536,2,128]{0,2,1:T(8,128)S(1)}, u32[]{:S(2)}) copy-start(f32[1536,2,128]{0,2,1:T(8,128)S(1)} %convolution_bitcast_fusion.1) | copy-start | bytes 4718596
  170.6 7.6 %copy-start.6 = (f32[512,64]{1,0:T(8,128)S(1)}, f32[512,64]{1,0:T(8,128)}, u32[]{:S(2)}) copy-start(f32[512,64]{1,0:T(8,128)} %copy-done.5) | copy-start | bytes 393220
  170.6 4.2 %collective-permute-start.6 = (bf16[512,2,128]{0,2,1:T(8,128)(2,1)S(1)}, bf16[512,2,128]{0,2,1:T(8,128)(2,1)S(1)}, u32[]{:S(2)}, u32[]{:S(2)}) collective-permute-start(bf16[512,2,128]{0,2,1:T(8,128)(2,1)S(1)} %slice.82), channel_id=1, source_target_pairs={{4,0},{8,4},{12,8},{16,12},{20,16},{24,20},{28,24},{5,1},{9,5},{13... | collective-permute-start | bytes 786440 | tf_op jit(solution)/shard_map/ppermute | solution.py:17
  172.1 6.3 %copy-start.26 = (f32[128]{0:T(128)S(1)}, f32[128]{0:T(128)}, u32[]{:S(2)}) copy-start(f32[128]{0:T(128)} %param.15) | copy-start | bytes 1540
  172.1 5.9 %collective-permute-start.5 = (bf16[512,2,128]{2,0,1:T(8,128)(2,1)S(1)}, bf16[512,2,128]{2,0,1:T(8,128)(2,1)S(1)}, u32[]{:S(2)}, u32[]{:S(2)}) collective-permute-start(bf16[512,2,128]{2,0,1:T(8,128)(2,1)S(1)} %fusion.17), channel_id=1, source_target_pairs={{4,0},{8,4},{12,8},{16,12},{20,16},{24,20},{28,24},{5,1},{9,5},{13... | collective-permute-start | bytes 786440 | tf_op jit(solution)/shard_map/ppermute | solution.py:17
  175.6 8.0 %collective-permute-start.7 = (bf16[512,2,128]{0,2,1:T(8,128)(2,1)}, bf16[512,2,128]{0,2,1:T(8,128)(2,1)}, u32[]{:S(2)}, u32[]{:S(2)}) collective-permute-start(bf16[512,2,128]{0,2,1:T(8,128)(2,1)} %fusion.15), channel_id=1, source_target_pairs={{4,0},{8,4},{12,8},{16,12},{20,16},{24,20},{28,24},{5,1},{9,5},{13... | collective-permute-start | bytes 786440 | tf_op jit(solution)/shard_map/ppermute | solution.py:17
  188.9 190.0 %reduce-scatter.5.cloned.1.call-start = ((), (), s32[]{:S(2)}) async-start(), calls=%async_computation.4 | async-start | bytes 12386304 | tf_op jit(solution)/shard_map/reduce_scatter | solution.py:163
  203.4 5.8 %copy-start.7 = (f32[512,64]{1,0:T(8,128)S(1)}, f32[512,64]{1,0:T(8,128)}, u32[]{:S(2)}) copy-start(f32[512,64]{1,0:T(8,128)} %copy-done.5) | copy-start | bytes 393220
  214.1 76.6 %copy-start.24 = (f32[5376]{0:T(1024)S(1)}, f32[5376]{0:T(1024)}, u32[]{:S(2)}) copy-start(f32[5376]{0:T(1024)} %param.10) | copy-start | bytes 64516
  218.0 75.1 %copy-start.30 = (f32[128]{0:T(128)S(1)}, f32[128]{0:T(128)}, u32[]{:S(2)}) copy-start(f32[128]{0:T(128)} %copy-done.29) | copy-start | bytes 1540
  218.0 75.2 %copy-start.28 = (f32[128]{0:T(128)S(1)}, f32[128]{0:T(128)}, u32[]{:S(2)}) copy-start(f32[128]{0:T(128)} %copy-done.27) | copy-start | bytes 1540
  (19 other events, 39.8 us)
Sparse Core Ops, SparseCore 0:
  13.2 105.0 all-gather.1
  189.1 101.5 reduce-scatter.2
  294.3 84.5 reduce-scatter.4
where the time goes:
time: 389 us; the launch traced here: 388 us
  waiting for transfers between devices  249 us (64%)
  matrix products  48.5 us (12%)
  other arithmetic  35.7 us (9%)
  local copies, waits for them, and re-layouts  22.7 us (6%)
  starting transfers between devices  17.8 us (5%)
  between operations  14.4 us (4%)
    all_gather x1, waiting for transfers between devices, shards(): gathered = lax.all_gather(normed_rows, 'tp', axis=0, tiled=True)  89.8 us
    reduce_scatter x1, waiting for transfers between devices, shards(): lax.psum_scatter(weight_term, 'seq', scatter_dimension=0, tiled=True)  83.8 us
    reduce_scatter x1, waiting for transfers between devices, shards(): lax.psum_scatter(partial_sum.astype(jnp.bfloat16), 'tp', scatter_dimensio...  71.8 us
    ppermute x8, starting transfers between devices, from_behind(): return lax.ppermute(array, axis, pairs)  17.7 us
    unnamed x68, local copies, waits for them, and re-layouts  11.1 us
    dot_general x1, matrix products, contract_first(): lax.dot_general(left, right, (((0,), (0,)), ((), ())), preferred_element_...  8.82 us
  transfers between devices with their start and end apart: 11, of which 6 were waited for; matrix products, arithmetic and copies ran while one was open for 18% of the time, Pallas kernels for 0%

commit v1 on v0

v1 whole, which is shorter than its diff:
```python
import functools
import math

import jax
import jax.numpy as jnp
from jax import lax
from jax.experimental import pallas as pl
from jax.experimental.pallas import tpu as pltpu
from jax.sharding import PartitionSpec as P

WINDOW = 1024
EPSILON = 1e-06
QUERY_SCALE = 168.0 ** (-0.5)
ROPE_BASE = 10000.0
VMEM_BYTES = 56 * 1024 * 1024
SMEM = pltpu.SMEM


def doc_begin(doc_lengths, positions):
    endings = jnp.cumsum(doc_lengths, dtype=jnp.int32)
    starts = endings - doc_lengths
    inside = starts[None, :] <= positions[:, None]
    return jnp.max(jnp.where(inside, starts[None, :], jnp.zeros_like(starts)[None, :]), axis=1)


def rope_tables(offsets, head_size):
    half_size = head_size // 2
    powers = jnp.arange(half_size, dtype=jnp.float32) * (2.0 / head_size)
    frequency = ROPE_BASE ** (-powers)
    angles = offsets.astype(jnp.float32)[:, None] * frequency[None, :]
    cosine = jnp.cos(angles)
    sine = jnp.sin(angles)
    return jnp.concatenate([cosine, cosine], axis=1), jnp.concatenate([-sine, sine], axis=1)


def half_turn(values):
    return pltpu.roll(values, values.shape[-1] // 2, values.ndim - 1)


def rope(values, cosine, sine):
    return values * cosine + half_turn(values) * sine


def rope_back(grads, cosine, sine):
    return grads * cosine + half_turn(grads * sine)


def inv_rms(values):
    return lax.rsqrt(jnp.mean(values * values, axis=-1, keepdims=True) + EPSILON)


def norm_back(grads, values, scale, gain):
    scaled = grads * gain
    mean = jnp.mean(values * scaled, axis=-1, keepdims=True)
    return scale * scaled - values * (scale * scale * scale * mean)


def dot_last(left, right):
    return lax.dot_general(left, right, (((1,), (1,)), ((), ())), preferred_element_type=jnp.float32)


def dot_first(left, right):
    return lax.dot_general(left, right, (((0,), (0,)), ((), ())), preferred_element_type=jnp.float32)


def full_spec(array):
    return pl.BlockSpec(array.shape, lambda *_: (0,) * array.ndim)


def any_spec():
    return pl.BlockSpec(memory_space=pl.ANY)


def smem_spec():
    return pl.BlockSpec(memory_space=SMEM)


def cost(flops, *arrays):
    size = sum(math.prod(a.shape) * jnp.dtype(a.dtype).itemsize for a in arrays)
    return pl.CostEstimate(flops=flops, bytes_accessed=size, transcendentals=0)


def params():
    return pltpu.CompilerParams(vmem_limit_bytes=VMEM_BYTES)


def project_body(count, info, gain, k_gain, cosine, sine, w_key, w_value, *rest):
    blocks = rest[:count]
    normed, key_value, raw_keys, held, sem = rest[count:]
    rows = held.shape[0]
    head_size = k_gain.shape[1]
    for index in range(count):

        @pl.when(info[0] == index)
        def _():
            copy = pltpu.make_async_copy(blocks[index], held, sem)
            copy.start()
            copy.wait()

    values = held[...].astype(jnp.float32)
    normed[...] = (values * inv_rms(values) * gain[...]).astype(jnp.bfloat16)
    keys = jnp.dot(normed[...], w_key[...], preferred_element_type=jnp.float32)
    raw_keys[...] = keys
    vals = jnp.dot(normed[...], w_value[...], preferred_element_type=jnp.float32)
    place = pl.ds(pl.multiple_of(info[1] * rows, rows), rows)
    cos_rows = cosine[place, :]
    sin_rows = sine[place, :]
    for head in range(w_key.shape[1] // head_size):
        cols = slice(head * head_size, (head + 1) * head_size)
        head_keys = keys[:, cols]
        turned = rope(head_keys * inv_rms(head_keys) * k_gain[...], cos_rows, sin_rows)
        low = 2 * head * head_size
        key_value[:, low : low + head_size] = turned.astype(jnp.bfloat16)
        key_value[:, low + head_size : low + 2 * head_size] = vals[:, cols].astype(jnp.bfloat16)


def project(info, blocks, in_gain, k_gain, cosine, sine, w_key, w_value):
    rows, width = blocks[0].shape
    cols = w_key.shape[1]
    outs = (
        jax.ShapeDtypeStruct((rows, width), jnp.bfloat16),
        jax.ShapeDtypeStruct((rows, 2 * cols), jnp.bfloat16),
        jax.ShapeDtypeStruct((rows, cols), jnp.float32),
    )
    dense = (in_gain, k_gain, cosine, sine, w_key, w_value)
    return pl.pallas_call(
        functools.partial(project_body, len(blocks)),
        name="project_block",
        grid=(1,),
        out_shape=outs,
        in_specs=[smem_spec()] + [full_spec(a) for a in dense] + [any_spec()] * len(blocks),
        out_specs=[full_spec(o) for o in outs],
        scratch_shapes=[pltpu.VMEM((rows, width), jnp.bfloat16), pltpu.SemaphoreType.DMA],
        compiler_params=params(),
        cost_estimate=cost(4 * rows * width * cols, blocks[0], w_key, w_value, *outs),
    )(info, *dense, *blocks)


def attend_body(reach, slots, info, lowest, q_gain, cosine, sine, queries, grads, *rest):
    blocks = rest[: (reach + 1) * slots]
    rest = rest[(reach + 1) * slots :]
    query_grads, own = rest[0], rest[1]
    far = rest[2 : 2 + reach]
    keys, values, key_sum, value_sum = rest[2 + reach :]
    rows = queries.shape[0]
    head_size = q_gain.shape[1]
    group = queries.shape[1] // head_size
    tile = blocks[0].shape[0]
    margin = reach * rows
    for slot in range(slots):
        start = info[slot] * tile
        for section in range(reach + 1):
            place = pl.ds(pl.multiple_of(section * rows + start, tile), tile)
            block = blocks[section * slots + slot]
            keys[place, :] = block[:, :head_size]
            values[place, :] = block[:, head_size:]
    key_sum[...] = jnp.zeros_like(key_sum)
    value_sum[...] = jnp.zeros_like(value_sum)
    for index in range(rows // tile):
        top = index * tile
        low = max(0, (top + margin - WINDOW + 1) // tile * tile)
        high = top + tile + margin
        width = high - low
        cos_rows = cosine[top : top + tile, :]
        sin_rows = sine[top : top + tile, :]
        raw = []
        scales = []
        turned = []
        for head in range(group):
            raw.append(queries[top : top + tile, head * head_size : (head + 1) * head_size].astype(jnp.float32))
            scales.append(inv_rms(raw[head]))
            turned.append(rope(raw[head] * scales[head] * q_gain[...], cos_rows, sin_rows) * QUERY_SCALE)
        query_rows = jnp.concatenate(turned, axis=0).astype(jnp.bfloat16)
        grad_rows = jnp.concatenate(
            [grads[top : top + tile, head * head_size : (head + 1) * head_size] for head in range(group)], axis=0
        )
        key_rows = keys[low:high, :]
        value_rows = values[low:high, :]
        columns = lax.broadcasted_iota(jnp.int32, (tile, width), 1) + low
        last = lax.broadcasted_iota(jnp.int32, (tile, width), 0) + (top + margin)
        allowed = (columns >= lowest[top : top + tile, :]) & (columns <= last)
        scores = dot_last(query_rows, key_rows).reshape(group, tile, width)
        exps = jnp.where(allowed[None], jnp.exp(scores), 0.0)
        probs = exps * (1.0 / jnp.sum(exps, axis=-1, keepdims=True))
        weights = probs.astype(jnp.bfloat16)
        along = dot_last(grad_rows, value_rows).reshape(group, tile, width)
        deltas = jnp.sum(weights.astype(jnp.float32) * along, axis=-1, keepdims=True)
        slopes = (probs * (along - deltas)).astype(jnp.bfloat16).reshape(group * tile, width)
        weights = weights.reshape(group * tile, width)
        key_sum[low:high, :] += dot_first(slopes, query_rows)
        value_sum[low:high, :] += dot_first(weights, grad_rows)
        back = jnp.dot(slopes, key_rows, preferred_element_type=jnp.float32)
        for head in range(group):
            turned_back = rope_back(back[head * tile : (head + 1) * tile] * QUERY_SCALE, cos_rows, sin_rows)
            result = norm_back(turned_back, raw[head], scales[head], q_gain[...])
            query_grads[top : top + tile, head * head_size : (head + 1) * head_size] = result.astype(jnp.bfloat16)
    for section in range(reach):
        span = slice(section * rows, (section + 1) * rows)
        far[section][:, :head_size] = key_sum[span, :].astype(jnp.bfloat16)
        far[section][:, head_size:] = value_sum[span, :].astype(jnp.bfloat16)
    own[:, :head_size] = key_sum[margin:, :]
    own[:, head_size:] = value_sum[margin:, :]


def attend(head, kv_heads, reach, info, lowest, q_gain, cosine, sine, queries, grads, blocks):
    rows = queries.shape[0]
    head_size = q_gain.shape[1]
    slots = len(blocks) // (reach + 1)
    tile = blocks[0].shape[0]
    cols = queries.shape[1] // kv_heads
    pick = lambda *_: (0, head)
    outs = (
        jax.ShapeDtypeStruct((rows, cols), jnp.bfloat16),
        jax.ShapeDtypeStruct((rows, 2 * head_size), jnp.float32),
    ) + (jax.ShapeDtypeStruct((rows, 2 * head_size), jnp.bfloat16),) * reach
    dense = (lowest, q_gain, cosine, sine)
    window = (reach + 1) * rows
    return pl.pallas_call(
        functools.partial(attend_body, reach, slots),
        name="attend_head",
        grid=(1,),
        out_shape=outs,
        in_specs=[smem_spec()]
        + [full_spec(a) for a in dense]
        + [pl.BlockSpec((rows, cols), pick)] * 2
        + [pl.BlockSpec((tile, 2 * head_size), pick)] * len(blocks),
        out_specs=[full_spec(o) for o in outs],
        scratch_shapes=[pltpu.VMEM((window, head_size), jnp.bfloat16)] * 2
        + [pltpu.VMEM((window, head_size), jnp.float32)] * 2,
        compiler_params=params(),
        cost_estimate=cost(10 * rows * window * cols, queries, grads, *blocks, *outs),
    )(info, *dense, queries, grads, *blocks)


def finish_body(reach, slots, info, k_gain, cosine, sine, own, *rest):
    arrived = rest[:reach]
    raw_keys = rest[reach : reach + slots]
    result = rest[reach + slots]
    head_size = k_gain.shape[1]
    rows = raw_keys[0].shape[0]
    for slot in range(slots):
        place = pl.ds(pl.multiple_of(info[slot] * rows, rows), rows)
        total = own[place, :]
        for part in arrived:
            total = total + part[place, :].astype(jnp.float32)
        values = raw_keys[slot][...]
        turned = rope_back(total[:, :head_size], cosine[place, :], sine[place, :])
        keys = norm_back(turned, values, inv_rms(values), k_gain[...])
        result[place, :head_size] = keys.astype(jnp.bfloat16)
        result[place, head_size:] = total[:, head_size:].astype(jnp.bfloat16)


def finish(head, info, k_gain, cosine, sine, own, arrived, raw_keys):
    head_size = k_gain.shape[1]
    out = jax.ShapeDtypeStruct(own.shape, jnp.bfloat16)
    dense = (k_gain, cosine, sine, own, *arrived)
    return pl.pallas_call(
        functools.partial(finish_body, len(arrived), len(raw_keys)),
        name="finish_kv",
        grid=(1,),
        out_shape=out,
        in_specs=[smem_spec()]
        + [full_spec(a) for a in dense]
        + [pl.BlockSpec((raw_keys[0].shape[0], head_size), lambda *_: (0, head))] * len(raw_keys),
        out_specs=full_spec(out),
        compiler_params=params(),
        cost_estimate=cost(0, own, *arrived, out),
    )(info, *dense, *raw_keys)


def weight_body(slots, info, grads, *rest):
    blocks = rest[:slots]
    send, keep, held = rest[slots:]
    rows = blocks[0].shape[0]
    chunk = send.shape[1]
    own = info[slots]
    left = jnp.concatenate([block[...] for block in blocks], axis=0)
    right = jnp.concatenate(
        [grads[pl.ds(pl.multiple_of(info[slot] * rows, rows), rows), :] for slot in range(slots)], axis=0
    )
    held[...] = dot_first(left, right)
    for pair in range(send.shape[0]):
        other = pl.ds(pl.multiple_of((2 * pair + 1 - own) * chunk, 8), chunk)
        mine = pl.ds(pl.multiple_of((2 * pair + own) * chunk, 8), chunk)
        send[pair] = held[other, :].astype(jnp.bfloat16)
        keep[pair] = held[mine, :].astype(jnp.bfloat16)


def weight_terms(info, grads, blocks, chunk):
    rows, width = blocks[0].shape
    cols = grads.shape[1]
    tile = math.lcm(2 * chunk, 128)
    pairs = tile // (2 * chunk)
    out = jax.ShapeDtypeStruct((width // (2 * chunk), chunk, cols), jnp.bfloat16)
    out_spec = pl.BlockSpec((pairs, chunk, cols), lambda step: (step, 0, 0))
    return pl.pallas_call(
        functools.partial(weight_body, len(blocks)),
        name="weight_terms",
        grid=(width // tile,),
        out_shape=(out, out),
        in_specs=[smem_spec(), full_spec(grads)]
        + [pl.BlockSpec((rows, tile), lambda step: (0, step))] * len(blocks),
        out_specs=(out_spec, out_spec),
        scratch_shapes=[pltpu.VMEM((tile, cols), jnp.float32)],
        compiler_params=params(),
        cost_estimate=cost(2 * len(blocks) * rows * width * cols, grads, *blocks, out, out),
    )(info, grads, *blocks)


def add(left, right):
    return left.astype(jnp.float32) + right.astype(jnp.float32)


def split_body(halves, info, *rest):
    keeps, arrivals, outs = rest[: len(halves)], rest[len(halves) : 2 * len(halves)], rest[2 * len(halves) :]
    for index, (cols, outer, inner) in enumerate(halves):
        own = info[index]
        for high in range(outer):
            for low in range(inner):
                for side, target in ((1 - own, outs[2 * index]), (own, outs[2 * index + 1])):
                    place = (high * 2 + side) * inner + low
                    total = add(keeps[index][place, :, cols], arrivals[index][place, :, cols])
                    target[high * inner + low] = total.astype(jnp.bfloat16)


def split_sum(info, keeps, arrivals, halves):
    outs = []
    for keep, (cols, outer, inner) in zip(keeps, halves):
        outs += [jax.ShapeDtypeStruct((outer * inner, keep.shape[1], cols.stop - cols.start), jnp.bfloat16)] * 2
    return pl.pallas_call(
        functools.partial(split_body, halves),
        name="split_sum",
        grid=(1,),
        out_shape=tuple(outs),
        in_specs=[smem_spec()] + [full_spec(a) for a in (*keeps, *arrivals)],
        out_specs=tuple(full_spec(o) for o in outs),
        compiler_params=params(),
        cost_estimate=cost(0, *keeps, *arrivals, *outs),
    )(info, *keeps, *arrivals)


def swap(array, bit):
    size = lax.axis_size("seq")
    return lax.ppermute(array, "seq", [(i, i ^ (1 << bit)) for i in range(size)])


def scatter_sum(send, keep):
    bits = lax.axis_size("seq").bit_length() - 1
    index = lax.axis_index("seq")
    half = keep.shape[2] // 2
    routes = (list(range(1, bits)), list(range(bits - 1, 0, -1)))
    lefts = [list(range(1, bits)), list(range(1, bits))]
    arrival = swap(send, 0)
    keeps, arrivals = [keep, keep], [arrival, arrival]
    cols = [slice(0, half), slice(half, 2 * half)]
    for step in range(bits - 1):
        turn = [route[step] for route in routes]
        halves = []
        for path in range(2):
            place = lefts[path].index(turn[path])
            halves.append((cols[path], 1 << (len(lefts[path]) - 1 - place), 1 << place))
            lefts[path].remove(turn[path])
        info = jnp.stack([(index >> bit) & 1 for bit in turn]).astype(jnp.int32)
        sent_a, kept_a, sent_b, kept_b = split_sum(info, keeps, arrivals, tuple(halves))
        arrivals = [swap(sent_a, turn[0]), swap(sent_b, turn[1])]
        keeps = [kept_a, kept_b]
        cols = [slice(0, half), slice(0, half)]
    return keeps, arrivals


def gather_body(heads, *rest):
    parts = rest[: 4 * heads]
    outs = rest[4 * heads :]
    size = parts[0].shape[2]
    for head in range(heads):
        for side in range(2):
            keep, arrival = parts[4 * head + side], parts[4 * head + 2 + side]
            outs[side][:, head * size : (head + 1) * size] = add(keep[0], arrival[0])


def gather_heads(parts, heads):
    _, rows, cols = parts[0].shape
    out = jax.ShapeDtypeStruct((rows, cols * heads), jnp.float32)
    return pl.pallas_call(
        functools.partial(gather_body, heads),
        name="gather_heads",
        grid=(1,),
        out_shape=(out, out),
        in_specs=[full_spec(a) for a in parts],
        out_specs=(full_spec(out), full_spec(out)),
        compiler_params=params(),
        cost_estimate=cost(0, *parts, out, out),
    )(*parts)


def arrival_table(count):
    table = []
    for place in range(count):
        arrivals = []
        for step in range(1, count):
            if place - step >= 0:
                arrivals.append((2 * (step - 1), place - step))
            if place + step < count:
                arrivals.append((2 * (step - 1) + 1, place + step))
        table.append(arrivals)
    return table


def shards(tokens, in_gain, raw_queries, w_key, w_value, q_gain, k_gain, doc_lengths, out_grad):
    tp_count = lax.axis_size("tp")
    seq_count = lax.axis_size("seq")
    head_size = q_gain.shape[0]
    kv_heads = w_key.shape[1] // head_size
    rows, width = tokens.shape
    shard_rows = rows * tp_count
    reach = (WINDOW - 2) // shard_rows + 1
    seq_index = lax.axis_index("seq")
    tp_index = lax.axis_index("tp")
    first_row = seq_index * shard_rows
    positions = first_row + jnp.arange(shard_rows, dtype=jnp.int32)
    begins = doc_begin(doc_lengths, positions)
    cosine, sine = rope_tables(positions - begins, head_size)
    lowest = jnp.maximum(begins, positions - (WINDOW - 1)) - (first_row - reach * shard_rows)
    lowest = lowest[:, None]
    gain_row = in_gain[None, :]
    q_row = q_gain[None, :]
    k_row = k_gain[None, :]

    table = arrival_table(tp_count)
    picks = jnp.array(table, dtype=jnp.int32).reshape(tp_count, tp_count - 1, 2)
    picks = lax.dynamic_index_in_dim(picks, tp_index, 0, keepdims=False)
    infos = [jnp.stack([jnp.int32(0), tp_index.astype(jnp.int32)])] + [picks[i] for i in range(tp_count - 1)]
    slot_places = jnp.concatenate([tp_index.astype(jnp.int32)[None], picks[:, 1]])

    normed_blocks, kv_blocks, raw_keys = [], [], []
    halo = [[] for _ in range(reach)]
    arrivals = []
    going_up = going_down = tokens
    for slot in range(tp_count):
        candidates = [tokens] if slot == 0 else list(arrivals)
        if slot < tp_count - 1:
            up_pairs = [(i, i + 1) for i in range(slot, tp_count - 1)]
            down_pairs = [(i + 1, i) for i in range(tp_count - 1 - slot)]
            going_up = lax.ppermute(going_up, "tp", up_pairs)
            going_down = lax.ppermute(going_down, "tp", down_pairs)
            arrivals += [going_up, going_down]
        normed, key_value, keys = project(
            infos[slot], candidates, gain_row, k_row, cosine, sine, w_key, w_value
        )
        normed_blocks.append(normed)
        kv_blocks.append(key_value)
        raw_keys.append(keys)
        for distance in range(1, reach + 1):
            pairs = [(i, i + distance) for i in range(seq_count - distance)]
            halo[distance - 1].append(lax.ppermute(key_value, "seq", pairs))

    blocks = []
    for distance in range(reach, 0, -1):
        blocks += halo[distance - 1]
    blocks += kv_blocks
    query_parts, kv_grads = [], []
    for head in range(kv_heads):
        outs = attend(head, kv_heads, reach, slot_places, lowest, q_row, cosine, sine, raw_queries, out_grad, blocks)
        query_parts.append(outs[0])
        back = []
        for section in range(reach):
            distance = reach - section
            pairs = [(i + distance, i) for i in range(seq_count - distance)]
            back.append(lax.ppermute(outs[2 + section], "seq", pairs))
        kv_grads.append(finish(head, slot_places, k_row, cosine, sine, outs[1], back, raw_keys))
    grad_queries = jnp.concatenate(query_parts, axis=1)

    grad_k = jnp.concatenate([g[:, :head_size] for g in kv_grads], axis=1)
    grad_v = jnp.concatenate([g[:, head_size:] for g in kv_grads], axis=1)
    partial_sum = dot_last(grad_k, w_key) + dot_last(grad_v, w_value)
    normed_grad = lax.psum_scatter(
        partial_sum.astype(jnp.bfloat16), "tp", scatter_dimension=0, tiled=True
    ).astype(jnp.float32)
    x_float = tokens.astype(jnp.float32)
    grad_x = norm_back(normed_grad, x_float, inv_rms(x_float), gain_row).astype(jnp.bfloat16)

    chunk = width // seq_count
    if chunk % 16 == 0 and seq_count & (seq_count - 1) == 0 and seq_count > 1 and width % math.lcm(2 * chunk, 128) == 0:
        info = jnp.concatenate([slot_places, (seq_index & 1).astype(jnp.int32)[None]])
        parts = []
        for head in range(kv_heads):
            send, keep = weight_terms(info, kv_grads[head], normed_blocks, chunk)
            keeps, comings = scatter_sum(send, keep)
            parts += [*keeps, *comings]
        grad_wk, grad_wv = gather_heads(parts, kv_heads)
    else:
        left = jnp.concatenate(normed_blocks, axis=0)
        order = (slot_places[:, None] * rows + jnp.arange(rows, dtype=jnp.int32)[None, :]).reshape(-1)
        right = jnp.take(jnp.concatenate([grad_k, grad_v], axis=1), order, axis=0)
        summed = lax.psum_scatter(dot_first(left, right), "seq", scatter_dimension=0, tiled=True)
        grad_wk = summed[:, : w_key.shape[1]]
        grad_wv = summed[:, w_key.shape[1] :]
    return (grad_x, grad_queries, grad_wk, grad_wv)


def solution(mesh):
    placed = (
        P(("seq", "tp"), None),
        P(),
        P("seq", "tp"),
        P(None, "tp"),
        P(None, "tp"),
        P(),
        P(),
        P(),
        P("seq", "tp"),
    )
    return jax.shard_map(
        shards,
        mesh=mesh,
        in_specs=placed,
        out_specs=(P(("seq", "tp"), None), P("seq", "tp"), P("seq", "tp"), P("seq", "tp")),
        check_vma=False,
    )
```

time: 389 us -> 301 us (0.77)
  waiting for transfers between devices: 249 us -> 124 us
  Pallas kernels: 0 us -> 72.4 us
  matrix products: 48.5 us -> 14 us
  starting transfers between devices: 17.8 us -> 51.1 us
  other arithmetic: 35.7 us -> 12.1 us
  local copies, waits for them, and re-layouts: 22.7 us -> 11.4 us
    all_gather x1 -> x0, waiting for transfers between devices: 89.8 us -> none  [shards(): gathered = lax.all_gather(normed_rows, 'tp', axis=0, tiled=True)]
    reduce_scatter x1 -> x0, waiting for transfers between devices: 83.8 us -> none  [shards(): lax.psum_scatter(weight_term, 'seq', scatter_dimension=0, tiled=True)]
    pallas_call x0 -> x15, Pallas kernels: none -> 72.4 us  [the longest x4 25.4 us: project(): pl.pallas_call(functools.partial(project_body, len(blocks)), name='projec...]
    ppermute x8 -> x28, waiting for transfers between devices: 3.2 us -> 72.8 us  [the longest x3 57.1 us: shards(): going_down = lax.ppermute(going_down, 'tp', down_pairs)]
    dot_general x11 -> x2, matrix products: 48.5 us -> 14 us  [dot_last(): lax.dot_general(left, right, (((1,), (1,)), ((), ())), preferred_element_...]
    ppermute x8 -> x28, starting transfers between devices: 17.7 us -> 51 us  [the longest x8 20 us: shards(): halo[distance - 1].append(lax.ppermute(key_value, 'seq', pairs))]
    reduce_scatter x1, waiting for transfers between devices: 71.8 us -> 51.6 us  [shards(): lax.psum_scatter(partial_sum.astype(jnp.bfloat16), 'tp', scatter_dimensio...]
    convert_element_type x9 -> x2, other arithmetic: 16.5 us -> 1.74 us  [the longest x1 1.73 us: shards(): norm_back(normed_grad, x_float, inv_rms(x_float), gain_row)]
  transfers between devices with their start and end apart: 11 -> 29, of which waited for: 6 -> 10; matrix products, arithmetic and copies ran while one was open for 18% -> 4% of each run, Pallas kernels for 0% -> 21%
where the time goes in v1:
time: 301 us; the launch traced here: 300 us
  waiting for transfers between devices  124 us (41%)
  Pallas kernels  72.4 us (24%)
  starting transfers between devices  51.1 us (17%)
  between operations  14.6 us (5%)
  matrix products  14 us (5%)
  other arithmetic  12.1 us (4%)
  local copies, waits for them, and re-layouts  11.4 us (4%)
    ppermute x3, waiting for transfers between devices, shards(): going_down = lax.ppermute(going_down, 'tp', down_pairs)  57.1 us
    reduce_scatter x1, waiting for transfers between devices, shards(): lax.psum_scatter(partial_sum.astype(jnp.bfloat16), 'tp', scatter_dimensio...  51.6 us
    pallas_call x4, Pallas kernels, project(): pl.pallas_call(functools.partial(project_body, len(blocks)), name='projec...  25.4 us
    ppermute x8, starting transfers between devices, shards(): halo[distance - 1].append(lax.ppermute(key_value, 'seq', pairs))  20 us
    pallas_call x2, Pallas kernels, attend(): pl.pallas_call(functools.partial(attend_body, reach, slots), name='attend...  16 us
    dot_general x2, matrix products, dot_last(): lax.dot_general(left, right, (((1,), (1,)), ((), ())), preferred_element_...  14 us
    pallas_call x4, Pallas kernels, split_sum(): pl.pallas_call(functools.partial(split_body, halves), name='split_sum', g...  12.7 us
    ppermute x10, starting transfers between devices, swap(): return lax.ppermute(array, 'seq', [(i, i ^ 1 << bit) for i in range(size)])  12.6 us
  transfers between devices with their start and end apart: 29, of which 10 were waited for; matrix products, arithmetic and copies ran while one was open for 4% of the time, Pallas kernels for 21%

profile of v1, /device:TPU:0, one launch (start us, length us, event | category | flops | bytes accessed | tf_op | source)
XLA Modules:
  0.0 299.9 jit_solution(11364816469411982141)
XLA Ops:
  8.5 5.6 %collective-permute-start.1 = (bf16[128,5376]{1,0:T(8,128)(2,1)}, bf16[128,5376]{1,0:T(8,128)(2,1)S(1)}, u32[]{:S(2)}, u32[]{:S(2)}) collective-permute-start(bf16[128,5376]{1,0:T(8,128)(2,1)} %rest_0_.1), channel_id=1, source_target_pairs={{0,1},{1,2},{2,3},{4,5},{5,6},{6,7},{8,9},{9,10},{10,11},{12,13},{... | collective-permute-start | bytes 4128776 | tf_op jit(solution)/shard_map/ppermute | solution.py:444
  14.2 28.4 %collective-permute-done.2.rest_1_ = bf16[128,5376]{1,0:T(8,128)(2,1)S(1)} collective-permute-done((bf16[128,5376]{1,0:T(8,128)(2,1)}, bf16[128,5376]{1,0:T(8,128)(2,1)S(1)}, u32[]{:S(2)}, u32[]{:S(2)}) %collective-permute-start.2) | collective-permute-done | bytes 1376288 | tf_op jit(solution)/shard_map/ppermute | solution.py:445
  47.2 28.7 %collective-permute-done.5.rest_3_ = bf16[128,5376]{1,0:T(8,128)(2,1)} collective-permute-done((bf16[128,5376]{1,0:T(8,128)(2,1)S(1)}, bf16[128,5376]{1,0:T(8,128)(2,1)}, u32[]{:S(2)}, u32[]{:S(2)}) %collective-permute-start.5) | collective-permute-done | bytes 1376288 | tf_op jit(solution)/shard_map/ppermute | solution.py:445
  82.9 6.3 %project_block.4 = (bf16[128,5376]{1,0:T(8,128)(2,1)}, bf16[128,512]{1,0:T(8,128)(2,1)}, f32[128,256]{1,0:T(8,128)}) custom-call(s32[2]{0:T(128)} %pad_add_fusion.1.info, f32[1,5376]{1,0:T(1,128)} %broadcast_in_dim.41.gain, f32[1,128]{1,0:T(1,128)} %bitcast.21, f32[512,128]{1,0:T(8,128)} %get-tuple-element.102.cosine, f32[512,128]{1,0:T(8,128)} %get-tuple-element.103.sine, ...), custom_call_target="tpu_custom_call" | custom-call | flops 704643072 | bytes 8519680 | tf_op jit(solution)/shard_map/project_block/pallas_call | solution.py:126
  90.5 3.9 %collective-permute-start = (bf16[128,512]{1,0:T(8,128)(2,1)}, bf16[128,512]{1,0:T(8,128)(2,1)S(1)}, u32[]{:S(2)}, u32[]{:S(2)}) collective-permute-start(bf16[128,512]{1,0:T(8,128)(2,1)} %get-tuple-element.46.rest_8_), channel_id=1, source_target_pairs={{0,8},{4,12},{8,16},{12,20},{16,24},{20,28},{1,9},{5,13},{9,17},{1... | collective-permute-start | bytes 393224 | tf_op jit(solution)/shard_map/ppermute | solution.py:455
  96.7 6.3 %project_block.5 = (bf16[128,5376]{1,0:T(8,128)(2,1)}, bf16[128,512]{1,0:T(8,128)(2,1)}, f32[128,256]{1,0:T(8,128)}) custom-call(s32[2]{0:T(128)} %get-tuple-element.99.info, f32[1,5376]{1,0:T(1,128)} %broadcast_in_dim.41.gain, f32[1,128]{1,0:T(1,128)} %bitcast.22, f32[512,128]{1,0:T(8,128)} %get-tuple-element.102.cosine, ...), custom_call_target="tpu_custom_call" | custom-call | flops 704643072 | bytes 8519680 | tf_op jit(solution)/shard_map/project_block/pallas_call | solution.py:126
  103.0 3.2 %collective-permute-start.11 = (bf16[128,512]{1,0:T(8,128)(2,1)}, bf16[128,512]{1,0:T(8,128)(2,1)S(1)}, u32[]{:S(2)}, u32[]{:S(2)}) collective-permute-start(bf16[128,512]{1,0:T(8,128)(2,1)} %get-tuple-element.47.rest_9_), channel_id=1, source_target_pairs={{0,4},{4,8},{8,12},{12,16},{16,20},{20,24},{24,28},{1,5},{5,9},{9,... | collective-permute-start | bytes 393224 | tf_op jit(solution)/shard_map/ppermute | solution.py:455
  106.3 6.4 %project_block.6 = (bf16[128,5376]{1,0:T(8,128)(2,1)}, bf16[128,512]{1,0:T(8,128)(2,1)}, f32[128,256]{1,0:T(8,128)}) custom-call(s32[2]{0:T(128)} %get-tuple-element.98.info, f32[1,5376]{1,0:T(1,128)} %broadcast_in_dim.41.gain, f32[1,128]{1,0:T(1,128)} %bitcast.23, f32[512,128]{1,0:T(8,128)} %get-tuple-element.102.cosine, ...), custom_call_target="tpu_custom_call" | custom-call | flops 704643072 | bytes 8519680 | tf_op jit(solution)/shard_map/project_block/pallas_call | solution.py:126
  112.7 3.4 %collective-permute-start.3 = (bf16[128,512]{1,0:T(8,128)(2,1)S(1)}, bf16[128,512]{1,0:T(8,128)(2,1)S(1)}, u32[]{:S(2)}, u32[]{:S(2)}) collective-permute-start(bf16[128,512]{1,0:T(8,128)(2,1)S(1)} %copy-done.25), channel_id=1, source_target_pairs={{0,8},{4,12},{8,16},{12,20},{16,24},{20,28},{1,9},{5,13},{9,17},{1... | collective-permute-start | bytes 393224 | tf_op jit(solution)/shard_map/ppermute | solution.py:455
  118.1 6.4 %project_block.7 = (bf16[128,5376]{1,0:T(8,128)(2,1)}, bf16[128,512]{1,0:T(8,128)(2,1)}, f32[128,256]{1,0:T(8,128)}) custom-call(s32[2]{0:T(128)} %get-tuple-element.97.info, f32[1,5376]{1,0:T(1,128)} %broadcast_in_dim.41.gain, f32[1,128]{1,0:T(1,128)} %bitcast.24, f32[512,128]{1,0:T(8,128)} %get-tuple-element.102.cosine, ...), custom_call_target="tpu_custom_call" | custom-call | flops 704643072 | bytes 8519680 | tf_op jit(solution)/shard_map/project_block/pallas_call | solution.py:126
  134.7 8.0 %attend_head.3 = (bf16[512,256]{1,0:T(8,128)(2,1)}, f32[512,256]{1,0:T(8,128)}, bf16[512,256]{1,0:T(8,128)(2,1)}, bf16[512,256]{1,0:T(8,128)(2,1)}) custom-call(s32[4]{0:T(128)} %pad_add_fusion.info, s32[512,1]{1,0:T(8,128)} %maximum_subtract_fusion.lowest, f32[1,128]{1,0:T(1,128)} %bitcast.30, f32[512,128]{1,0:T(8,128)} %get-tuple-element.102.cosine, ...), custom_call_target="tpu_custom_call" | custom-call | flops 2013265920 | bytes 3932160 | tf_op jit(solution)/shard_map/attend_head/pallas_call | solution.py:218
  145.2 8.0 %attend_head.2 = (bf16[512,256]{1,0:T(8,128)(2,1)}, f32[512,256]{1,0:T(8,128)}, bf16[512,256]{1,0:T(8,128)(2,1)}, bf16[512,256]{1,0:T(8,128)(2,1)}) custom-call(s32[4]{0:T(128)} %pad_add_fusion.info, s32[512,1]{1,0:T(8,128)} %maximum_subtract_fusion.lowest, f32[1,128]{1,0:T(1,128)} %bitcast.31, f32[512,128]{1,0:T(8,128)} %get-tuple-element.102.cosine, ...), custom_call_target="tpu_custom_call" | custom-call | flops 2013265920 | bytes 3932160 | tf_op jit(solution)/shard_map/attend_head/pallas_call | solution.py:218
  156.9 2.7 finish_kv.3.grads
  160.6 5.4 %collective-permute-done.14.rest_0_ = bf16[512,256]{1,0:T(8,128)(2,1)S(1)} collective-permute-done((bf16[512,256]{1,0:T(8,128)(2,1)}, bf16[512,256]{1,0:T(8,128)(2,1)S(1)}, u32[]{:S(2)}, u32[]{:S(2)}) %collective-permute-start.14) | collective-permute-done | bytes 262176 | tf_op jit(solution)/shard_map/ppermute | solution.py:469
  170.3 5.8 %fusion.7 = f32[512,5376]{1,0:T(8,128)} fusion(bf16[5376,256]{1,0:T(8,128)(2,1)S(1)} %copy-done.1, bf16[512,128]{1,0:T(8,128)(2,1)S(1)} %get-tuple-element.93, bf16[512,128]{1,0:T(8,128)(2,1)S(1)} %get-tuple-element.91), kind=kOutput, calls=%fused_computation.17 | convolution fusion | flops 1409810432 | bytes 14024704 | tf_op jit(solution)/shard_map/dot_general | solution.py:59
  176.1 8.2 %add_convert_fusion = bf16[512,5376]{1,0:T(8,128)(2,1)} fusion(f32[512,5376]{1,0:T(8,128)} %fusion.7, bf16[5376,256]{1,0:T(8,128)(2,1)S(1)} %copy-done, bf16[512,128]{1,0:T(8,128)(2,1)S(1)} %get-tuple-element.92, bf16[512,128]{1,0:T(8,128)(2,1)S(1)} %get-tuple-element.90), kind=kOutput, calls=%fused_computation | convolution fusion | flops 1415315456 | bytes 19529728 | tf_op jit(solution)/shard_map/dot_general | solution.py:59
  185.0 5.2 %weight_terms.2 = (bf16[4,672,256]{2,1,0:T(8,128)(2,1)}, bf16[4,672,256]{2,1,0:T(8,128)(2,1)}) custom-call(s32[5]{0:T(128)} %pad_add_fusion.4.info, bf16[512,256]{1,0:T(8,128)(2,1)} %finish_kv.2.grads, bf16[128,5376]{1,0:T(8,128)(2,1)} %get-tuple-element.62.rest_0_, bf16[128,5376]{1,0:T(8,128)(2,1)} %get-tuple-element.63.rest_1_, ...), custom_call_target="tpu_custom_call" | custom-call | flops 1409286144 | bytes 8519680 | tf_op jit(solution)/shard_map/weight_terms/pallas_call | solution.py:296
  192.7 5.2 %weight_terms.3 = (bf16[4,672,256]{2,1,0:T(8,128)(2,1)}, bf16[4,672,256]{2,1,0:T(8,128)(2,1)}) custom-call(s32[5]{0:T(128)} %pad_add_fusion.4.info, bf16[512,256]{1,0:T(8,128)(2,1)} %finish_kv.3.grads, bf16[128,5376]{1,0:T(8,128)(2,1)} %get-tuple-element.62.rest_0_, bf16[128,5376]{1,0:T(8,128)(2,1)} %get-tuple-element.63.rest_1_, ...), custom_call_target="tpu_custom_call" | custom-call | flops 1409286144 | bytes 8519680 | tf_op jit(solution)/shard_map/weight_terms/pallas_call | solution.py:296
  199.7 4.2 %split_sum.4 = (bf16[2,672,128]{2,1,0:T(8,128)(2,1)}, bf16[2,672,128]{2,1,0:T(8,128)(2,1)}, bf16[2,672,128]{2,1,0:T(8,128)(2,1)}, bf16[2,672,128]{2,1,0:T(8,128)(2,1)}) custom-call(s32[2]{0:T(128)} %pad_add_fusion.3.info, bf16[4,672,256]{2,1,0:T(8,128)(2,1)} %get-tuple-element.66.rest_0_.rest_1_, bf16[4,672,256]{2,1,0:T(8,128)(2,1)} %get-tuple-element.66.rest_0_.rest_1_, ...), custom_call_target="tpu_custom_call" | custom-call | bytes 6881280 | tf_op jit(solution)/shard_map/split_sum/pallas_call | solution.py:330
  203.8 2.9 collective-permute-start.19
  208.4 4.1 %split_sum.6 = (bf16[2,672,128]{2,1,0:T(8,128)(2,1)}, bf16[2,672,128]{2,1,0:T(8,128)(2,1)}, bf16[2,672,128]{2,1,0:T(8,128)(2,1)}, bf16[2,672,128]{2,1,0:T(8,128)(2,1)}) custom-call(s32[2]{0:T(128)} %pad_add_fusion.3.info, bf16[4,672,256]{2,1,0:T(8,128)(2,1)} %get-tuple-element.76.rest_0_.rest_1_, bf16[4,672,256]{2,1,0:T(8,128)(2,1)} %get-tuple-element.76.rest_0_.rest_1_, ...), custom_call_target="tpu_custom_call" | custom-call | bytes 6881280 | tf_op jit(solution)/shard_map/split_sum/pallas_call | solution.py:330
  231.3 2.7 collective-permute-done.26.rest_6_
  234.9 2.6 gather_heads.1
  237.5 51.6 %reduce-scatter.2.cloned.1.call-done = bf16[128,5376]{1,0:T(8,128)(2,1)} async-done(((bf16[512,5376]{1,0:T(8,128)(2,1)}), bf16[128,5376]{1,0:T(8,128)(2,1)}) %reduce-scatter.2.cloned.1.call-update) | async-done | bytes 1376272 | tf_op jit(solution)/shard_map/reduce_scatter | solution.py:476
  (144 shorter events, 70.2 us)
Async XLA Ops:
  7.2 281.9 %reduce-scatter.2.cloned.1.call-start = ((), (), s32[]{:S(2)}) async-start(), calls=%async_computation.1 | async-start | bytes 6881280 | tf_op jit(solution)/shard_map/reduce_scatter | solution.py:476
  7.2 35.3 %collective-permute-start.2 = (bf16[128,5376]{1,0:T(8,128)(2,1)}, bf16[128,5376]{1,0:T(8,128)(2,1)S(1)}, u32[]{:S(2)}, u32[]{:S(2)}) collective-permute-start(bf16[128,5376]{1,0:T(8,128)(2,1)} %rest_0_.1), channel_id=1, source_target_pairs={{1,0},{2,1},{3,2},{5,4},{6,5},{7,6},{9,8},{10,9},{11,10},{13,12},{... | collective-permute-start | bytes 4128776 | tf_op jit(solution)/shard_map/ppermute | solution.py:445
  8.5 35.3 %collective-permute-start.1 = (bf16[128,5376]{1,0:T(8,128)(2,1)}, bf16[128,5376]{1,0:T(8,128)(2,1)S(1)}, u32[]{:S(2)}, u32[]{:S(2)}) collective-permute-start(bf16[128,5376]{1,0:T(8,128)(2,1)} %rest_0_.1), channel_id=1, source_target_pairs={{0,1},{1,2},{2,3},{4,5},{5,6},{6,7},{8,9},{9,10},{10,11},{12,13},{... | collective-permute-start | bytes 4128776 | tf_op jit(solution)/shard_map/ppermute | solution.py:444
  42.5 33.4 %collective-permute-start.5 = (bf16[128,5376]{1,0:T(8,128)(2,1)S(1)}, bf16[128,5376]{1,0:T(8,128)(2,1)}, u32[]{:S(2)}, u32[]{:S(2)}) collective-permute-start(bf16[128,5376]{1,0:T(8,128)(2,1)S(1)} %collective-permute-done.2.rest_1_), channel_id=1, source_target_pairs={{1,0},{2,1},{5,4},{6,5},{9,8},{10,9},{13,12},{14,13},{17,16},{18,1... | collective-permute-start | bytes 4128776 | tf_op jit(solution)/shard_map/ppermute | solution.py:445
  43.8 33.3 %collective-permute-start.4 = (bf16[128,5376]{1,0:T(8,128)(2,1)S(1)}, bf16[128,5376]{1,0:T(8,128)(2,1)}, u32[]{:S(2)}, u32[]{:S(2)}) collective-permute-start(bf16[128,5376]{1,0:T(8,128)(2,1)S(1)} %collective-permute-done.1.rest_0_), channel_id=1, source_target_pairs={{1,2},{2,3},{5,6},{6,7},{9,10},{10,11},{13,14},{14,15},{17,18},{18... | collective-permute-start | bytes 4128776 | tf_op jit(solution)/shard_map/ppermute | solution.py:444
  75.9 36.8 %collective-permute-start.8 = (bf16[128,5376]{1,0:T(8,128)(2,1)}, bf16[128,5376]{1,0:T(8,128)(2,1)}, u32[]{:S(2)}, u32[]{:S(2)}) collective-permute-start(bf16[128,5376]{1,0:T(8,128)(2,1)} %collective-permute-done.5.rest_3_), channel_id=1, source_target_pairs={{1,0},{5,4},{9,8},{13,12},{17,16},{21,20},{25,24},{29,28}} | collective-permute-start | bytes 4128776 | tf_op jit(solution)/shard_map/ppermute | solution.py:445
  77.2 38.9 %collective-permute-start.7 = (bf16[128,5376]{1,0:T(8,128)(2,1)}, bf16[128,5376]{1,0:T(8,128)(2,1)}, u32[]{:S(2)}, u32[]{:S(2)}) collective-permute-start(bf16[128,5376]{1,0:T(8,128)(2,1)} %collective-permute-done.4.rest_2_), channel_id=1, source_target_pairs={{2,3},{6,7},{10,11},{14,15},{18,19},{22,23},{26,27},{30,31}} | collective-permute-start | bytes 4128776 | tf_op jit(solution)/shard_map/ppermute | solution.py:444
  89.2 35.2 %collective-permute-start.10 = (bf16[128,512]{1,0:T(8,128)(2,1)}, bf16[128,512]{1,0:T(8,128)(2,1)S(1)}, u32[]{:S(2)}, u32[]{:S(2)}) collective-permute-start(bf16[128,512]{1,0:T(8,128)(2,1)} %get-tuple-element.46.rest_8_), channel_id=1, source_target_pairs={{0,4},{4,8},{8,12},{12,16},{16,20},{20,24},{24,28},{1,5},{5,9},{9,... | collective-permute-start | bytes 393224 | tf_op jit(solution)/shard_map/ppermute | solution.py:455
  90.5 36.1 %collective-permute-start = (bf16[128,512]{1,0:T(8,128)(2,1)}, bf16[128,512]{1,0:T(8,128)(2,1)S(1)}, u32[]{:S(2)}, u32[]{:S(2)}) collective-permute-start(bf16[128,512]{1,0:T(8,128)(2,1)} %get-tuple-element.46.rest_8_), channel_id=1, source_target_pairs={{0,8},{4,12},{8,16},{12,20},{16,24},{20,28},{1,9},{5,13},{9,17},{1... | collective-permute-start | bytes 393224 | tf_op jit(solution)/shard_map/ppermute | solution.py:455
  103.0 25.4 %collective-permute-start.11 = (bf16[128,512]{1,0:T(8,128)(2,1)}, bf16[128,512]{1,0:T(8,128)(2,1)S(1)}, u32[]{:S(2)}, u32[]{:S(2)}) collective-permute-start(bf16[128,512]{1,0:T(8,128)(2,1)} %get-tuple-element.47.rest_9_), channel_id=1, source_target_pairs={{0,4},{4,8},{8,12},{12,16},{16,20},{20,24},{24,28},{1,5},{5,9},{9,... | collective-permute-start | bytes 393224 | tf_op jit(solution)/shard_map/ppermute | solution.py:455
  112.7 18.8 %collective-permute-start.3 = (bf16[128,512]{1,0:T(8,128)(2,1)S(1)}, bf16[128,512]{1,0:T(8,128)(2,1)S(1)}, u32[]{:S(2)}, u32[]{:S(2)}) collective-permute-start(bf16[128,512]{1,0:T(8,128)(2,1)S(1)} %copy-done.25), channel_id=1, source_target_pairs={{0,8},{4,12},{8,16},{12,20},{16,24},{20,28},{1,9},{5,13},{9,17},{1... | collective-permute-start | bytes 393224 | tf_op jit(solution)/shard_map/ppermute | solution.py:455
  116.1 15.3 %collective-permute-start.12 = (bf16[128,512]{1,0:T(8,128)(2,1)}, bf16[128,512]{1,0:T(8,128)(2,1)S(1)}, u32[]{:S(2)}, u32[]{:S(2)}) collective-permute-start(bf16[128,512]{1,0:T(8,128)(2,1)} %get-tuple-element.48.rest_10_), channel_id=1, source_target_pairs={{0,4},{4,8},{8,12},{12,16},{16,20},{20,24},{24,28},{1,5},{5,9},{9,... | collective-permute-start | bytes 393224 | tf_op jit(solution)/shard_map/ppermute | solution.py:455
  142.6 13.4 %collective-permute-start.16 = (bf16[512,256]{1,0:T(8,128)(2,1)}, bf16[512,256]{1,0:T(8,128)(2,1)S(1)}, u32[]{:S(2)}, u32[]{:S(2)}) collective-permute-start(bf16[512,256]{1,0:T(8,128)(2,1)} %get-tuple-element.58), channel_id=1, source_target_pairs={{8,0},{12,4},{16,8},{20,12},{24,16},{28,20},{9,1},{13,5},{17,9},{2... | collective-permute-start | bytes 786440 | tf_op jit(solution)/shard_map/ppermute | solution.py:469
  143.9 12.2 %collective-permute-start.17 = (bf16[512,256]{1,0:T(8,128)(2,1)}, bf16[512,256]{1,0:T(8,128)(2,1)S(1)}, u32[]{:S(2)}, u32[]{:S(2)}) collective-permute-start(bf16[512,256]{1,0:T(8,128)(2,1)} %get-tuple-element.59), channel_id=1, source_target_pairs={{4,0},{8,4},{12,8},{16,12},{20,16},{24,20},{28,24},{5,1},{9,5},{13... | collective-permute-start | bytes 786440 | tf_op jit(solution)/shard_map/ppermute | solution.py:469
  153.2 12.7 %collective-permute-start.14 = (bf16[512,256]{1,0:T(8,128)(2,1)}, bf16[512,256]{1,0:T(8,128)(2,1)S(1)}, u32[]{:S(2)}, u32[]{:S(2)}) collective-permute-start(bf16[512,256]{1,0:T(8,128)(2,1)} %get-tuple-element.51), channel_id=1, source_target_pairs={{8,0},{12,4},{16,8},{20,12},{24,16},{28,20},{9,1},{13,5},{17,9},{2... | collective-permute-start | bytes 786440 | tf_op jit(solution)/shard_map/ppermute | solution.py:469
  154.5 11.4 %collective-permute-start.15 = (bf16[512,256]{1,0:T(8,128)(2,1)}, bf16[512,256]{1,0:T(8,128)(2,1)S(1)}, u32[]{:S(2)}, u32[]{:S(2)}) collective-permute-start(bf16[512,256]{1,0:T(8,128)(2,1)} %get-tuple-element.52), channel_id=1, source_target_pairs={{4,0},{8,4},{12,8},{16,12},{20,16},{24,20},{28,24},{5,1},{9,5},{13... | collective-permute-start | bytes 786440 | tf_op jit(solution)/shard_map/ppermute | solution.py:469
  190.2 8.4 %collective-permute-start.18 = (bf16[4,672,256]{2,1,0:T(8,128)(2,1)}, bf16[4,672,256]{2,1,0:T(8,128)(2,1)S(1)}, u32[]{:S(2)}, u32[]{:S(2)}) collective-permute-start(bf16[4,672,256]{2,1,0:T(8,128)(2,1)} %get-tuple-element.67), channel_id=1, source_target_pairs={{0,4},{4,0},{8,12},{12,8},{16,20},{20,16},{24,28},{28,24},{1,5},{5... | collective-permute-start | bytes 4128776 | tf_op jit(solution)/shard_map/ppermute | solution.py:344
  197.9 9.4 %collective-permute-start.23 = (bf16[4,672,256]{2,1,0:T(8,128)(2,1)}, bf16[4,672,256]{2,1,0:T(8,128)(2,1)S(1)}, u32[]{:S(2)}, u32[]{:S(2)}) collective-permute-start(bf16[4,672,256]{2,1,0:T(8,128)(2,1)} %get-tuple-element.77), channel_id=1, source_target_pairs={{0,4},{4,0},{8,12},{12,8},{16,20},{20,16},{24,28},{28,24},{1,5},{5... | collective-permute-start | bytes 4128776 | tf_op jit(solution)/shard_map/ppermute | solution.py:344
  203.8 12.0 %collective-permute-start.19 = (bf16[2,672,128]{2,1,0:T(8,128)(2,1)}, bf16[2,672,128]{2,1,0:T(8,128)(2,1)S(1)}, u32[]{:S(2)}, u32[]{:S(2)}) collective-permute-start(bf16[2,672,128]{2,1,0:T(8,128)(2,1)} %get-tuple-element.70), channel_id=1, source_target_pairs={{0,8},{4,12},{8,0},{12,4},{16,24},{20,28},{24,16},{28,20},{1,9},{5... | collective-permute-start | bytes 1032200 | tf_op jit(solution)/shard_map/ppermute | solution.py:344
  206.7 10.7 %collective-permute-start.20 = (bf16[2,672,128]{2,1,0:T(8,128)(2,1)}, bf16[2,672,128]{2,1,0:T(8,128)(2,1)S(1)}, u32[]{:S(2)}, u32[]{:S(2)}) collective-permute-start(bf16[2,672,128]{2,1,0:T(8,128)(2,1)} %get-tuple-element.71), channel_id=1, source_target_pairs={{0,16},{4,20},{8,24},{12,28},{16,0},{20,4},{24,8},{28,12},{1,17},{... | collective-permute-start | bytes 1032200 | tf_op jit(solution)/shard_map/ppermute | solution.py:344
  212.5 10.6 %collective-permute-start.24 = (bf16[2,672,128]{2,1,0:T(8,128)(2,1)}, bf16[2,672,128]{2,1,0:T(8,128)(2,1)S(1)}, u32[]{:S(2)}, u32[]{:S(2)}) collective-permute-start(bf16[2,672,128]{2,1,0:T(8,128)(2,1)} %get-tuple-element.80), channel_id=1, source_target_pairs={{0,8},{4,12},{8,0},{12,4},{16,24},{20,28},{24,16},{28,20},{1,9},{5... | collective-permute-start | bytes 1032200 | tf_op jit(solution)/shard_map/ppermute | solution.py:344
  214.3 11.2 %collective-permute-start.25 = (bf16[2,672,128]{2,1,0:T(8,128)(2,1)}, bf16[2,672,128]{2,1,0:T(8,128)(2,1)S(1)}, u32[]{:S(2)}, u32[]{:S(2)}) collective-permute-start(bf16[2,672,128]{2,1,0:T(8,128)(2,1)} %get-tuple-element.81), channel_id=1, source_target_pairs={{0,16},{4,20},{8,24},{12,28},{16,0},{20,4},{24,8},{28,12},{1,17},{... | collective-permute-start | bytes 1032200 | tf_op jit(solution)/shard_map/ppermute | solution.py:344
  220.4 10.9 %collective-permute-start.21 = (bf16[1,672,128]{2,1,0:T(8,128)(2,1)}, bf16[1,672,128]{2,1,0:T(8,128)(2,1)S(1)}, u32[]{:S(2)}, u32[]{:S(2)}) collective-permute-start(bf16[1,672,128]{2,1,0:T(8,128)(2,1)} %get-tuple-element.74), channel_id=1, source_target_pairs={{0,16},{4,20},{8,24},{12,28},{16,0},{20,4},{24,8},{28,12},{1,17},{... | collective-permute-start | bytes 516104 | tf_op jit(solution)/shard_map/ppermute | solution.py:344
  221.3 10.1 %collective-permute-start.22 = (bf16[1,672,128]{2,1,0:T(8,128)(2,1)}, bf16[1,672,128]{2,1,0:T(8,128)(2,1)S(1)}, u32[]{:S(2)}, u32[]{:S(2)}) collective-permute-start(bf16[1,672,128]{2,1,0:T(8,128)(2,1)} %get-tuple-element.75), channel_id=1, source_target_pairs={{0,8},{4,12},{8,0},{12,4},{16,24},{20,28},{24,16},{28,20},{1,9},{5... | collective-permute-start | bytes 516104 | tf_op jit(solution)/shard_map/ppermute | solution.py:344
  (38 other events, 395.2 us)
Sparse Core Ops, SparseCore 0:
  184.5 104.5 reduce-scatter.1

commit v2 on v1

--- a/solution.py
+++ b/solution.py
@@ -12,7 +12,6 @@
 EPSILON = 1e-06
 QUERY_SCALE = 168.0 ** (-0.5)
 ROPE_BASE = 10000.0
-VMEM_BYTES = 56 * 1024 * 1024
 SMEM = pltpu.SMEM
 
 
@@ -75,65 +74,172 @@
     return pl.BlockSpec(memory_space=SMEM)
 
 
+def after(value, others):
+    return lax.optimization_barrier((value, others))[0]
+
+
 def cost(flops, *arrays):
     size = sum(math.prod(a.shape) * jnp.dtype(a.dtype).itemsize for a in arrays)
     return pl.CostEstimate(flops=flops, bytes_accessed=size, transcendentals=0)
 
 
-def params():
-    return pltpu.CompilerParams(vmem_limit_bytes=VMEM_BYTES)
+def params(megabytes=30):
+    return pltpu.CompilerParams(vmem_limit_bytes=megabytes * 1024 * 1024)
+
+
+def start_all(copies):
+    for copy in copies:
+        copy.start()
+
+
+def wait_all(copies):
+    for copy in copies:
+        copy.wait()
+
+
+def piece_copies(places, seq_index, arrays, target, sems):
+    copies = []
+    for number, (offset, low) in enumerate(places):
+        rows, cols = arrays[number].shape
+        start = pl.multiple_of(jnp.bitwise_xor(seq_index, offset) * rows, 16)
+        slot = target.at[pl.ds(start, rows), pl.ds(low, cols)]
+        copies.append(pltpu.make_async_copy(arrays[number], slot, sems.at[number]))
+    return copies
+
+
+def store_heads(key_value, raw_keys, rows, keys, values, k_gain, cos_rows, sin_rows):
+    head_size = k_gain.shape[1]
+    raw_keys[rows, :] = keys.astype(raw_keys.dtype)
+    for head in range(keys.shape[1] // head_size):
+        cols = slice(head * head_size, (head + 1) * head_size)
+        low = 2 * head * head_size
+        head_keys = keys[:, cols]
+        turned = rope(head_keys * inv_rms(head_keys) * k_gain[...], cos_rows, sin_rows)
+        key_value[rows, low : low + head_size] = turned.astype(jnp.bfloat16)
+        key_value[rows, low + head_size : low + 2 * head_size] = values[:, cols].astype(jnp.bfloat16)
 
 
 def project_body(count, info, gain, k_gain, cosine, sine, w_key, w_value, *rest):
     blocks = rest[:count]
-    normed, key_value, raw_keys, held, sem = rest[count:]
+    key_value, raw_keys, normed, held, key_held, value_held, sems = rest[count:]
     rows = held.shape[0]
-    head_size = k_gain.shape[1]
+
+    def block_copy(index):
+        return pltpu.make_async_copy(blocks[index], held, sems.at[2])
+
     for index in range(count):
-
-        @pl.when(info[0] == index)
-        def _():
-            copy = pltpu.make_async_copy(blocks[index], held, sem)
-            copy.start()
-            copy.wait()
-
+        pl.when(info[0] == index)(lambda index=index: block_copy(index).start())
+    own_copies = [
+        pltpu.make_async_copy(w_key, key_held, sems.at[0]),
+        pltpu.make_async_copy(w_value, value_held, sems.at[1]),
+    ]
+    start_all(own_copies)
+    for index in range(count):
+        pl.when(info[0] == index)(lambda index=index: block_copy(index).wait())
     values = held[...].astype(jnp.float32)
     normed[...] = (values * inv_rms(values) * gain[...]).astype(jnp.bfloat16)
-    keys = jnp.dot(normed[...], w_key[...], preferred_element_type=jnp.float32)
-    raw_keys[...] = keys
-    vals = jnp.dot(normed[...], w_value[...], preferred_element_type=jnp.float32)
     place = pl.ds(pl.multiple_of(info[1] * rows, rows), rows)
-    cos_rows = cosine[place, :]
-    sin_rows = sine[place, :]
-    for head in range(w_key.shape[1] // head_size):
-        cols = slice(head * head_size, (head + 1) * head_size)
-        head_keys = keys[:, cols]
-        turned = rope(head_keys * inv_rms(head_keys) * k_gain[...], cos_rows, sin_rows)
-        low = 2 * head * head_size
-        key_value[:, low : low + head_size] = turned.astype(jnp.bfloat16)
-        key_value[:, low + head_size : low + 2 * head_size] = vals[:, cols].astype(jnp.bfloat16)
+    wait_all(own_copies)
+    keys = jnp.dot(normed[...], key_held[...], preferred_element_type=jnp.float32)
+    vals = jnp.dot(normed[...], value_held[...], preferred_element_type=jnp.float32)
+    store_heads(key_value, raw_keys, slice(0, rows), keys, vals, k_gain, cosine[place, :], sine[place, :])
 
 
 def project(info, blocks, in_gain, k_gain, cosine, sine, w_key, w_value):
     rows, width = blocks[0].shape
     cols = w_key.shape[1]
-    outs = (
+    outs = [
+        jax.ShapeDtypeStruct((rows, 2 * cols), jnp.bfloat16),
+        jax.ShapeDtypeStruct((rows, cols), jnp.bfloat16),
         jax.ShapeDtypeStruct((rows, width), jnp.bfloat16),
-        jax.ShapeDtypeStruct((rows, 2 * cols), jnp.bfloat16),
-        jax.ShapeDtypeStruct((rows, cols), jnp.float32),
-    )
-    dense = (in_gain, k_gain, cosine, sine, w_key, w_value)
+    ]
+    scratch = [
+        pltpu.VMEM((rows, width), jnp.bfloat16),
+        pltpu.VMEM((width, cols), jnp.bfloat16),
+        pltpu.VMEM((width, cols), jnp.bfloat16),
+        pltpu.SemaphoreType.DMA((3,)),
+    ]
+    dense = (in_gain, k_gain, cosine, sine)
     return pl.pallas_call(
         functools.partial(project_body, len(blocks)),
         name="project_block",
         grid=(1,),
+        out_shape=tuple(outs),
+        in_specs=[smem_spec()] + [full_spec(a) for a in dense] + [any_spec()] * (2 + len(blocks)),
+        out_specs=tuple(full_spec(o) for o in outs),
+        scratch_shapes=scratch,
+        compiler_params=params(56),
+        cost_estimate=cost(4 * rows * width * cols, blocks[0], w_key, w_value, *outs),
+    )(info, *dense, w_key, w_value, *blocks)
+
+
+def project_pair_body(places, info, gain, k_gain, cosine, sine, w_key, w_value, ready, block, *rest):
+    pieces = rest[: len(places)]
+    key_value, raw_keys, normed, far_key_value, far_keys = rest[len(places) : len(places) + 5]
+    held, left, key_held, value_held, far_held, sems, far_sems = rest[len(places) + 5 :]
+    rows, width = held.shape
+    cols = w_key.shape[1]
+    block_copy = pltpu.make_async_copy(block, held, sems.at[2])
+    block_copy.start()
+    ready_copy = pltpu.make_async_copy(ready, left.at[pl.ds(0, rows)], sems.at[3])
+    ready_copy.start()
+    far_copies = piece_copies(places, info[0], pieces, far_held, far_sems)
+    start_all(far_copies)
+    own_copies = [
+        pltpu.make_async_copy(w_key, key_held, sems.at[0]),
+        pltpu.make_async_copy(w_value, value_held, sems.at[1]),
+    ]
+    start_all(own_copies)
+    block_copy.wait()
+    values = held[...].astype(jnp.float32)
+    normed[...] = (values * inv_rms(values) * gain[...]).astype(jnp.bfloat16)
+    ready_copy.wait()
+    left[rows:, :] = normed[...]
+    wait_all(far_copies)
+    both = jnp.dot(left[...], far_held[...], preferred_element_type=jnp.float32)
+    for number in range(2):
+        place = pl.ds(pl.multiple_of(info[1 + number] * rows, rows), rows)
+        span = slice(number * rows, (number + 1) * rows)
+        part = both[span]
+        store_heads(
+            far_key_value, far_keys, span, part[:, :cols], part[:, cols:], k_gain, cosine[place, :], sine[place, :]
+        )
+    place = pl.ds(pl.multiple_of(info[2] * rows, rows), rows)
+    wait_all(own_copies)
+    keys = jnp.dot(normed[...], key_held[...], preferred_element_type=jnp.float32)
+    vals = jnp.dot(normed[...], value_held[...], preferred_element_type=jnp.float32)
+    store_heads(key_value, raw_keys, slice(0, rows), keys, vals, k_gain, cosine[place, :], sine[place, :])
+
+
+def project_pair(info, ready, block, in_gain, k_gain, cosine, sine, w_key, w_value, pieces):
+    rows, width = block.shape
+    cols = w_key.shape[1]
+    places = [(offset, low) for offset, low, _ in pieces]
+    arrays = [piece for _, _, piece in pieces]
+    outs = tuple(
+        jax.ShapeDtypeStruct(shape, jnp.bfloat16)
+        for shape in ((rows, 2 * cols), (rows, cols), (rows, width), (2 * rows, 2 * cols), (2 * rows, cols))
+    )
+    dense = (in_gain, k_gain, cosine, sine)
+    return pl.pallas_call(
+        functools.partial(project_pair_body, places),
+        name="project_pair",
+        grid=(1,),
         out_shape=outs,
-        in_specs=[smem_spec()] + [full_spec(a) for a in dense] + [any_spec()] * len(blocks),
-        out_specs=[full_spec(o) for o in outs],
-        scratch_shapes=[pltpu.VMEM((rows, width), jnp.bfloat16), pltpu.SemaphoreType.DMA],
-        compiler_params=params(),
-        cost_estimate=cost(4 * rows * width * cols, blocks[0], w_key, w_value, *outs),
-    )(info, *dense, *blocks)
+        in_specs=[smem_spec()] + [full_spec(a) for a in dense] + [any_spec()] * (4 + len(arrays)),
+        out_specs=tuple(full_spec(o) for o in outs),
+        scratch_shapes=[
+            pltpu.VMEM((rows, width), jnp.bfloat16),
+            pltpu.VMEM((2 * rows, width), jnp.bfloat16),
+            pltpu.VMEM((width, cols), jnp.bfloat16),
+            pltpu.VMEM((width, cols), jnp.bfloat16),
+            pltpu.VMEM((width, 2 * cols), jnp.bfloat16),
+            pltpu.SemaphoreType.DMA((4,)),
+            pltpu.SemaphoreType.DMA((len(arrays),)),
+        ],
+        compiler_params=params(56),
+        cost_estimate=cost(12 * rows * width * cols, block, w_key, w_value, *arrays, *outs),
+    )(info, *dense, w_key, w_value, ready, block, *arrays)
 
 
 def attend_body(reach, slots, info, lowest, q_gain, cosine, sine, queries, grads, *rest):
@@ -206,9 +312,10 @@
     rows = queries.shape[0]
     head_size = q_gain.shape[1]
     slots = len(blocks) // (reach + 1)
-    tile = blocks[0].shape[0]
+    tile = rows // slots
     cols = queries.shape[1] // kv_heads
     pick = lambda *_: (0, head)
+    arrays = [array for array, _ in blocks]
     outs = (
         jax.ShapeDtypeStruct((rows, cols), jnp.bfloat16),
         jax.ShapeDtypeStruct((rows, 2 * head_size), jnp.float32),
@@ -223,19 +330,21 @@
         in_specs=[smem_spec()]
         + [full_spec(a) for a in dense]
         + [pl.BlockSpec((rows, cols), pick)] * 2
-        + [pl.BlockSpec((tile, 2 * head_size), pick)] * len(blocks),
+        + [pl.BlockSpec((tile, 2 * head_size), lambda *_, row=row: (row, head)) for _, row in blocks],
         out_specs=[full_spec(o) for o in outs],
         scratch_shapes=[pltpu.VMEM((window, head_size), jnp.bfloat16)] * 2
         + [pltpu.VMEM((window, head_size), jnp.float32)] * 2,
-        compiler_params=params(),
-        cost_estimate=cost(10 * rows * window * cols, queries, grads, *blocks, *outs),
-    )(info, *dense, queries, grads, *blocks)
-
-
-def finish_body(reach, slots, info, k_gain, cosine, sine, own, *rest):
+        compiler_params=params(56),
+        cost_estimate=cost(10 * rows * window * cols, queries, grads, *outs),
+    )(info, *dense, queries, grads, *arrays)
+
+
+def finish_body(reach, slots, earlier, info, k_gain, cosine, sine, own, *rest):
     arrived = rest[:reach]
     raw_keys = rest[reach : reach + slots]
-    result = rest[reach + slots]
+    before = rest[reach + slots : reach + slots + earlier]
+    outs = rest[reach + slots + earlier :]
+    result = outs[0]
     head_size = k_gain.shape[1]
     rows = raw_keys[0].shape[0]
     for slot in range(slots):
@@ -243,29 +352,46 @@
         total = own[place, :]
         for part in arrived:
             total = total + part[place, :].astype(jnp.float32)
-        values = raw_keys[slot][...]
+        values = raw_keys[slot][...].astype(jnp.float32)
         turned = rope_back(total[:, :head_size], cosine[place, :], sine[place, :])
         keys = norm_back(turned, values, inv_rms(values), k_gain[...])
         result[place, :head_size] = keys.astype(jnp.bfloat16)
         result[place, head_size:] = total[:, head_size:].astype(jnp.bfloat16)
-
-
-def finish(head, info, k_gain, cosine, sine, own, arrived, raw_keys):
+    if len(outs) > 1:
+        joined, away = outs[1:]
+        for head, part in enumerate((*before, result)):
+            joined[:, 2 * head * head_size : 2 * (head + 1) * head_size] = part[...]
+        for number, slot in enumerate((1, 3)):
+            place = pl.ds(pl.multiple_of(info[slot] * rows, 16), rows)
+            away[number * rows : (number + 1) * rows, :] = joined[place, :]
+
+
+def finish(head, info, k_gain, cosine, sine, own, arrived, raw_keys, before=None):
+    rows, cols = own.shape
     head_size = k_gain.shape[1]
-    out = jax.ShapeDtypeStruct(own.shape, jnp.bfloat16)
+    slots = len(raw_keys)
+    tile = rows // slots
+    arrays = [array for array, _ in raw_keys]
+    outs = [jax.ShapeDtypeStruct(own.shape, jnp.bfloat16)]
+    if before is not None:
+        width = cols * (len(before) + 1)
+        outs += [jax.ShapeDtypeStruct((count, width), jnp.bfloat16) for count in (rows, 2 * tile)]
+    before = before or []
     dense = (k_gain, cosine, sine, own, *arrived)
-    return pl.pallas_call(
-        functools.partial(finish_body, len(arrived), len(raw_keys)),
+    results = pl.pallas_call(
+        functools.partial(finish_body, len(arrived), slots, len(before)),
         name="finish_kv",
         grid=(1,),
-        out_shape=out,
+        out_shape=tuple(outs),
         in_specs=[smem_spec()]
         + [full_spec(a) for a in dense]
-        + [pl.BlockSpec((raw_keys[0].shape[0], head_size), lambda *_: (0, head))] * len(raw_keys),
-        out_specs=full_spec(out),
-        compiler_params=params(),
-        cost_estimate=cost(0, own, *arrived, out),
-    )(info, *dense, *raw_keys)
+        + [pl.BlockSpec((tile, head_size), lambda *_, row=row: (row, head)) for _, row in raw_keys]
+        + [full_spec(a) for a in before],
+        out_specs=tuple(full_spec(o) for o in outs),
+        compiler_params=params(56),
+        cost_estimate=cost(0, own, *arrived, *outs),
+    )(info, *dense, *arrays, *before)
+    return list(results)
 
 
 def weight_body(slots, info, grads, *rest):
@@ -323,17 +449,27 @@
                     target[high * inner + low] = total.astype(jnp.bfloat16)
 
 
+def row_steps(rows):
+    return max(n for n in range(1, 5) if rows % (16 * n) == 0) if rows % 16 == 0 else 1
+
+
 def split_sum(info, keeps, arrivals, halves):
     outs = []
     for keep, (cols, outer, inner) in zip(keeps, halves):
         outs += [jax.ShapeDtypeStruct((outer * inner, keep.shape[1], cols.stop - cols.start), jnp.bfloat16)] * 2
+    rows = keeps[0].shape[1]
+    steps = row_steps(rows)
+
+    def spec(array):
+        return pl.BlockSpec((array.shape[0], rows // steps, array.shape[2]), lambda step: (0, step, 0))
+
     return pl.pallas_call(
         functools.partial(split_body, halves),
         name="split_sum",
-        grid=(1,),
+        grid=(steps,),
         out_shape=tuple(outs),
-        in_specs=[smem_spec()] + [full_spec(a) for a in (*keeps, *arrivals)],
-        out_specs=tuple(full_spec(o) for o in outs),
+        in_specs=[smem_spec()] + [spec(a) for a in (*keeps, *arrivals)],
+        out_specs=tuple(spec(o) for o in outs),
         compiler_params=params(),
         cost_estimate=cost(0, *keeps, *arrivals, *outs),
     )(info, *keeps, *arrivals)
@@ -380,17 +516,149 @@
 
 def gather_heads(parts, heads):
     _, rows, cols = parts[0].shape
+    steps = row_steps(rows)
     out = jax.ShapeDtypeStruct((rows, cols * heads), jnp.float32)
+    out_spec = pl.BlockSpec((rows // steps, cols * heads), lambda step: (step, 0))
     return pl.pallas_call(
         functools.partial(gather_body, heads),
         name="gather_heads",
-        grid=(1,),
+        grid=(steps,),
         out_shape=(out, out),
-        in_specs=[full_spec(a) for a in parts],
-        out_specs=(full_spec(out), full_spec(out)),
+        in_specs=[pl.BlockSpec((1, rows // steps, cols), lambda step: (0, step, 0)) for a in parts],
+        out_specs=(out_spec, out_spec),
         compiler_params=params(),
         cost_estimate=cost(0, *parts, out, out),
     )(*parts)
+
+
+def input_terms_body(heads, w_key, w_value, *rest):
+    grads, out = rest[:heads], rest[heads]
+    size = grads[0].shape[1] // 2
+    left = jnp.concatenate([g[:, :size] for g in grads] + [g[:, size:] for g in grads], axis=1)
+    right = jnp.concatenate([w_key[...], w_value[...]], axis=1)
+    out[...] = dot_last(left, right).astype(jnp.bfloat16)
+
+
+def input_terms(kv_grads, w_key, w_value, skip):
+    width, cols = w_key.shape
+    rows = kv_grads[0].shape[0]
+    common = math.gcd(skip, width - skip)
+    tile = max(t for t in range(128, 1025, 128) if common % t == 0)
+    out = jax.ShapeDtypeStruct((rows, width - skip), jnp.bfloat16)
+    weight_spec = pl.BlockSpec((tile, cols), lambda step: (step + skip // tile, 0))
+    return pl.pallas_call(
+        functools.partial(input_terms_body, len(kv_grads)),
+        name="input_terms",
+        grid=((width - skip) // tile,),
+        out_shape=out,
+        in_specs=[weight_spec, weight_spec] + [full_spec(g) for g in kv_grads],
+        out_specs=pl.BlockSpec((rows, tile), lambda step: (0, step)),
+        compiler_params=params(),
+        cost_estimate=cost(4 * rows * (width - skip) * cols, out, *kv_grads),
+    )(w_key, w_value, *kv_grads)
+
+
+def pair_body(places, heads, info, w_key, w_value, joined, arrived, *rest):
+    pieces = rest[: len(places)]
+    away_out, own_out, key_held, value_held, held, own_sems, sems = rest[len(places) :]
+    rows, width = own_out.shape
+    size = w_key.shape[1] // heads
+    own_copies = [
+        pltpu.make_async_copy(w_key, key_held, own_sems.at[0]),
+        pltpu.make_async_copy(w_value, value_held, own_sems.at[1]),
+    ]
+    start_all(own_copies)
+    copies = piece_copies(places, info[0], pieces, held, sems)
+    start_all(copies)
+    own_rows = jnp.concatenate(
+        [joined[pl.ds(pl.multiple_of(info[1 + number] * rows, rows), rows), :] for number in range(2)], axis=0
+    )
+    sides = [
+        block[:, (2 * head + side) * size : (2 * head + side + 1) * size]
+        for block in (own_rows, arrived[...])
+        for side in range(2)
+        for head in range(heads)
+    ]
+    left = jnp.concatenate(sides, axis=1)
+    wait_all(own_copies)
+    wait_all(copies)
+    tile = max(t for t in range(128, 1025, 128) if width % t == 0)
+    for low in range(0, width, tile):
+        span = slice(low, low + tile)
+        right = jnp.concatenate([key_held[span, :], value_held[span, :], held[span, :]], axis=1)
+        total = dot_last(left, right)
+        own_out[:, span] = total[:rows]
+        away_out[:, span] = total[rows:].astype(jnp.bfloat16)
+
+
+def pair_terms(info, joined, arrived, pieces, w_key, w_value, heads):
+    rows = arrived.shape[0] // 2
+    width, cols = w_key.shape
+    places = [(offset, low) for offset, low, _ in pieces]
+    arrays = [piece for _, _, piece in pieces]
+    outs = (jax.ShapeDtypeStruct((rows, width), jnp.bfloat16), jax.ShapeDtypeStruct((rows, width), jnp.float32))
+    return pl.pallas_call(
+        functools.partial(pair_body, places, heads),
+        name="pair_terms",
+        grid=(1,),
+        out_shape=outs,
+        in_specs=[smem_spec(), any_spec(), any_spec(), full_spec(joined), full_spec(arrived)]
+        + [any_spec()] * len(arrays),
+        out_specs=tuple(full_spec(o) for o in outs),
+        scratch_shapes=[
+            pltpu.VMEM((width, cols), jnp.bfloat16),
+            pltpu.VMEM((width, cols), jnp.bfloat16),
+            pltpu.VMEM((width, 2 * cols), jnp.bfloat16),
+            pltpu.SemaphoreType.DMA((2,)),
+            pltpu.SemaphoreType.DMA((len(arrays),)),
+        ],
+        compiler_params=params(56),
+        cost_estimate=cost(16 * rows * width * cols, w_key, w_value, *arrays, *outs),
+    )(info, w_key, w_value, joined, arrived, *arrays)
+
+
+def input_grad_body(sums, rest_count, tokens, gain, *rest):
+    out = rest[-1]
+    values = tokens[...].astype(jnp.float32)
+    parts = []
+    if sums:
+        total = rest[0][...].astype(jnp.float32)
+        for piece in rest[1:sums]:
+            total = total + piece[...].astype(jnp.float32)
+        parts.append(total)
+    parts += [piece[...].astype(jnp.float32) for piece in rest[sums : sums + rest_count]]
+    grads = jnp.concatenate(parts, axis=1) if len(parts) > 1 else parts[0]
+    out[...] = norm_back(grads, values, inv_rms(values), gain[...]).astype(jnp.bfloat16)
+
+
+def input_grad(tokens, gain, sums, others):
+    out = jax.ShapeDtypeStruct(tokens.shape, jnp.bfloat16)
+    rows = tokens.shape[0]
+    tile = 32 if rows % 32 == 0 else rows
+    spec = lambda array: pl.BlockSpec((tile, array.shape[1]), lambda step: (step, 0))
+    return pl.pallas_call(
+        functools.partial(input_grad_body, len(sums), len(others)),
+        name="input_grad",
+        grid=(rows // tile,),
+        out_shape=out,
+        in_specs=[spec(tokens), full_spec(gain)] + [spec(a) for a in (*sums, *others)],
+        out_specs=spec(out),
+        compiler_params=params(),
+        cost_estimate=cost(0, tokens, *sums, *others, out),
+    )(tokens, gain, *sums, *others)
+
+
+def spread_corners(parts):
+    half = parts[0].shape[1] // 2
+    return [swap(parts[1][:, :half], 2), swap(parts[2][:, half:], 1)]
+
+
+def spread_end(arrays):
+    half = arrays[0].shape[1] // 2
+    spots = [(0, 0), (2, 0), (4, 0), (6, 0), (6, half)]
+    return [(offset, low, array) for (offset, low), array in zip(spots, arrays)] + [
+        (offset + 1, low, swap(array, 0)) for (offset, low), array in zip(spots, arrays)
+    ]
 
 
 def arrival_table(count):
@@ -406,32 +674,38 @@
     return table
 
 
-def shards(tokens, in_gain, raw_queries, w_key, w_value, q_gain, k_gain, doc_lengths, out_grad):
+def halo_of(key_value, reach):
+    seq_count = lax.axis_size("seq")
+    sent = []
+    for distance in range(1, reach + 1):
+        pairs = [(i, i + distance) for i in range(seq_count - distance)]
+        sent.append(lax.ppermute(key_value, "seq", pairs))
+    return sent
+
+
+def halo_back(sections):
+    seq_count = lax.axis_size("seq")
+    back = []
+    for section, array in enumerate(sections):
+        distance = len(sections) - section
+        pairs = [(i + distance, i) for i in range(seq_count - distance)]
+        back.append(lax.ppermute(array, "seq", pairs))
+    return back
+
+
+def shards_general(tokens, dense, rope_rows, lowest, raw_queries, out_grad, w_key, w_value, reach):
+    gain_row, q_row, k_row = dense
+    cosine, sine = rope_rows
     tp_count = lax.axis_size("tp")
-    seq_count = lax.axis_size("seq")
-    head_size = q_gain.shape[0]
+    place = lax.axis_index("tp").astype(jnp.int32)
+    rows = tokens.shape[0]
+    head_size = q_row.shape[1]
     kv_heads = w_key.shape[1] // head_size
-    rows, width = tokens.shape
-    shard_rows = rows * tp_count
-    reach = (WINDOW - 2) // shard_rows + 1
-    seq_index = lax.axis_index("seq")
-    tp_index = lax.axis_index("tp")
-    first_row = seq_index * shard_rows
-    positions = first_row + jnp.arange(shard_rows, dtype=jnp.int32)
-    begins = doc_begin(doc_lengths, positions)
-    cosine, sine = rope_tables(positions - begins, head_size)
-    lowest = jnp.maximum(begins, positions - (WINDOW - 1)) - (first_row - reach * shard_rows)
-    lowest = lowest[:, None]
-    gain_row = in_gain[None, :]
-    q_row = q_gain[None, :]
-    k_row = k_gain[None, :]
-
     table = arrival_table(tp_count)
     picks = jnp.array(table, dtype=jnp.int32).reshape(tp_count, tp_count - 1, 2)
-    picks = lax.dynamic_index_in_dim(picks, tp_index, 0, keepdims=False)
-    infos = [jnp.stack([jnp.int32(0), tp_index.astype(jnp.int32)])] + [picks[i] for i in range(tp_count - 1)]
-    slot_places = jnp.concatenate([tp_index.astype(jnp.int32)[None], picks[:, 1]])
-
+    picks = lax.dynamic_index_in_dim(picks, place, 0, keepdims=False)
+    infos = [jnp.stack([jnp.int32(0), place])] + [picks[i] for i in range(tp_count - 1)]
+    slot_places = jnp.concatenate([place[None], picks[:, 1]])
     normed_blocks, kv_blocks, raw_keys = [], [], []
     halo = [[] for _ in range(reach)]
     arrivals = []
@@ -439,63 +713,132 @@
     for slot in range(tp_count):
         candidates = [tokens] if slot == 0 else list(arrivals)
         if slot < tp_count - 1:
-            up_pairs = [(i, i + 1) for i in range(slot, tp_count - 1)]
-            down_pairs = [(i + 1, i) for i in range(tp_count - 1 - slot)]
-            going_up = lax.ppermute(going_up, "tp", up_pairs)
-            going_down = lax.ppermute(going_down, "tp", down_pairs)
+            going_up = lax.ppermute(going_up, "tp", [(i, i + 1) for i in range(slot, tp_count - 1)])
+            going_down = lax.ppermute(going_down, "tp", [(i + 1, i) for i in range(tp_count - 1 - slot)])
             arrivals += [going_up, going_down]
-        normed, key_value, keys = project(
-            infos[slot], candidates, gain_row, k_row, cosine, sine, w_key, w_value
-        )
+        key_value, keys, normed = project(infos[slot], candidates, gain_row, k_row, cosine, sine, w_key, w_value)
         normed_blocks.append(normed)
         kv_blocks.append(key_value)
-        raw_keys.append(keys)
-        for distance in range(1, reach + 1):
-            pairs = [(i, i + distance) for i in range(seq_count - distance)]
-            halo[distance - 1].append(lax.ppermute(key_value, "seq", pairs))
-
-    blocks = []
-    for distance in range(reach, 0, -1):
-        blocks += halo[distance - 1]
-    blocks += kv_blocks
+        raw_keys.append((keys, 0))
+        for distance, sent in enumerate(halo_of(key_value, reach)):
+            halo[distance].append((sent, 0))
+    blocks = [block for distance in range(reach, 0, -1) for block in halo[distance - 1]]
+    blocks += [(block, 0) for block in kv_blocks]
     query_parts, kv_grads = [], []
     for head in range(kv_heads):
         outs = attend(head, kv_heads, reach, slot_places, lowest, q_row, cosine, sine, raw_queries, out_grad, blocks)
         query_parts.append(outs[0])
-        back = []
-        for section in range(reach):
-            distance = reach - section
-            pairs = [(i + distance, i) for i in range(seq_count - distance)]
-            back.append(lax.ppermute(outs[2 + section], "seq", pairs))
-        kv_grads.append(finish(head, slot_places, k_row, cosine, sine, outs[1], back, raw_keys))
+        back = halo_back(outs[2:])
+        kv_grads += finish(head, slot_places, k_row, cosine, sine, outs[1], back, raw_keys)
     grad_queries = jnp.concatenate(query_parts, axis=1)
-
-    grad_k = jnp.concatenate([g[:, :head_size] for g in kv_grads], axis=1)
-    grad_v = jnp.concatenate([g[:, head_size:] for g in kv_grads], axis=1)
-    partial_sum = dot_last(grad_k, w_key) + dot_last(grad_v, w_value)
-    normed_grad = lax.psum_scatter(
-        partial_sum.astype(jnp.bfloat16), "tp", scatter_dimension=0, tiled=True
-    ).astype(jnp.float32)
-    x_float = tokens.astype(jnp.float32)
-    grad_x = norm_back(normed_grad, x_float, inv_rms(x_float), gain_row).astype(jnp.bfloat16)
-
+    partial_sum = input_terms(kv_grads, w_key, w_value, 0)
+    summed_part = lax.psum_scatter(partial_sum, "tp", scatter_dimension=0, tiled=True)
+    grad_x = input_grad(tokens, gain_row, [], [summed_part])
+    left = jnp.concatenate(normed_blocks, axis=0)
+    order = (slot_places[:, None] * rows + jnp.arange(rows, dtype=jnp.int32)[None, :]).reshape(-1)
+    joined = [g[:, :head_size] for g in kv_grads] + [g[:, head_size:] for g in kv_grads]
+    right = jnp.take(jnp.concatenate(joined, axis=1), order, axis=0)
+    summed = lax.psum_scatter(dot_first(left, right), "seq", scatter_dimension=0, tiled=True)
+    return (grad_x, grad_queries, summed[:, : w_key.shape[1]], summed[:, w_key.shape[1] :])
+
+
+def trade(array, distance):
+    return lax.ppermute(array, "tp", [(i, i ^ distance) for i in range(lax.axis_size("tp"))])
+
+
+def shards_paired(tokens, dense, rope_rows, lowest, raw_queries, out_grad, w_key, w_value, reach):
+    gain_row, q_row, k_row = dense
+    cosine, sine = rope_rows
+    seq_count = lax.axis_size("seq")
+    seq_index = lax.axis_index("seq").astype(jnp.int32)
+    place = lax.axis_index("tp").astype(jnp.int32)
+    width, cols = w_key.shape
+    head_size = q_row.shape[1]
+    kv_heads = cols // head_size
     chunk = width // seq_count
-    if chunk % 16 == 0 and seq_count & (seq_count - 1) == 0 and seq_count > 1 and width % math.lcm(2 * chunk, 128) == 0:
-        info = jnp.concatenate([slot_places, (seq_index & 1).astype(jnp.int32)[None]])
-        parts = []
-        for head in range(kv_heads):
-            send, keep = weight_terms(info, kv_grads[head], normed_blocks, chunk)
-            keeps, comings = scatter_sum(send, keep)
-            parts += [*keeps, *comings]
-        grad_wk, grad_wv = gather_heads(parts, kv_heads)
-    else:
-        left = jnp.concatenate(normed_blocks, axis=0)
-        order = (slot_places[:, None] * rows + jnp.arange(rows, dtype=jnp.int32)[None, :]).reshape(-1)
-        right = jnp.take(jnp.concatenate([grad_k, grad_v], axis=1), order, axis=0)
-        summed = lax.psum_scatter(dot_first(left, right), "seq", scatter_dimension=0, tiled=True)
-        grad_wk = summed[:, : w_key.shape[1]]
-        grad_wv = summed[:, w_key.shape[1] :]
+    zero = jnp.zeros_like(place)
+    slot_places = jnp.stack([place, place ^ 1, place ^ 2, place ^ 3])
+
+    distant = trade(tokens, 2)
+    own_slice = jnp.concatenate(
+        [lax.dynamic_slice_in_dim(weight, seq_index * chunk, chunk, 0) for weight in (w_key, w_value)], axis=1
+    )
+
+    partner_slice = trade(own_slice, 1)
+    spread = [partner_slice, swap(partner_slice, 1), swap(partner_slice, 2)]
+    info = jnp.stack([zero, place])
+    kv_0, keys_0, normed_0 = project(
+        info, [after(tokens, partner_slice)], gain_row, k_row, cosine, sine, w_key, w_value
+    )
+    halo_0 = halo_of(kv_0, reach)
+    partner_normed_0 = trade(normed_0, 1)
+    spread += spread_corners(after(spread, normed_0))
+    pieces = spread_end(spread)
+    info = jnp.stack([seq_index, place, place ^ 2])
+    kv_2, keys_2, normed_2, far_kv, far_keys = project_pair(
+        info, normed_0, after(distant, halo_0), gain_row, k_row, cosine, sine, w_key, w_value, pieces
+    )
+    arrived_kv = trade(far_kv, 1)
+    halo_2 = halo_of(kv_2, reach)
+    halo_far = halo_of(arrived_kv, reach)
+    arrived_keys = trade(after(far_keys, arrived_kv), 1)
+    partner_normed_2 = trade(after(normed_2, (arrived_kv, partner_normed_0)), 1)
+
+    blocks = []
+    for distance in range(reach, 0, -1):
+        outer = halo_far[distance - 1]
+        blocks += [(halo_0[distance - 1], 0), (outer, 0), (halo_2[distance - 1], 0), (outer, 1)]
+    blocks += [(kv_0, 0), (arrived_kv, 0), (kv_2, 0), (arrived_kv, 1)]
+    raw_keys = [(keys_0, 0), (arrived_keys, 0), (keys_2, 0), (arrived_keys, 1)]
+    normed = [normed_0, partner_normed_0, normed_2, partner_normed_2]
+    weight_info = jnp.concatenate([slot_places, (seq_index & 1)[None]])
+    query_parts, kv_grads, terms = [], [], []
+    for head in range(kv_heads):
+        outs = attend(head, kv_heads, reach, slot_places, lowest, q_row, cosine, sine, raw_queries, out_grad, blocks)
+        query_parts.append(outs[0])
+        back = halo_back(outs[2:])
+        before = kv_grads if head == kv_heads - 1 else None
+        results = finish(head, slot_places, k_row, cosine, sine, outs[1], back, raw_keys, before=before)
+        kv_grads = kv_grads + results[:1]
+        terms.append(weight_terms(weight_info, results[0], normed, chunk))
+    grad_queries = jnp.concatenate(query_parts, axis=1)
+
+    joined, away = results[1:]
+    arrived = after(trade(away, 1), terms)
+    info = jnp.stack([seq_index, place, place ^ 2])
+    away_terms, own_terms = pair_terms(info, joined, arrived, pieces, w_key, w_value, kv_heads)
+    other_terms = trade(away_terms, 2)
+    grad_x = input_grad(tokens, gain_row, [own_terms, other_terms], [])
+
+    parts = []
+    for send, keep in terms:
+        keeps, comings = scatter_sum(send, keep)
+        parts += [*keeps, *comings]
+    grad_wk, grad_wv = gather_heads(parts, kv_heads)
     return (grad_x, grad_queries, grad_wk, grad_wv)
+
+
+def shards(tokens, in_gain, raw_queries, w_key, w_value, q_gain, k_gain, doc_lengths, out_grad):
+    seq_count = lax.axis_size("seq")
+    tp_count = lax.axis_size("tp")
+    rows, width = tokens.shape
+    shard_rows = rows * tp_count
+    reach = (WINDOW - 2) // shard_rows + 1
+    first_row = lax.axis_index("seq") * shard_rows
+    positions = first_row + jnp.arange(shard_rows, dtype=jnp.int32)
+    begins = doc_begin(doc_lengths, positions)
+    rope_rows = rope_tables(positions - begins, q_gain.shape[0])
+    lowest = jnp.maximum(begins, positions - (WINDOW - 1)) - (first_row - reach * shard_rows)
+    dense = (in_gain[None, :], q_gain[None, :], k_gain[None, :])
+    chunk = width // seq_count
+    paired = (
+        tp_count == 1 << 2
+        and seq_count == 1 << 3
+        and chunk % 16 == 0
+        and width % math.lcm(2 * chunk, 128) == 0
+    )
+    run = shards_paired if paired else shards_general
+    return run(tokens, dense, rope_rows, lowest[:, None], raw_queries, out_grad, w_key, w_value, reach)
 
 
 def solution(mesh):

time: 301 us -> 248 us (0.82)
  matrix products: 14 us -> 0 us
  waiting for transfers between devices: 124 us -> 110 us
  between operations: 14.6 us -> 1.05 us
  other arithmetic: 12.1 us -> 5.93 us
  Pallas kernels: 72.4 us -> 66.3 us
  starting transfers between devices: 51.1 us -> 54.4 us
    reduce_scatter x1 -> x0, waiting for transfers between devices: 51.6 us -> none  [shards(): lax.psum_scatter(partial_sum.astype(jnp.bfloat16), 'tp', scatter_dimensio...]
    ppermute x18, waiting for transfers between devices: 65 us -> 89.9 us  [the longest x8 81.4 us: trade(): lax.ppermute(array, 'tp', [(i, i ^ distance) for i in range(lax.axis_size...]
    pallas_call x2 -> x5, Pallas kernels: 5.29 us -> 29 us  [the longest x1 10.9 us: pair_terms(): pl.pallas_call(functools.partial(pair_body, places, heads), name='pair_te...]
    pallas_call x4 -> x1, Pallas kernels: 25.4 us -> 6.15 us  [project(): pl.pallas_call(functools.partial(project_body, len(blocks)), name='projec...]
    dot_general x2 -> x0, matrix products: 14 us -> none  [dot_last(): lax.dot_general(left, right, (((1,), (1,)), ((), ())), preferred_element_...]
    ppermute x10 -> x19, waiting for transfers between devices: 7.84 us -> 20.1 us  [swap(): return lax.ppermute(array, 'seq', [(i, i ^ 1 << bit) for i in range(size)])]
    ppermute x10 -> x19, starting transfers between devices: 12.6 us -> 20.7 us  [swap(): return lax.ppermute(array, 'seq', [(i, i ^ 1 << bit) for i in range(size)])]
    pallas_call x4, Pallas kernels: 12.7 us -> 5.98 us  [split_sum(): pl.pallas_call(functools.partial(split_body, halves), name='split_sum', g...]
  transfers between devices with their start and end apart: 29 -> 37, of which waited for: 10 -> 16; matrix products, arithmetic and copies ran while one was open for 4% -> 3% of each run, Pallas kernels for 21% -> 26%
where the time goes in v2:
time: 248 us; the launch traced here: 247 us
  waiting for transfers between devices  110 us (44%)
  Pallas kernels  66.3 us (27%)
  starting transfers between devices  54.4 us (22%)
  local copies, waits for them, and re-layouts  8.82 us (4%)
  other arithmetic  5.93 us (2%)
    ppermute x8, waiting for transfers between devices, trade(): lax.ppermute(array, 'tp', [(i, i ^ distance) for i in range(lax.axis_size...  81.4 us
    ppermute x19, starting transfers between devices, swap(): return lax.ppermute(array, 'seq', [(i, i ^ 1 << bit) for i in range(size)])  20.7 us
    ppermute x19, waiting for transfers between devices, swap(): return lax.ppermute(array, 'seq', [(i, i ^ 1 << bit) for i in range(size)])  20.1 us
    pallas_call x2, Pallas kernels, attend(): pl.pallas_call(functools.partial(attend_body, reach, slots), name='attend...  16 us
    ppermute x6, starting transfers between devices, halo_of(): sent.append(lax.ppermute(key_value, 'seq', pairs))  15.8 us
    ppermute x8, starting transfers between devices, trade(): lax.ppermute(array, 'tp', [(i, i ^ distance) for i in range(lax.axis_size...  12.6 us
    pallas_call x1, Pallas kernels, pair_terms(): pl.pallas_call(functools.partial(pair_body, places, heads), name='pair_te...  10.9 us
    pallas_call x1, Pallas kernels, project_pair(): pl.pallas_call(functools.partial(project_pair_body, places), name='projec...  8.35 us
  transfers between devices with their start and end apart: 37, of which 16 were waited for; matrix products, arithmetic and copies ran while one was open for 3% of the time, Pallas kernels for 26%

profile of v2, /device:TPU:0, one launch (start us, length us, event | category | flops | bytes accessed | tf_op | source)
XLA Modules:
  0.0 246.5 jit_solution(724450852025832756)
XLA Ops:
  2.0 3.1 %collective-permute-start = (bf16[672,512]{1,0:T(8,128)(2,1)S(1)}, bf16[672,512]{1,0:T(8,128)(2,1)}, u32[]{:S(2)}, u32[]{:S(2)}) collective-permute-start(bf16[672,512]{1,0:T(8,128)(2,1)S(1)} %pad_maximum_fusion), channel_id=1, source_target_pairs={{0,1},{1,0},{2,3},{3,2},{4,5},{5,4},{6,7},{7,6},{8,9},{9,8},{10,11... | collective-permute-start | bytes 2064392 | tf_op jit(solution)/shard_map/ppermute | solution.py:746
  7.9 27.3 %collective-permute-done.rest_0_ = bf16[672,512]{1,0:T(8,128)(2,1)} collective-permute-done((bf16[672,512]{1,0:T(8,128)(2,1)S(1)}, bf16[672,512]{1,0:T(8,128)(2,1)}, u32[]{:S(2)}, u32[]{:S(2)}) %collective-permute-start) | collective-permute-done | bytes 688160 | tf_op jit(solution)/shard_map/ppermute | solution.py:746
  41.6 6.1 %project_block.1 = (bf16[128,512]{1,0:T(8,128)(2,1)}, bf16[128,256]{1,0:T(8,128)(2,1)}, bf16[128,5376]{1,0:T(8,128)(2,1)}) custom-call(s32[2]{0:T(128)} %pad_add_fusion.2.info, f32[1,5376]{1,0:T(1,128)} %broadcast_in_dim.32.gain, f32[1,128]{1,0:T(1,128)} %bitcast.15, f32[512,128]{1,0:T(8,128)} %get-tuple-element.107.cosine, ...), custom_call_target="tpu_custom_call" | custom-call | flops 704643072 | bytes 8454144 | tf_op jit(solution)/shard_map/project_block/pallas_call | solution.py:163
  47.9 4.2 %collective-permute-done.4.rest_1_ = bf16[672,512]{1,0:T(8,128)(2,1)S(1)} collective-permute-done((bf16[672,512]{1,0:T(8,128)(2,1)}, bf16[672,512]{1,0:T(8,128)(2,1)S(1)}, u32[]{:S(2)}, u32[]{:S(2)}) %collective-permute-start.4) | collective-permute-done | bytes 688160 | tf_op jit(solution)/shard_map/ppermute | solution.py:480
  52.1 3.2 %collective-permute-start.1 = (bf16[128,512]{1,0:T(8,128)(2,1)}, bf16[128,512]{1,0:T(8,128)(2,1)S(1)}, u32[]{:S(2)}, u32[]{:S(2)}) collective-permute-start(bf16[128,512]{1,0:T(8,128)(2,1)} %get-tuple-element.55.rest_8_), channel_id=1, source_target_pairs={{0,8},{4,12},{8,16},{12,20},{16,24},{20,28},{1,9},{5,13},{9,17},{1... | collective-permute-start | bytes 393224 | tf_op jit(solution)/shard_map/ppermute | solution.py:682
  58.1 3.3 %collective-permute-start.6 = (bf16[672,256]{1,0:T(8,128)(2,1)S(1)}, bf16[672,256]{1,0:T(8,128)(2,1)}, u32[]{:S(2)}, u32[]{:S(2)}) collective-permute-start(bf16[672,256]{1,0:T(8,128)(2,1)S(1)} %slice.6), channel_id=1, source_target_pairs={{0,16},{4,20},{8,24},{12,28},{16,0},{20,4},{24,8},{28,12},{1,17},{... | collective-permute-start | bytes 1032200 | tf_op jit(solution)/shard_map/ppermute | solution.py:480
  63.3 4.0 %collective-permute-done.2.block = bf16[128,5376]{1,0:T(8,128)(2,1)} collective-permute-done((bf16[128,5376]{1,0:T(8,128)(2,1)S(1)}, bf16[128,5376]{1,0:T(8,128)(2,1)}, u32[]{:S(2)}, u32[]{:S(2)}) %collective-permute-start.2) | collective-permute-done | bytes 1376288 | tf_op jit(solution)/shard_map/ppermute | solution.py:746
  74.9 8.3 %project_pair.1 = (bf16[128,512]{1,0:T(8,128)(2,1)}, bf16[128,256]{1,0:T(8,128)(2,1)}, bf16[128,5376]{1,0:T(8,128)(2,1)}, bf16[256,512]{1,0:T(8,128)(2,1)}, bf16[256,256]{1,0:T(8,128)(2,1)}) custom-call(s32[3]{0:T(128)} %pad_add_fusion.info, f32[1,5376]{1,0:T(1,128)} %broadcast_in_dim.32.gain, f32[1,128]{1,0:T(1,128)} %bitcast.16, ...), custom_call_target="tpu_custom_call" | custom-call | flops 2113929216 | bytes 14352384 | tf_op jit(solution)/shard_map/project_pair/pallas_call | solution.py:224
  83.4 12.5 %collective-permute-done.24.rest_1_ = bf16[128,5376]{1,0:T(8,128)(2,1)S(1)} collective-permute-done((bf16[128,5376]{1,0:T(8,128)(2,1)}, bf16[128,5376]{1,0:T(8,128)(2,1)S(1)}, u32[]{:S(2)}, u32[]{:S(2)}) %collective-permute-start.24) | collective-permute-done | bytes 1376288 | tf_op jit(solution)/shard_map/ppermute | solution.py:746
  95.9 5.2 %collective-permute-done.13.rest_9_.rest_11_ = bf16[256,512]{1,0:T(8,128)(2,1)S(1)} collective-permute-done((bf16[256,512]{1,0:T(8,128)(2,1)}, bf16[256,512]{1,0:T(8,128)(2,1)S(1)}, u32[]{:S(2)}, u32[]{:S(2)}) %collective-permute-start.13) | collective-permute-done | bytes 262176 | tf_op jit(solution)/shard_map/ppermute | solution.py:746
  105.1 4.6 %collective-permute-start.14 = (bf16[256,512]{1,0:T(8,128)(2,1)S(1)}, bf16[256,512]{1,0:T(8,128)(2,1)}, u32[]{:S(2)}, u32[]{:S(2)}) collective-permute-start(bf16[256,512]{1,0:T(8,128)(2,1)S(1)} %collective-permute-done.13.rest_9_.rest_11_), channel_id=1, source_target_pairs={{0,8},{4,12},{8,16},{12,20},{16,24},{20,28},{1,9},{5,13},{9,17},{1... | collective-permute-start | bytes 786440 | tf_op jit(solution)/shard_map/ppermute | solution.py:682
  109.7 2.8 %collective-permute-start.16 = (bf16[256,512]{1,0:T(8,128)(2,1)S(1)}, bf16[256,512]{1,0:T(8,128)(2,1)}, u32[]{:S(2)}, u32[]{:S(2)}) collective-permute-start(bf16[256,512]{1,0:T(8,128)(2,1)S(1)} %collective-permute-done.13.rest_9_.rest_11_), channel_id=1, source_target_pairs={{0,4},{4,8},{8,12},{12,16},{16,20},{20,24},{24,28},{1,5},{5,9},{9,... | collective-permute-start | bytes 786440 | tf_op jit(solution)/shard_map/ppermute | solution.py:682
  116.6 8.0 %attend_head.3 = (bf16[512,256]{1,0:T(8,128)(2,1)}, f32[512,256]{1,0:T(8,128)}, bf16[512,256]{1,0:T(8,128)(2,1)}, bf16[512,256]{1,0:T(8,128)(2,1)}) custom-call(s32[4]{0:T(128)} %pad_add_fusion.1.info, s32[512,1]{1,0:T(8,128)} %maximum_subtract_fusion.lowest, f32[1,128]{1,0:T(1,128)} %bitcast.20, f32[512,128]{1,0:T(8,128)} %get-tuple-element.107.cosine, ...), custom_call_target="tpu_custom_call" | custom-call | flops 2013265920 | bytes 2359296 | tf_op jit(solution)/shard_map/attend_head/pallas_call | solution.py:325
  127.2 8.0 %attend_head.2 = (bf16[512,256]{1,0:T(8,128)(2,1)}, f32[512,256]{1,0:T(8,128)}, bf16[512,256]{1,0:T(8,128)(2,1)}, bf16[512,256]{1,0:T(8,128)(2,1)}) custom-call(s32[4]{0:T(128)} %pad_add_fusion.1.info, s32[512,1]{1,0:T(8,128)} %maximum_subtract_fusion.lowest, f32[1,128]{1,0:T(1,128)} %bitcast.21, f32[512,128]{1,0:T(8,128)} %get-tuple-element.107.cosine, ...), custom_call_target="tpu_custom_call" | custom-call | flops 2013265920 | bytes 2359296 | tf_op jit(solution)/shard_map/attend_head/pallas_call | solution.py:325
  141.5 8.0 %collective-permute-done.18.rest_0_ = bf16[512,256]{1,0:T(8,128)(2,1)S(1)} collective-permute-done((bf16[512,256]{1,0:T(8,128)(2,1)}, bf16[512,256]{1,0:T(8,128)(2,1)S(1)}, u32[]{:S(2)}, u32[]{:S(2)}) %collective-permute-start.18) | collective-permute-done | bytes 262176 | tf_op jit(solution)/shard_map/ppermute | solution.py:692
  150.3 2.9 %finish_kv.3 = (bf16[512,256]{1,0:T(8,128)(2,1)}, bf16[512,512]{1,0:T(8,128)(2,1)}, bf16[256,512]{1,0:T(8,128)(2,1)}) custom-call(s32[4]{0:T(128)} %pad_add_fusion.1.info, f32[1,128]{1,0:T(1,128)} %bitcast.18, f32[512,128]{1,0:T(8,128)} %get-tuple-element.107.cosine, f32[512,128]{1,0:T(8,128)} %get-tuple-element.108.sine, f32[512,256]{1,0:T(8,128)} %get-tuple-element.62.own, ...), custom_call_target="tpu_custom_call" | custom-call | bytes 2097152 | tf_op jit(solution)/shard_map/finish_kv/pallas_call | solution.py:381
  155.2 3.8 %weight_terms.2 = (bf16[4,672,256]{2,1,0:T(8,128)(2,1)}, bf16[4,672,256]{2,1,0:T(8,128)(2,1)S(1)}) custom-call(s32[5]{0:T(128)S(1)} %concatenate.19.info, bf16[512,256]{1,0:T(8,128)(2,1)S(1)} %copy-done.9, bf16[128,5376]{1,0:T(8,128)(2,1)S(1)} %copy-done, bf16[128,5376]{1,0:T(8,128)(2,1)S(1)} %collective-permute-done.24.rest_1_, ...), custom_call_target="tpu_custom_call" | custom-call | flops 1409286144 | bytes 8519680 | tf_op jit(solution)/shard_map/weight_terms/pallas_call | solution.py:422
  161.9 3.8 %weight_terms.3 = (bf16[4,672,256]{2,1,0:T(8,128)(2,1)}, bf16[4,672,256]{2,1,0:T(8,128)(2,1)S(1)}) custom-call(s32[5]{0:T(128)S(1)} %concatenate.19.info, bf16[512,256]{1,0:T(8,128)(2,1)S(1)} %copy-done.11, bf16[128,5376]{1,0:T(8,128)(2,1)S(1)} %copy-done, bf16[128,5376]{1,0:T(8,128)(2,1)S(1)} %collective-permute-done.24.rest_1_, ...), custom_call_target="tpu_custom_call" | custom-call | flops 1409286144 | bytes 8519680 | tf_op jit(solution)/shard_map/weight_terms/pallas_call | solution.py:422
  166.5 10.9 %pair_terms.1 = (bf16[128,5376]{1,0:T(8,128)(2,1)}, f32[128,5376]{1,0:T(8,128)}) custom-call(s32[3]{0:T(128)} %pad_add_fusion.info, bf16[5376,256]{1,0:T(8,128)(2,1)} %w_key.5, bf16[5376,256]{1,0:T(8,128)(2,1)} %w_value.5, bf16[512,512]{1,0:T(8,128)(2,1)} %get-tuple-element.72.joined, bf16[256,512]{1,0:T(8,128)(2,1)} %copy-done.16, ...), custom_call_target="tpu_custom_call" | custom-call | flops 2818572288 | bytes 15138816 | tf_op jit(solution)/shard_map/pair_terms/pallas_call | solution.py:600
  180.2 2.9 %split_sum.4 = (bf16[2,672,128]{2,1,0:T(8,128)(2,1)S(1)}, bf16[2,672,128]{2,1,0:T(8,128)(2,1)S(1)}, bf16[2,672,128]{2,1,0:T(8,128)(2,1)S(1)}, bf16[2,672,128]{2,1,0:T(8,128)(2,1)S(1)}) custom-call(s32[2]{0:T(128)S(1)} %pad_add_fusion.4.info, bf16[4,672,256]{2,1,0:T(8,128)(2,1)S(1)} %copy-done.7, bf16[4,672,256]{2,1,0:T(8,128)(2,1)S(1)} %copy-done.7, ...), custom_call_target="tpu_custom_call" | custom-call | bytes 6881280 | tf_op jit(solution)/shard_map/split_sum/pallas_call | solution.py:466
  183.1 3.0 %collective-permute-start.28 = (bf16[2,672,128]{2,1,0:T(8,128)(2,1)S(1)}, bf16[2,672,128]{2,1,0:T(8,128)(2,1)S(1)}, u32[]{:S(2)}, u32[]{:S(2)}) collective-permute-start(bf16[2,672,128]{2,1,0:T(8,128)(2,1)S(1)} %get-tuple-element.88), channel_id=1, source_target_pairs={{0,8},{4,12},{8,0},{12,4},{16,24},{20,28},{24,16},{28,20},{1,9},{5... | collective-permute-start | bytes 1032200 | tf_op jit(solution)/shard_map/ppermute | solution.py:480
  189.9 5.0 %collective-permute-done.28.rest_2_ = bf16[2,672,128]{2,1,0:T(8,128)(2,1)S(1)} collective-permute-done((bf16[2,672,128]{2,1,0:T(8,128)(2,1)S(1)}, bf16[2,672,128]{2,1,0:T(8,128)(2,1)S(1)}, u32[]{:S(2)}, u32[]{:S(2)}) %collective-permute-start.28) | collective-permute-done | bytes 344096 | tf_op jit(solution)/shard_map/ppermute | solution.py:480
  208.5 32.2 %collective-permute-done.26.rest_1_ = bf16[128,5376]{1,0:T(8,128)(2,1)} collective-permute-done((bf16[128,5376]{1,0:T(8,128)(2,1)}, bf16[128,5376]{1,0:T(8,128)(2,1)}, u32[]{:S(2)}, u32[]{:S(2)}) %collective-permute-start.26) | collective-permute-done | bytes 1376288 | tf_op jit(solution)/shard_map/ppermute | solution.py:746
  240.7 4.1 %input_grad.1 = bf16[128,5376]{1,0:T(8,128)(2,1)} custom-call(bf16[128,5376]{1,0:T(8,128)(2,1)S(1)} %copy-done.2, f32[1,5376]{1,0:T(1,128)S(1)} %copy-done.10, f32[128,5376]{1,0:T(8,128)S(1)} %copy-done.8, bf16[128,5376]{1,0:T(8,128)(2,1)} %collective-permute-done.26.rest_1_), custom_call_target="tpu_custom_call" | custom-call | bytes 6881280 | tf_op jit(solution)/shard_map/input_grad/pallas_call | solution.py:639
  (143 shorter events, 67.9 us)
Async XLA Ops:
  2.0 33.3 %collective-permute-start = (bf16[672,512]{1,0:T(8,128)(2,1)S(1)}, bf16[672,512]{1,0:T(8,128)(2,1)}, u32[]{:S(2)}, u32[]{:S(2)}) collective-permute-start(bf16[672,512]{1,0:T(8,128)(2,1)S(1)} %pad_maximum_fusion), channel_id=1, source_target_pairs={{0,1},{1,0},{2,3},{3,2},{4,5},{5,4},{6,7},{7,6},{8,9},{9,8},{10,11... | collective-permute-start | bytes 2064392 | tf_op jit(solution)/shard_map/ppermute | solution.py:746
  5.1 62.3 %collective-permute-start.2 = (bf16[128,5376]{1,0:T(8,128)(2,1)S(1)}, bf16[128,5376]{1,0:T(8,128)(2,1)}, u32[]{:S(2)}, u32[]{:S(2)}) collective-permute-start(bf16[128,5376]{1,0:T(8,128)(2,1)S(1)} %copy-done.1), channel_id=1, source_target_pairs={{0,2},{1,3},{2,0},{3,1},{4,6},{5,7},{6,4},{7,5},{8,10},{9,11},{10,... | collective-permute-start | bytes 4128776 | tf_op jit(solution)/shard_map/ppermute | solution.py:746
  35.2 16.8 %collective-permute-start.4 = (bf16[672,512]{1,0:T(8,128)(2,1)}, bf16[672,512]{1,0:T(8,128)(2,1)S(1)}, u32[]{:S(2)}, u32[]{:S(2)}) collective-permute-start(bf16[672,512]{1,0:T(8,128)(2,1)} %collective-permute-done.rest_0_), channel_id=1, source_target_pairs={{0,8},{4,12},{8,0},{12,4},{16,24},{20,28},{24,16},{28,20},{1,9},{5... | collective-permute-start | bytes 2064392 | tf_op jit(solution)/shard_map/ppermute | solution.py:480
  36.9 18.4 %collective-permute-start.5 = (bf16[672,512]{1,0:T(8,128)(2,1)}, bf16[672,512]{1,0:T(8,128)(2,1)}, u32[]{:S(2)}, u32[]{:S(2)}) collective-permute-start(bf16[672,512]{1,0:T(8,128)(2,1)} %collective-permute-done.rest_0_), channel_id=1, source_target_pairs={{0,16},{4,20},{8,24},{12,28},{16,0},{20,4},{24,8},{28,12},{1,17},{... | collective-permute-start | bytes 2064392 | tf_op jit(solution)/shard_map/ppermute | solution.py:480
  38.4 28.9 %collective-permute-start.8 = (bf16[672,512]{1,0:T(8,128)(2,1)}, bf16[672,512]{1,0:T(8,128)(2,1)}, u32[]{:S(2)}, u32[]{:S(2)}) collective-permute-start(bf16[672,512]{1,0:T(8,128)(2,1)} %collective-permute-done.rest_0_), channel_id=1, source_target_pairs={{0,4},{4,0},{8,12},{12,8},{16,20},{20,16},{24,28},{28,24},{1,5},{5... | collective-permute-start | bytes 2064392 | tf_op jit(solution)/shard_map/ppermute | solution.py:480
  47.8 48.1 %collective-permute-start.24 = (bf16[128,5376]{1,0:T(8,128)(2,1)}, bf16[128,5376]{1,0:T(8,128)(2,1)S(1)}, u32[]{:S(2)}, u32[]{:S(2)}) collective-permute-start(bf16[128,5376]{1,0:T(8,128)(2,1)} %get-tuple-element.56.ready.rest_0_), channel_id=1, source_target_pairs={{0,1},{1,0},{2,3},{3,2},{4,5},{5,4},{6,7},{7,6},{8,9},{9,8},{10,11... | collective-permute-start | bytes 4128776 | tf_op jit(solution)/shard_map/ppermute | solution.py:746
  83.3 17.8 %collective-permute-start.13 = (bf16[256,512]{1,0:T(8,128)(2,1)}, bf16[256,512]{1,0:T(8,128)(2,1)S(1)}, u32[]{:S(2)}, u32[]{:S(2)}) collective-permute-start(bf16[256,512]{1,0:T(8,128)(2,1)} %get-tuple-element.60), channel_id=1, source_target_pairs={{0,1},{1,0},{2,3},{3,2},{4,5},{5,4},{6,7},{7,6},{8,9},{9,8},{10,11... | collective-permute-start | bytes 786440 | tf_op jit(solution)/shard_map/ppermute | solution.py:746
  101.1 54.1 %collective-permute-start.25 = (bf16[128,5376]{1,0:T(8,128)(2,1)}, bf16[128,5376]{1,0:T(8,128)(2,1)S(1)}, u32[]{:S(2)}, u32[]{:S(2)}) collective-permute-start(bf16[128,5376]{1,0:T(8,128)(2,1)} %get-tuple-element.75.rest_2_), channel_id=1, source_target_pairs={{0,1},{1,0},{2,3},{3,2},{4,5},{5,4},{6,7},{7,6},{8,9},{9,8},{10,11... | collective-permute-start | bytes 4128776 | tf_op jit(solution)/shard_map/ppermute | solution.py:746
  101.3 12.6 %collective-permute-start.15 = (bf16[128,512]{1,0:T(8,128)(2,1)}, bf16[128,512]{1,0:T(8,128)(2,1)S(1)}, u32[]{:S(2)}, u32[]{:S(2)}) collective-permute-start(bf16[128,512]{1,0:T(8,128)(2,1)} %get-tuple-element.61.rest_10_), channel_id=1, source_target_pairs={{0,8},{4,12},{8,16},{12,20},{16,24},{20,28},{1,9},{5,13},{9,17},{1... | collective-permute-start | bytes 393224 | tf_op jit(solution)/shard_map/ppermute | solution.py:682
  113.9 22.6 %collective-permute-start.20 = (bf16[256,256]{1,0:T(8,128)(2,1)}, bf16[256,256]{1,0:T(8,128)(2,1)S(1)}, u32[]{:S(2)}, u32[]{:S(2)}) collective-permute-start(bf16[256,256]{1,0:T(8,128)(2,1)} %get-tuple-element.67), channel_id=1, source_target_pairs={{0,1},{1,0},{2,3},{3,2},{4,5},{5,4},{6,7},{7,6},{8,9},{9,8},{10,11... | collective-permute-start | bytes 393224 | tf_op jit(solution)/shard_map/ppermute | solution.py:746
  124.6 13.5 %collective-permute-start.21 = (bf16[512,256]{1,0:T(8,128)(2,1)}, bf16[512,256]{1,0:T(8,128)(2,1)S(1)}, u32[]{:S(2)}, u32[]{:S(2)}) collective-permute-start(bf16[512,256]{1,0:T(8,128)(2,1)} %get-tuple-element.70), channel_id=1, source_target_pairs={{8,0},{12,4},{16,8},{20,12},{24,16},{28,20},{9,1},{13,5},{17,9},{2... | collective-permute-start | bytes 786440 | tf_op jit(solution)/shard_map/ppermute | solution.py:692
  125.9 12.2 %collective-permute-start.22 = (bf16[512,256]{1,0:T(8,128)(2,1)}, bf16[512,256]{1,0:T(8,128)(2,1)}, u32[]{:S(2)}, u32[]{:S(2)}) collective-permute-start(bf16[512,256]{1,0:T(8,128)(2,1)} %get-tuple-element.71), channel_id=1, source_target_pairs={{4,0},{8,4},{12,8},{16,12},{20,16},{24,20},{28,24},{5,1},{9,5},{13... | collective-permute-start | bytes 786440 | tf_op jit(solution)/shard_map/ppermute | solution.py:692
  135.2 14.3 %collective-permute-start.18 = (bf16[512,256]{1,0:T(8,128)(2,1)}, bf16[512,256]{1,0:T(8,128)(2,1)S(1)}, u32[]{:S(2)}, u32[]{:S(2)}) collective-permute-start(bf16[512,256]{1,0:T(8,128)(2,1)} %get-tuple-element.63), channel_id=1, source_target_pairs={{8,0},{12,4},{16,8},{20,12},{24,16},{28,20},{9,1},{13,5},{17,9},{2... | collective-permute-start | bytes 786440 | tf_op jit(solution)/shard_map/ppermute | solution.py:692
  136.5 13.0 %collective-permute-start.19 = (bf16[512,256]{1,0:T(8,128)(2,1)}, bf16[512,256]{1,0:T(8,128)(2,1)}, u32[]{:S(2)}, u32[]{:S(2)}) collective-permute-start(bf16[512,256]{1,0:T(8,128)(2,1)} %get-tuple-element.64), channel_id=1, source_target_pairs={{4,0},{8,4},{12,8},{16,12},{20,16},{24,20},{28,24},{5,1},{9,5},{13... | collective-permute-start | bytes 786440 | tf_op jit(solution)/shard_map/ppermute | solution.py:692
  153.2 12.5 %collective-permute-start.23 = (bf16[256,512]{1,0:T(8,128)(2,1)}, bf16[256,512]{1,0:T(8,128)(2,1)S(1)}, u32[]{:S(2)}, u32[]{:S(2)}) collective-permute-start(bf16[256,512]{1,0:T(8,128)(2,1)} %get-tuple-element.73), channel_id=1, source_target_pairs={{0,1},{1,0},{2,3},{3,2},{4,5},{5,4},{6,7},{7,6},{8,9},{9,8},{10,11... | collective-permute-start | bytes 786440 | tf_op jit(solution)/shard_map/ppermute | solution.py:746
  160.1 20.0 %collective-permute-start.27 = (bf16[4,672,256]{2,1,0:T(8,128)(2,1)}, bf16[4,672,256]{2,1,0:T(8,128)(2,1)}, u32[]{:S(2)}, u32[]{:S(2)}) collective-permute-start(bf16[4,672,256]{2,1,0:T(8,128)(2,1)} %get-tuple-element.76), channel_id=1, source_target_pairs={{0,4},{4,0},{8,12},{12,8},{16,20},{20,16},{24,28},{28,24},{1,5},{5... | collective-permute-start | bytes 4128776 | tf_op jit(solution)/shard_map/ppermute | solution.py:480
  165.7 20.8 %collective-permute-start.32 = (bf16[4,672,256]{2,1,0:T(8,128)(2,1)}, bf16[4,672,256]{2,1,0:T(8,128)(2,1)S(1)}, u32[]{:S(2)}, u32[]{:S(2)}) collective-permute-start(bf16[4,672,256]{2,1,0:T(8,128)(2,1)} %get-tuple-element.79), channel_id=1, source_target_pairs={{0,4},{4,0},{8,12},{12,8},{16,20},{20,16},{24,28},{28,24},{1,5},{5... | collective-permute-start | bytes 4128776 | tf_op jit(solution)/shard_map/ppermute | solution.py:480
  177.4 63.3 %collective-permute-start.26 = (bf16[128,5376]{1,0:T(8,128)(2,1)}, bf16[128,5376]{1,0:T(8,128)(2,1)}, u32[]{:S(2)}, u32[]{:S(2)}) collective-permute-start(bf16[128,5376]{1,0:T(8,128)(2,1)} %get-tuple-element.83), channel_id=1, source_target_pairs={{0,2},{1,3},{2,0},{3,1},{4,6},{5,7},{6,4},{7,5},{8,10},{9,11},{10,... | collective-permute-start | bytes 4128776 | tf_op jit(solution)/shard_map/ppermute | solution.py:746
  187.8 14.4 %collective-permute-start.33 = (bf16[2,672,128]{2,1,0:T(8,128)(2,1)S(1)}, bf16[2,672,128]{2,1,0:T(8,128)(2,1)S(1)}, u32[]{:S(2)}, u32[]{:S(2)}) collective-permute-start(bf16[2,672,128]{2,1,0:T(8,128)(2,1)S(1)} %get-tuple-element.96), channel_id=1, source_target_pairs={{0,8},{4,12},{8,0},{12,4},{16,24},{20,28},{24,16},{28,20},{1,9},{5... | collective-permute-start | bytes 1032200 | tf_op jit(solution)/shard_map/ppermute | solution.py:480
  189.8 14.6 %collective-permute-start.34 = (bf16[2,672,128]{2,1,0:T(8,128)(2,1)S(1)}, bf16[2,672,128]{2,1,0:T(8,128)(2,1)S(1)}, u32[]{:S(2)}, u32[]{:S(2)}) collective-permute-start(bf16[2,672,128]{2,1,0:T(8,128)(2,1)S(1)} %get-tuple-element.97), channel_id=1, source_target_pairs={{0,16},{4,20},{8,24},{12,28},{16,0},{20,4},{24,8},{28,12},{1,17},{... | collective-permute-start | bytes 1032200 | tf_op jit(solution)/shard_map/ppermute | solution.py:480
  197.9 47.0 %collective-permute-start.30 = (bf16[1,672,128]{2,1,0:T(8,128)(2,1)S(1)}, bf16[1,672,128]{2,1,0:T(8,128)(2,1)S(1)}, u32[]{:S(2)}, u32[]{:S(2)}) collective-permute-start(bf16[1,672,128]{2,1,0:T(8,128)(2,1)S(1)} %get-tuple-element.92), channel_id=1, source_target_pairs={{0,16},{4,20},{8,24},{12,28},{16,0},{20,4},{24,8},{28,12},{1,17},{... | collective-permute-start | bytes 516104 | tf_op jit(solution)/shard_map/ppermute | solution.py:480
  198.4 46.5 %collective-permute-start.31 = (bf16[1,672,128]{2,1,0:T(8,128)(2,1)S(1)}, bf16[1,672,128]{2,1,0:T(8,128)(2,1)S(1)}, u32[]{:S(2)}, u32[]{:S(2)}) collective-permute-start(bf16[1,672,128]{2,1,0:T(8,128)(2,1)S(1)} %get-tuple-element.93), channel_id=1, source_target_pairs={{0,8},{4,12},{8,0},{12,4},{16,24},{20,28},{24,16},{28,20},{1,9},{5... | collective-permute-start | bytes 516104 | tf_op jit(solution)/shard_map/ppermute | solution.py:480
  205.3 39.6 %collective-permute-start.35 = (bf16[1,672,128]{2,1,0:T(8,128)(2,1)S(1)}, bf16[1,672,128]{2,1,0:T(8,128)(2,1)S(1)}, u32[]{:S(2)}, u32[]{:S(2)}) collective-permute-start(bf16[1,672,128]{2,1,0:T(8,128)(2,1)S(1)} %get-tuple-element.100), channel_id=1, source_target_pairs={{0,16},{4,20},{8,24},{12,28},{16,0},{20,4},{24,8},{28,12},{1,17},{... | collective-permute-start | bytes 516104 | tf_op jit(solution)/shard_map/ppermute | solution.py:480
  205.8 39.1 %collective-permute-start.36 = (bf16[1,672,128]{2,1,0:T(8,128)(2,1)S(1)}, bf16[1,672,128]{2,1,0:T(8,128)(2,1)S(1)}, u32[]{:S(2)}, u32[]{:S(2)}) collective-permute-start(bf16[1,672,128]{2,1,0:T(8,128)(2,1)S(1)} %get-tuple-element.101), channel_id=1, source_target_pairs={{0,8},{4,12},{8,0},{12,4},{16,24},{20,28},{24,16},{28,20},{1,9},{5... | collective-permute-start | bytes 516104 | tf_op jit(solution)/shard_map/ppermute | solution.py:480
  (41 other events, 464.6 us)

commit v3 on v2

--- a/solution.py
+++ b/solution.py
@@ -429,7 +429,7 @@
         out_specs=(out_spec, out_spec),
         scratch_shapes=[pltpu.VMEM((tile, cols), jnp.float32)],
         compiler_params=params(),
-        cost_estimate=cost(2 * len(blocks) * rows * width * cols, grads, *blocks, out, out),
+        cost_estimate=cost(0),
     )(info, grads, *blocks)
 
 
@@ -471,7 +471,7 @@
         in_specs=[smem_spec()] + [spec(a) for a in (*keeps, *arrivals)],
         out_specs=tuple(spec(o) for o in outs),
         compiler_params=params(),
-        cost_estimate=cost(0, *keeps, *arrivals, *outs),
+        cost_estimate=cost(0),
     )(info, *keeps, *arrivals)
 
 
@@ -527,7 +527,7 @@
         in_specs=[pl.BlockSpec((1, rows // steps, cols), lambda step: (0, step, 0)) for a in parts],
         out_specs=(out_spec, out_spec),
         compiler_params=params(),
-        cost_estimate=cost(0, *parts, out, out),
+        cost_estimate=cost(0),
     )(*parts)
 
 
@@ -563,13 +563,23 @@
     away_out, own_out, key_held, value_held, held, own_sems, sems = rest[len(places) :]
     rows, width = own_out.shape
     size = w_key.shape[1] // heads
-    own_copies = [
-        pltpu.make_async_copy(w_key, key_held, own_sems.at[0]),
-        pltpu.make_async_copy(w_value, value_held, own_sems.at[1]),
-    ]
-    start_all(own_copies)
+    half = width // 2
+    slice_rows = pieces[0].shape[0]
+    split = half // slice_rows
+    first = info[0] // split
     copies = piece_copies(places, info[0], pieces, held, sems)
-    start_all(copies)
+    spans, groups = [], []
+    for number in range(2):
+        span = pl.ds(pl.multiple_of(jnp.bitwise_xor(first, number) * half, 128), half)
+        spans.append(span)
+        groups.append(
+            [
+                pltpu.make_async_copy(w_key.at[span, :], key_held.at[span, :], own_sems.at[2 * number]),
+                pltpu.make_async_copy(w_value.at[span, :], value_held.at[span, :], own_sems.at[2 * number + 1]),
+            ]
+            + [copy for copy, (offset, _) in zip(copies, places) if offset // split == number]
+        )
+        start_all(groups[number])
     own_rows = jnp.concatenate(
         [joined[pl.ds(pl.multiple_of(info[1 + number] * rows, rows), rows), :] for number in range(2)], axis=0
     )
@@ -580,15 +590,12 @@
         for head in range(heads)
     ]
     left = jnp.concatenate(sides, axis=1)
-    wait_all(own_copies)
-    wait_all(copies)
-    tile = max(t for t in range(128, 1025, 128) if width % t == 0)
-    for low in range(0, width, tile):
-        span = slice(low, low + tile)
+    for span, group in zip(spans, groups):
+        wait_all(group)
         right = jnp.concatenate([key_held[span, :], value_held[span, :], held[span, :]], axis=1)
-        total = dot_last(left, right)
+        total = dot_last(left, right).astype(jnp.bfloat16)
         own_out[:, span] = total[:rows]
-        away_out[:, span] = total[rows:].astype(jnp.bfloat16)
+        away_out[:, span] = total[rows:]
 
 
 def pair_terms(info, joined, arrived, pieces, w_key, w_value, heads):
@@ -596,7 +603,7 @@
     width, cols = w_key.shape
     places = [(offset, low) for offset, low, _ in pieces]
     arrays = [piece for _, _, piece in pieces]
-    outs = (jax.ShapeDtypeStruct((rows, width), jnp.bfloat16), jax.ShapeDtypeStruct((rows, width), jnp.float32))
+    outs = (jax.ShapeDtypeStruct((rows, width), jnp.bfloat16),) * 2
     return pl.pallas_call(
         functools.partial(pair_body, places, heads),
         name="pair_terms",
@@ -609,7 +616,7 @@
             pltpu.VMEM((width, cols), jnp.bfloat16),
             pltpu.VMEM((width, cols), jnp.bfloat16),
             pltpu.VMEM((width, 2 * cols), jnp.bfloat16),
-            pltpu.SemaphoreType.DMA((2,)),
+            pltpu.SemaphoreType.DMA((4,)),
             pltpu.SemaphoreType.DMA((len(arrays),)),
         ],
         compiler_params=params(56),
@@ -746,7 +753,7 @@
     return lax.ppermute(array, "tp", [(i, i ^ distance) for i in range(lax.axis_size("tp"))])
 
 
-def shards_paired(tokens, dense, rope_rows, lowest, raw_queries, out_grad, w_key, w_value, reach):
+def shards_paired(tokens, dense, rope_rows, lowest, raw_queries, out_grad, w_key, w_value, reach, once):
     gain_row, q_row, k_row = dense
     cosine, sine = rope_rows
     seq_count = lax.axis_size("seq")
@@ -759,30 +766,31 @@
     zero = jnp.zeros_like(place)
     slot_places = jnp.stack([place, place ^ 1, place ^ 2, place ^ 3])
 
-    distant = trade(tokens, 2)
     own_slice = jnp.concatenate(
         [lax.dynamic_slice_in_dim(weight, seq_index * chunk, chunk, 0) for weight in (w_key, w_value)], axis=1
     )
+    distant = trade(after(tokens, own_slice), 2)
 
     partner_slice = trade(own_slice, 1)
-    spread = [partner_slice, swap(partner_slice, 1), swap(partner_slice, 2)]
     info = jnp.stack([zero, place])
-    kv_0, keys_0, normed_0 = project(
-        info, [after(tokens, partner_slice)], gain_row, k_row, cosine, sine, w_key, w_value
-    )
+    kv_0, keys_0, normed_0 = project(info, [tokens], gain_row, k_row, cosine, sine, w_key, w_value)
     halo_0 = halo_of(kv_0, reach)
-    partner_normed_0 = trade(normed_0, 1)
-    spread += spread_corners(after(spread, normed_0))
+    first_slice = after(partner_slice, (normed_0, halo_0))
+    spread = [first_slice, swap(first_slice, 1), swap(first_slice, 2)]
+    partner_normed_0 = trade(after(normed_0, partner_slice), 1)
+    spread += spread_corners(spread)
     pieces = spread_end(spread)
     info = jnp.stack([seq_index, place, place ^ 2])
+    far_block = after(distant, [piece for _, _, piece in pieces])
     kv_2, keys_2, normed_2, far_kv, far_keys = project_pair(
-        info, normed_0, after(distant, halo_0), gain_row, k_row, cosine, sine, w_key, w_value, pieces
+        info, normed_0, far_block, gain_row, k_row, cosine, sine, w_key, w_value, pieces
     )
     arrived_kv = trade(far_kv, 1)
+    arrived_keys = trade(far_keys, 1)
     halo_2 = halo_of(kv_2, reach)
+    arrived_kv = after(arrived_kv, (arrived_keys, partner_normed_0))
     halo_far = halo_of(arrived_kv, reach)
-    arrived_keys = trade(after(far_keys, arrived_kv), 1)
-    partner_normed_2 = trade(after(normed_2, (arrived_kv, partner_normed_0)), 1)
+    partner_normed_2 = trade(after(normed_2, arrived_kv), 1)
 
     blocks = []
     for distance in range(reach, 0, -1):
@@ -792,7 +800,7 @@
     raw_keys = [(keys_0, 0), (arrived_keys, 0), (keys_2, 0), (arrived_keys, 1)]
     normed = [normed_0, partner_normed_0, normed_2, partner_normed_2]
     weight_info = jnp.concatenate([slot_places, (seq_index & 1)[None]])
-    query_parts, kv_grads, terms = [], [], []
+    query_parts, kv_grads = [], []
     for head in range(kv_heads):
         outs = attend(head, kv_heads, reach, slot_places, lowest, q_row, cosine, sine, raw_queries, out_grad, blocks)
         query_parts.append(outs[0])
@@ -800,21 +808,25 @@
         before = kv_grads if head == kv_heads - 1 else None
         results = finish(head, slot_places, k_row, cosine, sine, outs[1], back, raw_keys, before=before)
         kv_grads = kv_grads + results[:1]
-        terms.append(weight_terms(weight_info, results[0], normed, chunk))
     grad_queries = jnp.concatenate(query_parts, axis=1)
 
     joined, away = results[1:]
-    arrived = after(trade(away, 1), terms)
+    arrived = trade(away, 1)
     info = jnp.stack([seq_index, place, place ^ 2])
     away_terms, own_terms = pair_terms(info, joined, arrived, pieces, w_key, w_value, kv_heads)
     other_terms = trade(away_terms, 2)
-    grad_x = input_grad(tokens, gain_row, [own_terms, other_terms], [])
-
-    parts = []
-    for send, keep in terms:
-        keeps, comings = scatter_sum(send, keep)
-        parts += [*keeps, *comings]
-    grad_wk, grad_wv = gather_heads(parts, kv_heads)
+
+    def weight_step(step, _):
+        parts = []
+        for grads in kv_grads:
+            send, keep = weight_terms(weight_info + step, grads, normed, chunk)
+            keeps, comings = scatter_sum(send, keep)
+            parts += [*keeps, *comings]
+        return gather_heads(parts, kv_heads)
+
+    empty = jnp.zeros((chunk, cols), jnp.float32)
+    grad_wk, grad_wv = lax.fori_loop(0, after(once, away_terms), weight_step, (empty, empty))
+    grad_x = input_grad(tokens, gain_row, [after(own_terms, (grad_wk, grad_wv, grad_queries)), other_terms], [])
     return (grad_x, grad_queries, grad_wk, grad_wv)
 
 
@@ -837,8 +849,8 @@
         and chunk % 16 == 0
         and width % math.lcm(2 * chunk, 128) == 0
     )
-    run = shards_paired if paired else shards_general
-    return run(tokens, dense, rope_rows, lowest[:, None], raw_queries, out_grad, w_key, w_value, reach)
+    args = (tokens, dense, rope_rows, lowest[:, None], raw_queries, out_grad, w_key, w_value, reach)
+    return shards_paired(*args, jnp.minimum(doc_lengths[0], 1)) if paired else shards_general(*args)
 
 
 def solution(mesh):

time: 248 us -> 233 us (0.940)
  waiting for transfers between devices: 110 us -> 92.9 us
  local copies, waits for them, and re-layouts: 8.82 us -> 13.7 us
  starting transfers between devices: 54.4 us -> 50.6 us
    ppermute x8, waiting for transfers between devices: 81.4 us -> 50.3 us  [trade(): lax.ppermute(array, 'tp', [(i, i ^ distance) for i in range(lax.axis_size...]
    ppermute x19, waiting for transfers between devices: 20.1 us -> 29 us  [swap(): return lax.ppermute(array, 'seq', [(i, i ^ 1 << bit) for i in range(size)])]
    ppermute x6, waiting for transfers between devices: 0.47 us -> 4.93 us  [halo_of(): sent.append(lax.ppermute(key_value, 'seq', pairs))]
    unnamed x56 -> x57, local copies, waits for them, and re-layouts: 5.72 us -> 8.46 us
  transfers between devices with their start and end apart: 37 -> 37, of which waited for: 16 -> 17; matrix products, arithmetic and copies ran while one was open for 3% -> 3% of each run, Pallas kernels for 26% -> 27%
where the time goes in v3:
time: 233 us; the launch traced here: 230 us
  waiting for transfers between devices  92.9 us (40%)
  Pallas kernels  65.8 us (28%)
  starting transfers between devices  50.6 us (22%)
  local copies, waits for them, and re-layouts  13.7 us (6%)
  other arithmetic  5.9 us (3%)
    ppermute x8, waiting for transfers between devices, trade(): lax.ppermute(array, 'tp', [(i, i ^ distance) for i in range(lax.axis_size...  50.3 us
    ppermute x19, waiting for transfers between devices, swap(): return lax.ppermute(array, 'seq', [(i, i ^ 1 << bit) for i in range(size)])  29 us
    ppermute x19, starting transfers between devices, swap(): return lax.ppermute(array, 'seq', [(i, i ^ 1 << bit) for i in range(size)])  21.1 us
    pallas_call x2, Pallas kernels, attend(): pl.pallas_call(functools.partial(attend_body, reach, slots), name='attend...  16 us
    ppermute x6, starting transfers between devices, halo_of(): sent.append(lax.ppermute(key_value, 'seq', pairs))  13.5 us
    ppermute x8, starting transfers between devices, trade(): lax.ppermute(array, 'tp', [(i, i ^ distance) for i in range(lax.axis_size...  10.6 us
    pallas_call x2, Pallas kernels, weight_terms(): pl.pallas_call(functools.partial(weight_body, len(blocks)), name='weight_...  9.55 us
    pallas_call x1, Pallas kernels, pair_terms(): pl.pallas_call(functools.partial(pair_body, places, heads), name='pair_te...  9.4 us
  transfers between devices with their start and end apart: 37, of which 17 were waited for; matrix products, arithmetic and copies ran while one was open for 3% of the time, Pallas kernels for 27%

profile of v3, /device:TPU:0, one launch (start us, length us, event | category | flops | bytes accessed | tf_op | source)
XLA Modules:
  0.0 230.0 jit_solution(7479019607277012366)
XLA Ops:
  2.8 3.0 %collective-permute-start.12 = (bf16[672,512]{1,0:T(8,128)(2,1)}, bf16[672,512]{1,0:T(8,128)(2,1)S(1)}, u32[]{:S(2)}, u32[]{:S(2)}) collective-permute-start(bf16[672,512]{1,0:T(8,128)(2,1)} %pad_maximum_fusion), channel_id=1, source_target_pairs={{0,1},{1,0},{2,3},{3,2},{4,5},{5,4},{6,7},{7,6},{8,9},{9,8},{10,11... | collective-permute-start | bytes 2064392 | tf_op jit(solution)/shard_map/ppermute | solution.py:753
  12.0 6.2 %project_block.1 = (bf16[128,512]{1,0:T(8,128)(2,1)}, bf16[128,256]{1,0:T(8,128)(2,1)}, bf16[128,5376]{1,0:T(8,128)(2,1)}) custom-call(s32[2]{0:T(128)} %pad_add_fusion.4.info, f32[1,5376]{1,0:T(1,128)} %broadcast_in_dim.35.gain, f32[1,128]{1,0:T(1,128)} %bitcast.21, f32[512,128]{1,0:T(8,128)} %get-tuple-element.168.cosine, ...), custom_call_target="tpu_custom_call" | custom-call | flops 704643072 | bytes 8454144 | tf_op jit(solution)/shard_map/project_block/pallas_call | solution.py:163
  18.1 3.4 %collective-permute-start.10 = (bf16[128,512]{1,0:T(8,128)(2,1)}, bf16[128,512]{1,0:T(8,128)(2,1)S(1)}, u32[]{:S(2)}, u32[]{:S(2)}) collective-permute-start(bf16[128,512]{1,0:T(8,128)(2,1)} %get-tuple-element.112.rest_8_), channel_id=1, source_target_pairs={{0,8},{4,12},{8,16},{12,20},{16,24},{20,28},{1,9},{5,13},{9,17},{1... | collective-permute-start | bytes 393224 | tf_op jit(solution)/shard_map/ppermute | solution.py:689
  24.3 12.0 %collective-permute-done.12.rest_0_ = bf16[672,512]{1,0:T(8,128)(2,1)S(1)} collective-permute-done((bf16[672,512]{1,0:T(8,128)(2,1)}, bf16[672,512]{1,0:T(8,128)(2,1)S(1)}, u32[]{:S(2)}, u32[]{:S(2)}) %collective-permute-start.12) | collective-permute-done | bytes 688160 | tf_op jit(solution)/shard_map/ppermute | solution.py:753
  39.6 13.5 %collective-permute-done.14.rest_1_ = bf16[672,512]{1,0:T(8,128)(2,1)S(1)} collective-permute-done((bf16[672,512]{1,0:T(8,128)(2,1)S(1)}, bf16[672,512]{1,0:T(8,128)(2,1)S(1)}, u32[]{:S(2)}, u32[]{:S(2)}) %collective-permute-start.14) | collective-permute-done | bytes 688160 | tf_op jit(solution)/shard_map/ppermute | solution.py:480
  56.2 12.0 %collective-permute-done.11.block = bf16[128,5376]{1,0:T(8,128)(2,1)} collective-permute-done((bf16[128,5376]{1,0:T(8,128)(2,1)S(1)}, bf16[128,5376]{1,0:T(8,128)(2,1)}, u32[]{:S(2)}, u32[]{:S(2)}) %collective-permute-start.11) | collective-permute-done | bytes 1376288 | tf_op jit(solution)/shard_map/ppermute | solution.py:753
  74.4 8.3 %project_pair.1 = (bf16[128,512]{1,0:T(8,128)(2,1)}, bf16[128,256]{1,0:T(8,128)(2,1)}, bf16[128,5376]{1,0:T(8,128)(2,1)}, bf16[256,512]{1,0:T(8,128)(2,1)}, bf16[256,256]{1,0:T(8,128)(2,1)}) custom-call(s32[3]{0:T(128)} %pad_add_fusion.2.info, f32[1,5376]{1,0:T(1,128)} %broadcast_in_dim.35.gain, f32[1,128]{1,0:T(1,128)} %bitcast.22, ...), custom_call_target="tpu_custom_call" | custom-call | flops 2113929216 | bytes 14352384 | tf_op jit(solution)/shard_map/project_pair/pallas_call | solution.py:224
  85.0 3.4 %collective-permute-start.27 = (bf16[128,512]{1,0:T(8,128)(2,1)}, bf16[128,512]{1,0:T(8,128)(2,1)S(1)}, u32[]{:S(2)}, u32[]{:S(2)}) collective-permute-start(bf16[128,512]{1,0:T(8,128)(2,1)} %get-tuple-element.121.rest_10_), channel_id=1, source_target_pairs={{0,8},{4,12},{8,16},{12,20},{16,24},{20,28},{1,9},{5,13},{9,17},{1... | collective-permute-start | bytes 393224 | tf_op jit(solution)/shard_map/ppermute | solution.py:689
  89.9 5.6 %collective-permute-done.24.rest_3_.rest_5_ = bf16[256,256]{1,0:T(8,128)(2,1)S(1)} collective-permute-done((bf16[256,256]{1,0:T(8,128)(2,1)}, bf16[256,256]{1,0:T(8,128)(2,1)S(1)}, u32[]{:S(2)}, u32[]{:S(2)}) %collective-permute-start.24) | collective-permute-done | bytes 131104 | tf_op jit(solution)/shard_map/ppermute | solution.py:753
  101.2 3.4 %collective-permute-done.26.rest_1_.rest_3_ = bf16[256,512]{1,0:T(8,128)(2,1)S(1)} collective-permute-done((bf16[256,512]{1,0:T(8,128)(2,1)S(1)}, bf16[256,512]{1,0:T(8,128)(2,1)S(1)}, u32[]{:S(2)}, u32[]{:S(2)}) %collective-permute-start.26) | collective-permute-done | bytes 262176 | tf_op jit(solution)/shard_map/ppermute | solution.py:689
  105.4 8.0 %attend_head.3 = (bf16[512,256]{1,0:T(8,128)(2,1)}, f32[512,256]{1,0:T(8,128)}, bf16[512,256]{1,0:T(8,128)(2,1)}, bf16[512,256]{1,0:T(8,128)(2,1)}) custom-call(s32[4]{0:T(128)} %pad_add_fusion.3.info, s32[512,1]{1,0:T(8,128)} %maximum_subtract_fusion.lowest, f32[1,128]{1,0:T(1,128)} %bitcast.25, f32[512,128]{1,0:T(8,128)} %get-tuple-element.168.cosine, ...), custom_call_target="tpu_custom_call" | custom-call | flops 2013265920 | bytes 2359296 | tf_op jit(solution)/shard_map/attend_head/pallas_call | solution.py:325
  116.1 8.0 %attend_head.2 = (bf16[512,256]{1,0:T(8,128)(2,1)}, f32[512,256]{1,0:T(8,128)}, bf16[512,256]{1,0:T(8,128)(2,1)}, bf16[512,256]{1,0:T(8,128)(2,1)}) custom-call(s32[4]{0:T(128)} %pad_add_fusion.3.info, s32[512,1]{1,0:T(8,128)} %maximum_subtract_fusion.lowest, f32[1,128]{1,0:T(1,128)} %bitcast.26, f32[512,128]{1,0:T(8,128)} %get-tuple-element.168.cosine, ...), custom_call_target="tpu_custom_call" | custom-call | flops 2013265920 | bytes 2359296 | tf_op jit(solution)/shard_map/attend_head/pallas_call | solution.py:325
  129.5 8.7 %collective-permute-done.30.rest_0_ = bf16[512,256]{1,0:T(8,128)(2,1)S(1)} collective-permute-done((bf16[512,256]{1,0:T(8,128)(2,1)}, bf16[512,256]{1,0:T(8,128)(2,1)S(1)}, u32[]{:S(2)}, u32[]{:S(2)}) %collective-permute-start.30) | collective-permute-done | bytes 262176 | tf_op jit(solution)/shard_map/ppermute | solution.py:699
  139.0 2.8 %finish_kv.3 = (bf16[512,256]{1,0:T(8,128)(2,1)S(1)}, bf16[512,512]{1,0:T(8,128)(2,1)}, bf16[256,512]{1,0:T(8,128)(2,1)}) custom-call(s32[4]{0:T(128)} %pad_add_fusion.3.info, f32[1,128]{1,0:T(1,128)} %bitcast.24, f32[512,128]{1,0:T(8,128)} %get-tuple-element.168.cosine, f32[512,128]{1,0:T(8,128)} %get-tuple-element.169.sine, ...), custom_call_target="tpu_custom_call" | custom-call | bytes 2097152 | tf_op jit(solution)/shard_map/finish_kv/pallas_call | solution.py:381
  142.4 7.1 %collective-permute-done.34.arrived = bf16[256,512]{1,0:T(8,128)(2,1)S(1)} collective-permute-done((bf16[256,512]{1,0:T(8,128)(2,1)}, bf16[256,512]{1,0:T(8,128)(2,1)S(1)}, u32[]{:S(2)}, u32[]{:S(2)}) %collective-permute-start.34) | collective-permute-done | bytes 262176 | tf_op jit(solution)/shard_map/ppermute | solution.py:753
  150.3 9.4 %pair_terms.1 = (bf16[128,5376]{1,0:T(8,128)(2,1)}, bf16[128,5376]{1,0:T(8,128)(2,1)}) custom-call(s32[3]{0:T(128)} %pad_add_fusion.2.info, bf16[5376,256]{1,0:T(8,128)(2,1)} %w_key.5, bf16[5376,256]{1,0:T(8,128)(2,1)} %w_value.5, bf16[512,512]{1,0:T(8,128)(2,1)} %get-tuple-element.130.joined, bf16[256,512]{1,0:T(8,128)(2,1)} %copy-done.13, ...), custom_call_target="tpu_custom_call" | custom-call | flops 2818572288 | bytes 13762560 | tf_op jit(solution)/shard_map/pair_terms/pallas_call | solution.py:607
  163.5 46.0 %while.12 = (s32[]{:T(128)}, f32[672,256]{1,0:T(8,128)}, f32[672,256]{1,0:T(8,128)}, s32[]{:T(128)}, s32[5]{0:T(128)S(1)}, /*index=5*/bf16[512,256]{1,0:T(8,128)...) while((s32[]{:T(128)}, f32[672,256]{1,0:T(8,128)}, ...), condition=%wide.region_3.4_spmd, body=%wide.region_2.3_spmd.sunk | while | flops 18 | bytes 30278384 | solution.py:828
  163.5 4.8 %weight_terms.2 = (bf16[4,672,256]{2,1,0:T(8,128)(2,1)}, bf16[4,672,256]{2,1,0:T(8,128)(2,1)S(1)}) custom-call(s32[5]{0:T(128)S(1)} %broadcast_add_fusion.2.info, bf16[512,256]{1,0:T(8,128)(2,1)S(1)} %get-tuple-element.315.grads, bf16[128,5376]{1,0:T(8,128)(2,1)} %get-tuple-element.316.rest_0_, bf16[128,5376]{1,0:T(8,128)(2,1)} %get-tuple-element.317.rest_1_, ...), custom_call_target="tpu_custom_call" | custom-call | tf_op jit(solution)/shard_map/while/body/weight_terms/pallas_call | solution.py:422
  169.8 4.8 %weight_terms.3 = (bf16[4,672,256]{2,1,0:T(8,128)(2,1)}, bf16[4,672,256]{2,1,0:T(8,128)(2,1)S(1)}) custom-call(s32[5]{0:T(128)S(1)} %broadcast_add_fusion.2.info, bf16[512,256]{1,0:T(8,128)(2,1)S(1)} %get-tuple-element.320.grads, bf16[128,5376]{1,0:T(8,128)(2,1)} %get-tuple-element.316.rest_0_, bf16[128,5376]{1,0:T(8,128)(2,1)} %get-tuple-element.317.rest_1_, ...), custom_call_target="tpu_custom_call" | custom-call | tf_op jit(solution)/shard_map/while/body/weight_terms/pallas_call | solution.py:422
  176.5 2.8 %split_sum.4 = (bf16[2,672,128]{2,1,0:T(8,128)(2,1)S(1)}, bf16[2,672,128]{2,1,0:T(8,128)(2,1)S(1)}, bf16[2,672,128]{2,1,0:T(8,128)(2,1)S(1)}, bf16[2,672,128]{2,1,0:T(8,128)(2,1)S(1)}) custom-call(s32[2]{0:T(128)S(1)} %pad_add_fusion.8.info, bf16[4,672,256]{2,1,0:T(8,128)(2,1)S(1)} %copy-done.1, bf16[4,672,256]{2,1,0:T(8,128)(2,1)S(1)} %copy-done.1, ...), custom_call_target="tpu_custom_call" | custom-call | tf_op jit(solution)/shard_map/while/body/split_sum/pallas_call | solution.py:466
  179.3 3.0 %collective-permute-start.1 = (bf16[2,672,128]{2,1,0:T(8,128)(2,1)S(1)}, bf16[2,672,128]{2,1,0:T(8,128)(2,1)S(1)}, u32[]{:S(2)}, u32[]{:S(2)}) collective-permute-start(bf16[2,672,128]{2,1,0:T(8,128)(2,1)S(1)} %get-tuple-element.262), channel_id=1, source_target_pairs={{0,8},{4,12},{8,0},{12,4},{16,24},{20,28},{24,16},{28,20},{1,9},{5... | collective-permute-start | bytes 1032200 | tf_op jit(solution)/shard_map/while/body/ppermute | solution.py:480
  186.7 4.5 %collective-permute-done.1.rest_2_ = bf16[2,672,128]{2,1,0:T(8,128)(2,1)S(1)} collective-permute-done((bf16[2,672,128]{2,1,0:T(8,128)(2,1)S(1)}, bf16[2,672,128]{2,1,0:T(8,128)(2,1)S(1)}, u32[]{:S(2)}, u32[]{:S(2)}) %collective-permute-start.1) | collective-permute-done | bytes 344096 | tf_op jit(solution)/shard_map/while/body/ppermute | solution.py:480
  209.5 13.6 %collective-permute-done.36.rest_1_ = bf16[128,5376]{1,0:T(8,128)(2,1)} collective-permute-done((bf16[128,5376]{1,0:T(8,128)(2,1)}, bf16[128,5376]{1,0:T(8,128)(2,1)}, u32[]{:S(2)}, u32[]{:S(2)}) %collective-permute-start.36) | collective-permute-done | bytes 1376288 | tf_op jit(solution)/shard_map/ppermute | solution.py:753
  225.8 4.2 %input_grad.1 = bf16[128,5376]{1,0:T(8,128)(2,1)} custom-call(bf16[128,5376]{1,0:T(8,128)(2,1)S(1)} %copy-done.3, f32[1,5376]{1,0:T(1,128)S(1)} %copy-done.5, bf16[128,5376]{1,0:T(8,128)(2,1)S(1)} %copy-done.4, bf16[128,5376]{1,0:T(8,128)(2,1)} %collective-permute-done.36.rest_1_), custom_call_target="tpu_custom_call" | custom-call | bytes 5505024 | tf_op jit(solution)/shard_map/input_grad/pallas_call | solution.py:646
  (152 shorter events, 76.4 us)
Async XLA Ops:
  2.8 33.5 %collective-permute-start.12 = (bf16[672,512]{1,0:T(8,128)(2,1)}, bf16[672,512]{1,0:T(8,128)(2,1)S(1)}, u32[]{:S(2)}, u32[]{:S(2)}) collective-permute-start(bf16[672,512]{1,0:T(8,128)(2,1)} %pad_maximum_fusion), channel_id=1, source_target_pairs={{0,1},{1,0},{2,3},{3,2},{4,5},{5,4},{6,7},{7,6},{8,9},{9,8},{10,11... | collective-permute-start | bytes 2064392 | tf_op jit(solution)/shard_map/ppermute | solution.py:753
  5.8 62.3 %collective-permute-start.11 = (bf16[128,5376]{1,0:T(8,128)(2,1)S(1)}, bf16[128,5376]{1,0:T(8,128)(2,1)}, u32[]{:S(2)}, u32[]{:S(2)}) collective-permute-start(bf16[128,5376]{1,0:T(8,128)(2,1)S(1)} %copy-done.2), channel_id=1, source_target_pairs={{0,2},{1,3},{2,0},{3,1},{4,6},{5,7},{6,4},{7,5},{8,10},{9,11},{10,... | collective-permute-start | bytes 4128776 | tf_op jit(solution)/shard_map/ppermute | solution.py:753
  36.3 16.8 %collective-permute-start.14 = (bf16[672,512]{1,0:T(8,128)(2,1)S(1)}, bf16[672,512]{1,0:T(8,128)(2,1)S(1)}, u32[]{:S(2)}, u32[]{:S(2)}) collective-permute-start(bf16[672,512]{1,0:T(8,128)(2,1)S(1)} %collective-permute-done.12.rest_0_), channel_id=1, source_target_pairs={{0,8},{4,12},{8,0},{12,4},{16,24},{20,28},{24,16},{28,20},{1,9},{5... | collective-permute-start | bytes 2064392 | tf_op jit(solution)/shard_map/ppermute | solution.py:480
  38.0 16.5 %collective-permute-start.15 = (bf16[672,512]{1,0:T(8,128)(2,1)S(1)}, bf16[672,512]{1,0:T(8,128)(2,1)S(1)}, u32[]{:S(2)}, u32[]{:S(2)}) collective-permute-start(bf16[672,512]{1,0:T(8,128)(2,1)S(1)} %collective-permute-done.12.rest_0_), channel_id=1, source_target_pairs={{0,16},{4,20},{8,24},{12,28},{16,0},{20,4},{24,8},{28,12},{1,17},{... | collective-permute-start | bytes 2064392 | tf_op jit(solution)/shard_map/ppermute | solution.py:480
  39.6 28.6 %collective-permute-start.18 = (bf16[672,512]{1,0:T(8,128)(2,1)S(1)}, bf16[672,512]{1,0:T(8,128)(2,1)S(1)}, u32[]{:S(2)}, u32[]{:S(2)}) collective-permute-start(bf16[672,512]{1,0:T(8,128)(2,1)S(1)} %collective-permute-done.12.rest_0_), channel_id=1, source_target_pairs={{0,4},{4,0},{8,12},{12,8},{16,20},{20,16},{24,28},{28,24},{1,5},{5... | collective-permute-start | bytes 2064392 | tf_op jit(solution)/shard_map/ppermute | solution.py:480
  39.6 50.3 %collective-permute-start.25 = (bf16[128,5376]{1,0:T(8,128)(2,1)}, bf16[128,5376]{1,0:T(8,128)(2,1)}, u32[]{:S(2)}, u32[]{:S(2)}) collective-permute-start(bf16[128,5376]{1,0:T(8,128)(2,1)} %get-tuple-element.119.ready), channel_id=1, source_target_pairs={{0,1},{1,0},{2,3},{3,2},{4,5},{5,4},{6,7},{7,6},{8,9},{9,8},{10,11... | collective-permute-start | bytes 4128776 | tf_op jit(solution)/shard_map/ppermute | solution.py:753
  53.1 16.4 %collective-permute-start.16 = (bf16[672,256]{1,0:T(8,128)(2,1)S(1)}, bf16[672,256]{1,0:T(8,128)(2,1)}, u32[]{:S(2)}, u32[]{:S(2)}) collective-permute-start(bf16[672,256]{1,0:T(8,128)(2,1)S(1)} %slice.12), channel_id=1, source_target_pairs={{0,16},{4,20},{8,24},{12,28},{16,0},{20,4},{24,8},{28,12},{1,17},{... | collective-permute-start | bytes 1032200 | tf_op jit(solution)/shard_map/ppermute | solution.py:480
  54.6 15.0 %collective-permute-start.17 = (bf16[672,256]{1,0:T(8,128)(2,1)S(1)}, bf16[672,256]{1,0:T(8,128)(2,1)}, u32[]{:S(2)}, u32[]{:S(2)}) collective-permute-start(bf16[672,256]{1,0:T(8,128)(2,1)S(1)} %slice.13), channel_id=1, source_target_pairs={{0,8},{4,12},{8,0},{12,4},{16,24},{20,28},{24,16},{28,20},{1,9},{5... | collective-permute-start | bytes 1032200 | tf_op jit(solution)/shard_map/ppermute | solution.py:480
  82.8 12.7 %collective-permute-start.23 = (bf16[256,512]{1,0:T(8,128)(2,1)}, bf16[256,512]{1,0:T(8,128)(2,1)S(1)}, u32[]{:S(2)}, u32[]{:S(2)}) collective-permute-start(bf16[256,512]{1,0:T(8,128)(2,1)} %get-tuple-element.117), channel_id=1, source_target_pairs={{0,1},{1,0},{2,3},{3,2},{4,5},{5,4},{6,7},{7,6},{8,9},{9,8},{10,11... | collective-permute-start | bytes 786440 | tf_op jit(solution)/shard_map/ppermute | solution.py:753
  82.8 12.6 %collective-permute-start.24 = (bf16[256,256]{1,0:T(8,128)(2,1)}, bf16[256,256]{1,0:T(8,128)(2,1)S(1)}, u32[]{:S(2)}, u32[]{:S(2)}) collective-permute-start(bf16[256,256]{1,0:T(8,128)(2,1)} %get-tuple-element.118), channel_id=1, source_target_pairs={{0,1},{1,0},{2,3},{3,2},{4,5},{5,4},{6,7},{7,6},{8,9},{9,8},{10,11... | collective-permute-start | bytes 393224 | tf_op jit(solution)/shard_map/ppermute | solution.py:753
  85.0 16.2 %collective-permute-start.27 = (bf16[128,512]{1,0:T(8,128)(2,1)}, bf16[128,512]{1,0:T(8,128)(2,1)S(1)}, u32[]{:S(2)}, u32[]{:S(2)}) collective-permute-start(bf16[128,512]{1,0:T(8,128)(2,1)} %get-tuple-element.121.rest_10_), channel_id=1, source_target_pairs={{0,8},{4,12},{8,16},{12,20},{16,24},{20,28},{1,9},{5,13},{9,17},{1... | collective-permute-start | bytes 393224 | tf_op jit(solution)/shard_map/ppermute | solution.py:689
  88.4 12.8 %collective-permute-start.29 = (bf16[128,512]{1,0:T(8,128)(2,1)}, bf16[128,512]{1,0:T(8,128)(2,1)S(1)}, u32[]{:S(2)}, u32[]{:S(2)}) collective-permute-start(bf16[128,512]{1,0:T(8,128)(2,1)} %get-tuple-element.121.rest_10_), channel_id=1, source_target_pairs={{0,4},{4,8},{8,12},{12,16},{16,20},{20,24},{24,28},{1,5},{5,9},{9,... | collective-permute-start | bytes 393224 | tf_op jit(solution)/shard_map/ppermute | solution.py:689
  99.4 62.3 %collective-permute-start.35 = (bf16[128,5376]{1,0:T(8,128)(2,1)}, bf16[128,5376]{1,0:T(8,128)(2,1)}, u32[]{:S(2)}, u32[]{:S(2)}) collective-permute-start(bf16[128,5376]{1,0:T(8,128)(2,1)} %get-tuple-element.136), channel_id=1, source_target_pairs={{0,1},{1,0},{2,3},{3,2},{4,5},{5,4},{6,7},{7,6},{8,9},{9,8},{10,11... | collective-permute-start | bytes 4128776 | tf_op jit(solution)/shard_map/ppermute | solution.py:753
  113.5 13.4 %collective-permute-start.32 = (bf16[512,256]{1,0:T(8,128)(2,1)}, bf16[512,256]{1,0:T(8,128)(2,1)S(1)}, u32[]{:S(2)}, u32[]{:S(2)}) collective-permute-start(bf16[512,256]{1,0:T(8,128)(2,1)} %get-tuple-element.128), channel_id=1, source_target_pairs={{8,0},{12,4},{16,8},{20,12},{24,16},{28,20},{9,1},{13,5},{17,9},{2... | collective-permute-start | bytes 786440 | tf_op jit(solution)/shard_map/ppermute | solution.py:699
  114.8 12.1 %collective-permute-start.33 = (bf16[512,256]{1,0:T(8,128)(2,1)}, bf16[512,256]{1,0:T(8,128)(2,1)S(1)}, u32[]{:S(2)}, u32[]{:S(2)}) collective-permute-start(bf16[512,256]{1,0:T(8,128)(2,1)} %get-tuple-element.129), channel_id=1, source_target_pairs={{4,0},{8,4},{12,8},{16,12},{20,16},{24,20},{28,24},{5,1},{9,5},{13... | collective-permute-start | bytes 786440 | tf_op jit(solution)/shard_map/ppermute | solution.py:699
  124.1 14.1 %collective-permute-start.30 = (bf16[512,256]{1,0:T(8,128)(2,1)}, bf16[512,256]{1,0:T(8,128)(2,1)S(1)}, u32[]{:S(2)}, u32[]{:S(2)}) collective-permute-start(bf16[512,256]{1,0:T(8,128)(2,1)} %get-tuple-element.123), channel_id=1, source_target_pairs={{8,0},{12,4},{16,8},{20,12},{24,16},{28,20},{9,1},{13,5},{17,9},{2... | collective-permute-start | bytes 786440 | tf_op jit(solution)/shard_map/ppermute | solution.py:699
  125.4 12.8 %collective-permute-start.31 = (bf16[512,256]{1,0:T(8,128)(2,1)}, bf16[512,256]{1,0:T(8,128)(2,1)S(1)}, u32[]{:S(2)}, u32[]{:S(2)}) collective-permute-start(bf16[512,256]{1,0:T(8,128)(2,1)} %get-tuple-element.124), channel_id=1, source_target_pairs={{4,0},{8,4},{12,8},{16,12},{20,16},{24,20},{28,24},{5,1},{9,5},{13... | collective-permute-start | bytes 786440 | tf_op jit(solution)/shard_map/ppermute | solution.py:699
  159.7 63.4 %collective-permute-start.36 = (bf16[128,5376]{1,0:T(8,128)(2,1)}, bf16[128,5376]{1,0:T(8,128)(2,1)}, u32[]{:S(2)}, u32[]{:S(2)}) collective-permute-start(bf16[128,5376]{1,0:T(8,128)(2,1)} %get-tuple-element.133), channel_id=1, source_target_pairs={{0,2},{1,3},{2,0},{3,1},{4,6},{5,7},{6,4},{7,5},{8,10},{9,11},{10,... | collective-permute-start | bytes 4128776 | tf_op jit(solution)/shard_map/ppermute | solution.py:753
  179.3 11.8 %collective-permute-start.1 = (bf16[2,672,128]{2,1,0:T(8,128)(2,1)S(1)}, bf16[2,672,128]{2,1,0:T(8,128)(2,1)S(1)}, u32[]{:S(2)}, u32[]{:S(2)}) collective-permute-start(bf16[2,672,128]{2,1,0:T(8,128)(2,1)S(1)} %get-tuple-element.262), channel_id=1, source_target_pairs={{0,8},{4,12},{8,0},{12,4},{16,24},{20,28},{24,16},{28,20},{1,9},{5... | collective-permute-start | bytes 1032200 | tf_op jit(solution)/shard_map/while/body/ppermute | solution.py:480
  182.3 11.0 %collective-permute-start.2 = (bf16[2,672,128]{2,1,0:T(8,128)(2,1)S(1)}, bf16[2,672,128]{2,1,0:T(8,128)(2,1)S(1)}, u32[]{:S(2)}, u32[]{:S(2)}) collective-permute-start(bf16[2,672,128]{2,1,0:T(8,128)(2,1)S(1)} %get-tuple-element.263), channel_id=1, source_target_pairs={{0,16},{4,20},{8,24},{12,28},{16,0},{20,4},{24,8},{28,12},{1,17},{... | collective-permute-start | bytes 1032200 | tf_op jit(solution)/shard_map/while/body/ppermute | solution.py:480
  184.6 13.9 %collective-permute-start.6 = (bf16[2,672,128]{2,1,0:T(8,128)(2,1)S(1)}, bf16[2,672,128]{2,1,0:T(8,128)(2,1)S(1)}, u32[]{:S(2)}, u32[]{:S(2)}) collective-permute-start(bf16[2,672,128]{2,1,0:T(8,128)(2,1)S(1)} %get-tuple-element.272), channel_id=1, source_target_pairs={{0,8},{4,12},{8,0},{12,4},{16,24},{20,28},{24,16},{28,20},{1,9},{5... | collective-permute-start | bytes 1032200 | tf_op jit(solution)/shard_map/while/body/ppermute | solution.py:480
  186.6 14.0 %collective-permute-start.7 = (bf16[2,672,128]{2,1,0:T(8,128)(2,1)S(1)}, bf16[2,672,128]{2,1,0:T(8,128)(2,1)S(1)}, u32[]{:S(2)}, u32[]{:S(2)}) collective-permute-start(bf16[2,672,128]{2,1,0:T(8,128)(2,1)S(1)} %get-tuple-element.273), channel_id=1, source_target_pairs={{0,16},{4,20},{8,24},{12,28},{16,0},{20,4},{24,8},{28,12},{1,17},{... | collective-permute-start | bytes 1032200 | tf_op jit(solution)/shard_map/while/body/ppermute | solution.py:480
  194.1 10.4 %collective-permute-start.3 = (bf16[1,672,128]{2,1,0:T(8,128)(2,1)S(1)}, bf16[1,672,128]{2,1,0:T(8,128)(2,1)S(1)}, u32[]{:S(2)}, u32[]{:S(2)}) collective-permute-start(bf16[1,672,128]{2,1,0:T(8,128)(2,1)S(1)} %get-tuple-element.266), channel_id=1, source_target_pairs={{0,16},{4,20},{8,24},{12,28},{16,0},{20,4},{24,8},{28,12},{1,17},{... | collective-permute-start | bytes 516104 | tf_op jit(solution)/shard_map/while/body/ppermute | solution.py:480
  195.1 9.4 %collective-permute-start.4 = (bf16[1,672,128]{2,1,0:T(8,128)(2,1)S(1)}, bf16[1,672,128]{2,1,0:T(8,128)(2,1)S(1)}, u32[]{:S(2)}, u32[]{:S(2)}) collective-permute-start(bf16[1,672,128]{2,1,0:T(8,128)(2,1)S(1)} %get-tuple-element.267), channel_id=1, source_target_pairs={{0,8},{4,12},{8,0},{12,4},{16,24},{20,28},{24,16},{28,20},{1,9},{5... | collective-permute-start | bytes 516104 | tf_op jit(solution)/shard_map/while/body/ppermute | solution.py:480
  (43 other events, 337.3 us)

commit v4 on v3

--- a/solution.py
+++ b/solution.py
@@ -168,7 +168,7 @@
         in_specs=[smem_spec()] + [full_spec(a) for a in dense] + [any_spec()] * (2 + len(blocks)),
         out_specs=tuple(full_spec(o) for o in outs),
         scratch_shapes=scratch,
-        compiler_params=params(56),
+        compiler_params=params(63),
         cost_estimate=cost(4 * rows * width * cols, blocks[0], w_key, w_value, *outs),
     )(info, *dense, w_key, w_value, *blocks)
 
@@ -237,7 +237,7 @@
             pltpu.SemaphoreType.DMA((4,)),
             pltpu.SemaphoreType.DMA((len(arrays),)),
         ],
-        compiler_params=params(56),
+        compiler_params=params(63),
         cost_estimate=cost(12 * rows * width * cols, block, w_key, w_value, *arrays, *outs),
     )(info, *dense, w_key, w_value, ready, block, *arrays)
 
@@ -282,20 +282,19 @@
         )
         key_rows = keys[low:high, :]
         value_rows = values[low:high, :]
-        columns = lax.broadcasted_iota(jnp.int32, (tile, width), 1) + low
-        last = lax.broadcasted_iota(jnp.int32, (tile, width), 0) + (top + margin)
-        allowed = (columns >= lowest[top : top + tile, :]) & (columns <= last)
-        scores = dot_last(query_rows, key_rows).reshape(group, tile, width)
-        exps = jnp.where(allowed[None], jnp.exp(scores), 0.0)
-        probs = exps * (1.0 / jnp.sum(exps, axis=-1, keepdims=True))
+        places = lax.broadcasted_iota(jnp.int32, (width, tile), 0) + low
+        last = lax.broadcasted_iota(jnp.int32, (width, tile), 1) + (top + margin)
+        allowed = (places >= lowest[:, top : top + tile]) & (places <= last)
+        allowed = jnp.concatenate([allowed] * group, axis=1)
+        exps = jnp.where(allowed, jnp.exp(dot_last(key_rows, query_rows)), 0.0)
+        probs = exps * (1.0 / jnp.sum(exps, axis=0, keepdims=True))
         weights = probs.astype(jnp.bfloat16)
-        along = dot_last(grad_rows, value_rows).reshape(group, tile, width)
-        deltas = jnp.sum(weights.astype(jnp.float32) * along, axis=-1, keepdims=True)
-        slopes = (probs * (along - deltas)).astype(jnp.bfloat16).reshape(group * tile, width)
-        weights = weights.reshape(group * tile, width)
-        key_sum[low:high, :] += dot_first(slopes, query_rows)
-        value_sum[low:high, :] += dot_first(weights, grad_rows)
-        back = jnp.dot(slopes, key_rows, preferred_element_type=jnp.float32)
+        along = dot_last(value_rows, grad_rows)
+        deltas = jnp.sum(weights.astype(jnp.float32) * along, axis=0, keepdims=True)
+        slopes = (probs * (along - deltas)).astype(jnp.bfloat16)
+        key_sum[low:high, :] += jnp.dot(slopes, query_rows, preferred_element_type=jnp.float32)
+        value_sum[low:high, :] += jnp.dot(weights, grad_rows, preferred_element_type=jnp.float32)
+        back = dot_first(slopes, key_rows)
         for head in range(group):
             turned_back = rope_back(back[head * tile : (head + 1) * tile] * QUERY_SCALE, cos_rows, sin_rows)
             result = norm_back(turned_back, raw[head], scales[head], q_gain[...])
@@ -334,7 +333,7 @@
         out_specs=[full_spec(o) for o in outs],
         scratch_shapes=[pltpu.VMEM((window, head_size), jnp.bfloat16)] * 2
         + [pltpu.VMEM((window, head_size), jnp.float32)] * 2,
-        compiler_params=params(56),
+        compiler_params=params(63),
         cost_estimate=cost(10 * rows * window * cols, queries, grads, *outs),
     )(info, *dense, queries, grads, *arrays)
 
@@ -388,7 +387,7 @@
         + [pl.BlockSpec((tile, head_size), lambda *_, row=row: (row, head)) for _, row in raw_keys]
         + [full_spec(a) for a in before],
         out_specs=tuple(full_spec(o) for o in outs),
-        compiler_params=params(56),
+        compiler_params=params(63),
         cost_estimate=cost(0, own, *arrived, *outs),
     )(info, *dense, *arrays, *before)
     return list(results)
@@ -619,7 +618,7 @@
             pltpu.SemaphoreType.DMA((4,)),
             pltpu.SemaphoreType.DMA((len(arrays),)),
         ],
-        compiler_params=params(56),
+        compiler_params=params(63),
         cost_estimate=cost(16 * rows * width * cols, w_key, w_value, *arrays, *outs),
     )(info, w_key, w_value, joined, arrived, *arrays)
 
@@ -650,7 +649,7 @@
         out_shape=out,
         in_specs=[spec(tokens), full_spec(gain)] + [spec(a) for a in (*sums, *others)],
         out_specs=spec(out),
-        compiler_params=params(),
+        compiler_params=params(63),
         cost_estimate=cost(0, tokens, *sums, *others, out),
     )(tokens, gain, *sums, *others)
 
@@ -849,7 +848,7 @@
         and chunk % 16 == 0
         and width % math.lcm(2 * chunk, 128) == 0
     )
-    args = (tokens, dense, rope_rows, lowest[:, None], raw_queries, out_grad, w_key, w_value, reach)
+    args = (tokens, dense, rope_rows, lowest[None, :], raw_queries, out_grad, w_key, w_value, reach)
     return shards_paired(*args, jnp.minimum(doc_lengths[0], 1)) if paired else shards_general(*args)
 
 

time: 233 us -> 228 us (0.979)
  waiting for transfers between devices: 92.9 us -> 97.4 us
  starting transfers between devices: 50.6 us -> 47.2 us
  local copies, waits for them, and re-layouts: 13.7 us -> 10.9 us
    unnamed x57 -> x41, local copies, waits for them, and re-layouts: 8.46 us -> 4.88 us
    ppermute x19, starting transfers between devices: 21.1 us -> 18.8 us  [swap(): return lax.ppermute(array, 'seq', [(i, i ^ 1 << bit) for i in range(size)])]
  transfers between devices with their start and end apart: 37 -> 37, of which waited for: 17 -> 17; matrix products, arithmetic and copies ran while one was open for 3% -> 4% of each run, Pallas kernels for 27% -> 27%
where the time goes in v4:
time: 228 us; the launch traced here: 227 us
  waiting for transfers between devices  97.4 us (43%)
  Pallas kernels  65.2 us (29%)
  starting transfers between devices  47.2 us (21%)
  local copies, waits for them, and re-layouts  10.9 us (5%)
  other arithmetic  4.79 us (2%)
    ppermute x8, waiting for transfers between devices, trade(): lax.ppermute(array, 'tp', [(i, i ^ distance) for i in range(lax.axis_size...  52.2 us
    ppermute x19, waiting for transfers between devices, swap(): return lax.ppermute(array, 'seq', [(i, i ^ 1 << bit) for i in range(size)])  31 us
    ppermute x19, starting transfers between devices, swap(): return lax.ppermute(array, 'seq', [(i, i ^ 1 << bit) for i in range(size)])  18.8 us
    pallas_call x2, Pallas kernels, attend(): pl.pallas_call(functools.partial(attend_body, reach, slots), name='attend...  15 us
    ppermute x6, starting transfers between devices, halo_of(): sent.append(lax.ppermute(key_value, 'seq', pairs))  13.4 us
    ppermute x8, starting transfers between devices, trade(): lax.ppermute(array, 'tp', [(i, i ^ distance) for i in range(lax.axis_size...  9.72 us
    pallas_call x2, Pallas kernels, weight_terms(): pl.pallas_call(functools.partial(weight_body, len(blocks)), name='weight_...  9.52 us
    pallas_call x1, Pallas kernels, pair_terms(): pl.pallas_call(functools.partial(pair_body, places, heads), name='pair_te...  9.41 us
  transfers between devices with their start and end apart: 37, of which 17 were waited for; matrix products, arithmetic and copies ran while one was open for 4% of the time, Pallas kernels for 27%

profile of v4, /device:TPU:0, one launch (start us, length us, event | category | flops | bytes accessed | tf_op | source)
XLA Modules:
  0.0 226.6 jit_solution(9286529427880558715)
XLA Ops:
  1.9 3.1 %collective-permute-start.12 = (bf16[672,512]{1,0:T(8,128)(2,1)S(1)}, bf16[672,512]{1,0:T(8,128)(2,1)}, u32[]{:S(2)}, u32[]{:S(2)}) collective-permute-start(bf16[672,512]{1,0:T(8,128)(2,1)S(1)} %pad_maximum_fusion), channel_id=1, source_target_pairs={{0,1},{1,0},{2,3},{3,2},{4,5},{5,4},{6,7},{7,6},{8,9},{9,8},{10,11... | collective-permute-start | bytes 2064392 | tf_op jit(solution)/shard_map/ppermute | solution.py:752
  11.1 6.2 %project_block.1 = (bf16[128,512]{1,0:T(8,128)(2,1)}, bf16[128,256]{1,0:T(8,128)(2,1)}, bf16[128,5376]{1,0:T(8,128)(2,1)}) custom-call(s32[2]{0:T(128)} %pad_add_fusion.4.info, f32[1,5376]{1,0:T(1,128)} %broadcast_in_dim.35.gain, f32[1,128]{1,0:T(1,128)} %bitcast.21, f32[512,128]{1,0:T(8,128)} %get-tuple-element.168.cosine, ...), custom_call_target="tpu_custom_call" | custom-call | flops 704643072 | bytes 8454144 | tf_op jit(solution)/shard_map/project_block/pallas_call | solution.py:163
  17.2 3.4 %collective-permute-start.10 = (bf16[128,512]{1,0:T(8,128)(2,1)}, bf16[128,512]{1,0:T(8,128)(2,1)S(1)}, u32[]{:S(2)}, u32[]{:S(2)}) collective-permute-start(bf16[128,512]{1,0:T(8,128)(2,1)} %get-tuple-element.112.rest_8_), channel_id=1, source_target_pairs={{0,8},{4,12},{8,16},{12,20},{16,24},{20,28},{1,9},{5,13},{9,17},{1... | collective-permute-start | bytes 393224 | tf_op jit(solution)/shard_map/ppermute | solution.py:688
  23.5 11.5 %collective-permute-done.12.rest_0_ = bf16[672,512]{1,0:T(8,128)(2,1)} collective-permute-done((bf16[672,512]{1,0:T(8,128)(2,1)S(1)}, bf16[672,512]{1,0:T(8,128)(2,1)}, u32[]{:S(2)}, u32[]{:S(2)}) %collective-permute-start.12) | collective-permute-done | bytes 688160 | tf_op jit(solution)/shard_map/ppermute | solution.py:752
  38.1 13.6 %collective-permute-done.14.rest_1_ = bf16[672,512]{1,0:T(8,128)(2,1)S(1)} collective-permute-done((bf16[672,512]{1,0:T(8,128)(2,1)}, bf16[672,512]{1,0:T(8,128)(2,1)S(1)}, u32[]{:S(2)}, u32[]{:S(2)}) %collective-permute-start.14) | collective-permute-done | bytes 688160 | tf_op jit(solution)/shard_map/ppermute | solution.py:479
  54.8 12.7 %collective-permute-done.11.block = bf16[128,5376]{1,0:T(8,128)(2,1)} collective-permute-done((bf16[128,5376]{1,0:T(8,128)(2,1)}, bf16[128,5376]{1,0:T(8,128)(2,1)}, u32[]{:S(2)}, u32[]{:S(2)}) %collective-permute-start.11) | collective-permute-done | bytes 1376288 | tf_op jit(solution)/shard_map/ppermute | solution.py:752
  72.6 8.4 %project_pair.1 = (bf16[128,512]{1,0:T(8,128)(2,1)}, bf16[128,256]{1,0:T(8,128)(2,1)}, bf16[128,5376]{1,0:T(8,128)(2,1)}, bf16[256,512]{1,0:T(8,128)(2,1)}, bf16[256,256]{1,0:T(8,128)(2,1)}) custom-call(s32[3]{0:T(128)} %pad_add_fusion.2.info, f32[1,5376]{1,0:T(1,128)} %broadcast_in_dim.35.gain, f32[1,128]{1,0:T(1,128)} %bitcast.22, ...), custom_call_target="tpu_custom_call" | custom-call | flops 2113929216 | bytes 14352384 | tf_op jit(solution)/shard_map/project_pair/pallas_call | solution.py:224
  83.1 3.4 %collective-permute-start.27 = (bf16[128,512]{1,0:T(8,128)(2,1)}, bf16[128,512]{1,0:T(8,128)(2,1)S(1)}, u32[]{:S(2)}, u32[]{:S(2)}) collective-permute-start(bf16[128,512]{1,0:T(8,128)(2,1)} %get-tuple-element.121.rest_10_), channel_id=1, source_target_pairs={{0,8},{4,12},{8,16},{12,20},{16,24},{20,28},{1,9},{5,13},{9,17},{1... | collective-permute-start | bytes 393224 | tf_op jit(solution)/shard_map/ppermute | solution.py:688
  87.8 6.6 %collective-permute-done.24.rest_3_.rest_5_ = bf16[256,256]{1,0:T(8,128)(2,1)S(1)} collective-permute-done((bf16[256,256]{1,0:T(8,128)(2,1)}, bf16[256,256]{1,0:T(8,128)(2,1)S(1)}, u32[]{:S(2)}, u32[]{:S(2)}) %collective-permute-start.24) | collective-permute-done | bytes 131104 | tf_op jit(solution)/shard_map/ppermute | solution.py:752
  99.7 3.9 %collective-permute-done.26.rest_1_.rest_3_ = bf16[256,512]{1,0:T(8,128)(2,1)S(1)} collective-permute-done((bf16[256,512]{1,0:T(8,128)(2,1)S(1)}, bf16[256,512]{1,0:T(8,128)(2,1)S(1)}, u32[]{:S(2)}, u32[]{:S(2)}) %collective-permute-start.26) | collective-permute-done | bytes 262176 | tf_op jit(solution)/shard_map/ppermute | solution.py:688
  104.4 7.5 %attend_head.3 = (bf16[512,256]{1,0:T(8,128)(2,1)}, f32[512,256]{1,0:T(8,128)}, bf16[512,256]{1,0:T(8,128)(2,1)}, bf16[512,256]{1,0:T(8,128)(2,1)}) custom-call(s32[4]{0:T(128)} %pad_add_fusion.3.info, s32[1,512]{1,0:T(1,128)} %maximum_subtract_fusion.lowest, f32[1,128]{1,0:T(1,128)} %bitcast.25, f32[512,128]{1,0:T(8,128)} %get-tuple-element.168.cosine, ...), custom_call_target="tpu_custom_call" | custom-call | flops 2013265920 | bytes 2359296 | tf_op jit(solution)/shard_map/attend_head/pallas_call | solution.py:324
  114.5 7.5 %attend_head.2 = (bf16[512,256]{1,0:T(8,128)(2,1)}, f32[512,256]{1,0:T(8,128)}, bf16[512,256]{1,0:T(8,128)(2,1)}, bf16[512,256]{1,0:T(8,128)(2,1)}) custom-call(s32[4]{0:T(128)} %pad_add_fusion.3.info, s32[1,512]{1,0:T(1,128)} %maximum_subtract_fusion.lowest, f32[1,128]{1,0:T(1,128)} %bitcast.26, f32[512,128]{1,0:T(8,128)} %get-tuple-element.168.cosine, ...), custom_call_target="tpu_custom_call" | custom-call | flops 2013265920 | bytes 2359296 | tf_op jit(solution)/shard_map/attend_head/pallas_call | solution.py:324
  127.5 8.8 %collective-permute-done.30.rest_0_ = bf16[512,256]{1,0:T(8,128)(2,1)S(1)} collective-permute-done((bf16[512,256]{1,0:T(8,128)(2,1)}, bf16[512,256]{1,0:T(8,128)(2,1)S(1)}, u32[]{:S(2)}, u32[]{:S(2)}) %collective-permute-start.30) | collective-permute-done | bytes 262176 | tf_op jit(solution)/shard_map/ppermute | solution.py:698
  141.8 6.2 %collective-permute-done.34.arrived = bf16[256,512]{1,0:T(8,128)(2,1)S(1)} collective-permute-done((bf16[256,512]{1,0:T(8,128)(2,1)}, bf16[256,512]{1,0:T(8,128)(2,1)S(1)}, u32[]{:S(2)}, u32[]{:S(2)}) %collective-permute-start.34) | collective-permute-done | bytes 262176 | tf_op jit(solution)/shard_map/ppermute | solution.py:752
  148.7 9.4 %pair_terms.1 = (bf16[128,5376]{1,0:T(8,128)(2,1)}, bf16[128,5376]{1,0:T(8,128)(2,1)}) custom-call(s32[3]{0:T(128)} %pad_add_fusion.2.info, bf16[5376,256]{1,0:T(8,128)(2,1)} %w_key.5, bf16[5376,256]{1,0:T(8,128)(2,1)} %w_value.5, bf16[512,512]{1,0:T(8,128)(2,1)} %get-tuple-element.130.joined, bf16[256,512]{1,0:T(8,128)(2,1)} %copy-done.8, ...), custom_call_target="tpu_custom_call" | custom-call | flops 2818572288 | bytes 13762560 | tf_op jit(solution)/shard_map/pair_terms/pallas_call | solution.py:606
  161.8 44.8 %while.12 = (s32[]{:T(128)}, f32[672,256]{1,0:T(8,128)}, f32[672,256]{1,0:T(8,128)}, s32[]{:T(128)}, s32[5]{0:T(128)S(1)}, /*index=5*/bf16[512,256]{1,0:T(8,128)...) while((s32[]{:T(128)}, f32[672,256]{1,0:T(8,128)}, ...), condition=%wide.region_3.4_spmd, body=%wide.region_2.3_spmd.sunk | while | flops 18 | bytes 30278384 | solution.py:827
  161.8 4.8 %weight_terms.2 = (bf16[4,672,256]{2,1,0:T(8,128)(2,1)}, bf16[4,672,256]{2,1,0:T(8,128)(2,1)S(1)}) custom-call(s32[5]{0:T(128)S(1)} %broadcast_add_fusion.2.info, bf16[512,256]{1,0:T(8,128)(2,1)S(1)} %get-tuple-element.315.grads, bf16[128,5376]{1,0:T(8,128)(2,1)} %get-tuple-element.316.rest_0_, bf16[128,5376]{1,0:T(8,128)(2,1)} %get-tuple-element.317.rest_1_, ...), custom_call_target="tpu_custom_call" | custom-call | tf_op jit(solution)/shard_map/while/body/weight_terms/pallas_call | solution.py:421
  167.5 4.7 %weight_terms.3 = (bf16[4,672,256]{2,1,0:T(8,128)(2,1)}, bf16[4,672,256]{2,1,0:T(8,128)(2,1)S(1)}) custom-call(s32[5]{0:T(128)S(1)} %broadcast_add_fusion.2.info, bf16[512,256]{1,0:T(8,128)(2,1)S(1)} %get-tuple-element.320.grads, bf16[128,5376]{1,0:T(8,128)(2,1)} %get-tuple-element.316.rest_0_, bf16[128,5376]{1,0:T(8,128)(2,1)} %get-tuple-element.317.rest_1_, ...), custom_call_target="tpu_custom_call" | custom-call | tf_op jit(solution)/shard_map/while/body/weight_terms/pallas_call | solution.py:421
  174.2 2.8 %split_sum.4 = (bf16[2,672,128]{2,1,0:T(8,128)(2,1)S(1)}, bf16[2,672,128]{2,1,0:T(8,128)(2,1)S(1)}, bf16[2,672,128]{2,1,0:T(8,128)(2,1)S(1)}, bf16[2,672,128]{2,1,0:T(8,128)(2,1)S(1)}) custom-call(s32[2]{0:T(128)S(1)} %pad_add_fusion.8.info, bf16[4,672,256]{2,1,0:T(8,128)(2,1)S(1)} %copy-done.1, bf16[4,672,256]{2,1,0:T(8,128)(2,1)S(1)} %copy-done.1, ...), custom_call_target="tpu_custom_call" | custom-call | tf_op jit(solution)/shard_map/while/body/split_sum/pallas_call | solution.py:465
  177.0 3.0 %collective-permute-start.1 = (bf16[2,672,128]{2,1,0:T(8,128)(2,1)S(1)}, bf16[2,672,128]{2,1,0:T(8,128)(2,1)S(1)}, u32[]{:S(2)}, u32[]{:S(2)}) collective-permute-start(bf16[2,672,128]{2,1,0:T(8,128)(2,1)S(1)} %get-tuple-element.262), channel_id=1, source_target_pairs={{0,8},{4,12},{8,0},{12,4},{16,24},{20,28},{24,16},{28,20},{1,9},{5... | collective-permute-start | bytes 1032200 | tf_op jit(solution)/shard_map/while/body/ppermute | solution.py:479
  183.8 5.1 %collective-permute-done.1.rest_2_ = bf16[2,672,128]{2,1,0:T(8,128)(2,1)S(1)} collective-permute-done((bf16[2,672,128]{2,1,0:T(8,128)(2,1)S(1)}, bf16[2,672,128]{2,1,0:T(8,128)(2,1)S(1)}, u32[]{:S(2)}, u32[]{:S(2)}) %collective-permute-start.1) | collective-permute-done | bytes 344096 | tf_op jit(solution)/shard_map/while/body/ppermute | solution.py:479
  201.9 2.8 %collective-permute-done.8.rest_6_ = bf16[1,672,128]{2,1,0:T(8,128)(2,1)S(1)} collective-permute-done((bf16[1,672,128]{2,1,0:T(8,128)(2,1)S(1)}, bf16[1,672,128]{2,1,0:T(8,128)(2,1)S(1)}, u32[]{:S(2)}, u32[]{:S(2)}) %collective-permute-start.8) | collective-permute-done | bytes 172064 | tf_op jit(solution)/shard_map/while/body/ppermute | solution.py:479
  206.6 15.2 %collective-permute-done.36.rest_1_ = bf16[128,5376]{1,0:T(8,128)(2,1)} collective-permute-done((bf16[128,5376]{1,0:T(8,128)(2,1)}, bf16[128,5376]{1,0:T(8,128)(2,1)}, u32[]{:S(2)}, u32[]{:S(2)}) %collective-permute-start.36) | collective-permute-done | bytes 1376288 | tf_op jit(solution)/shard_map/ppermute | solution.py:752
  221.9 4.7 %input_grad.1 = bf16[128,5376]{1,0:T(8,128)(2,1)} custom-call(bf16[128,5376]{1,0:T(8,128)(2,1)} %tokens.1, f32[1,5376]{1,0:T(1,128)} %broadcast_in_dim.35.gain, bf16[128,5376]{1,0:T(8,128)(2,1)} %get-tuple-element.142.rest_0_, bf16[128,5376]{1,0:T(8,128)(2,1)} %collective-permute-done.36.rest_1_), custom_call_target="tpu_custom_call" | custom-call | bytes 5505024 | tf_op jit(solution)/shard_map/input_grad/pallas_call | solution.py:645
  (135 shorter events, 70.3 us)
Async XLA Ops:
  1.9 33.0 %collective-permute-start.12 = (bf16[672,512]{1,0:T(8,128)(2,1)S(1)}, bf16[672,512]{1,0:T(8,128)(2,1)}, u32[]{:S(2)}, u32[]{:S(2)}) collective-permute-start(bf16[672,512]{1,0:T(8,128)(2,1)S(1)} %pad_maximum_fusion), channel_id=1, source_target_pairs={{0,1},{1,0},{2,3},{3,2},{4,5},{5,4},{6,7},{7,6},{8,9},{9,8},{10,11... | collective-permute-start | bytes 2064392 | tf_op jit(solution)/shard_map/ppermute | solution.py:752
  4.9 62.5 %collective-permute-start.11 = (bf16[128,5376]{1,0:T(8,128)(2,1)}, bf16[128,5376]{1,0:T(8,128)(2,1)}, u32[]{:S(2)}, u32[]{:S(2)}) collective-permute-start(bf16[128,5376]{1,0:T(8,128)(2,1)} %tokens.1), channel_id=1, source_target_pairs={{0,2},{1,3},{2,0},{3,1},{4,6},{5,7},{6,4},{7,5},{8,10},{9,11},{10,... | collective-permute-start | bytes 4128776 | tf_op jit(solution)/shard_map/ppermute | solution.py:752
  34.9 16.8 %collective-permute-start.14 = (bf16[672,512]{1,0:T(8,128)(2,1)}, bf16[672,512]{1,0:T(8,128)(2,1)S(1)}, u32[]{:S(2)}, u32[]{:S(2)}) collective-permute-start(bf16[672,512]{1,0:T(8,128)(2,1)} %collective-permute-done.12.rest_0_), channel_id=1, source_target_pairs={{0,8},{4,12},{8,0},{12,4},{16,24},{20,28},{24,16},{28,20},{1,9},{5... | collective-permute-start | bytes 2064392 | tf_op jit(solution)/shard_map/ppermute | solution.py:479
  36.6 16.6 %collective-permute-start.15 = (bf16[672,512]{1,0:T(8,128)(2,1)}, bf16[672,512]{1,0:T(8,128)(2,1)S(1)}, u32[]{:S(2)}, u32[]{:S(2)}) collective-permute-start(bf16[672,512]{1,0:T(8,128)(2,1)} %collective-permute-done.12.rest_0_), channel_id=1, source_target_pairs={{0,16},{4,20},{8,24},{12,28},{16,0},{20,4},{24,8},{28,12},{1,17},{... | collective-permute-start | bytes 2064392 | tf_op jit(solution)/shard_map/ppermute | solution.py:479
  38.1 29.4 %collective-permute-start.18 = (bf16[672,512]{1,0:T(8,128)(2,1)}, bf16[672,512]{1,0:T(8,128)(2,1)S(1)}, u32[]{:S(2)}, u32[]{:S(2)}) collective-permute-start(bf16[672,512]{1,0:T(8,128)(2,1)} %collective-permute-done.12.rest_0_), channel_id=1, source_target_pairs={{0,4},{4,0},{8,12},{12,8},{16,20},{20,16},{24,28},{28,24},{1,5},{5... | collective-permute-start | bytes 2064392 | tf_op jit(solution)/shard_map/ppermute | solution.py:479
  38.1 49.7 %collective-permute-start.25 = (bf16[128,5376]{1,0:T(8,128)(2,1)}, bf16[128,5376]{1,0:T(8,128)(2,1)}, u32[]{:S(2)}, u32[]{:S(2)}) collective-permute-start(bf16[128,5376]{1,0:T(8,128)(2,1)} %get-tuple-element.119.ready), channel_id=1, source_target_pairs={{0,1},{1,0},{2,3},{3,2},{4,5},{5,4},{6,7},{7,6},{8,9},{9,8},{10,11... | collective-permute-start | bytes 4128776 | tf_op jit(solution)/shard_map/ppermute | solution.py:752
  51.8 16.2 %collective-permute-start.16 = (bf16[672,256]{1,0:T(8,128)(2,1)S(1)}, bf16[672,256]{1,0:T(8,128)(2,1)S(1)}, u32[]{:S(2)}, u32[]{:S(2)}) collective-permute-start(bf16[672,256]{1,0:T(8,128)(2,1)S(1)} %slice.12), channel_id=1, source_target_pairs={{0,16},{4,20},{8,24},{12,28},{16,0},{20,4},{24,8},{28,12},{1,17},{... | collective-permute-start | bytes 1032200 | tf_op jit(solution)/shard_map/ppermute | solution.py:479
  53.2 14.8 %collective-permute-start.17 = (bf16[672,256]{1,0:T(8,128)(2,1)S(1)}, bf16[672,256]{1,0:T(8,128)(2,1)}, u32[]{:S(2)}, u32[]{:S(2)}) collective-permute-start(bf16[672,256]{1,0:T(8,128)(2,1)S(1)} %slice.13), channel_id=1, source_target_pairs={{0,8},{4,12},{8,0},{12,4},{16,24},{20,28},{24,16},{28,20},{1,9},{5... | collective-permute-start | bytes 1032200 | tf_op jit(solution)/shard_map/ppermute | solution.py:479
  81.0 13.4 %collective-permute-start.23 = (bf16[256,512]{1,0:T(8,128)(2,1)}, bf16[256,512]{1,0:T(8,128)(2,1)S(1)}, u32[]{:S(2)}, u32[]{:S(2)}) collective-permute-start(bf16[256,512]{1,0:T(8,128)(2,1)} %get-tuple-element.117), channel_id=1, source_target_pairs={{0,1},{1,0},{2,3},{3,2},{4,5},{5,4},{6,7},{7,6},{8,9},{9,8},{10,11... | collective-permute-start | bytes 786440 | tf_op jit(solution)/shard_map/ppermute | solution.py:752
  81.1 13.3 %collective-permute-start.24 = (bf16[256,256]{1,0:T(8,128)(2,1)}, bf16[256,256]{1,0:T(8,128)(2,1)S(1)}, u32[]{:S(2)}, u32[]{:S(2)}) collective-permute-start(bf16[256,256]{1,0:T(8,128)(2,1)} %get-tuple-element.118), channel_id=1, source_target_pairs={{0,1},{1,0},{2,3},{3,2},{4,5},{5,4},{6,7},{7,6},{8,9},{9,8},{10,11... | collective-permute-start | bytes 393224 | tf_op jit(solution)/shard_map/ppermute | solution.py:752
  83.1 16.6 %collective-permute-start.27 = (bf16[128,512]{1,0:T(8,128)(2,1)}, bf16[128,512]{1,0:T(8,128)(2,1)S(1)}, u32[]{:S(2)}, u32[]{:S(2)}) collective-permute-start(bf16[128,512]{1,0:T(8,128)(2,1)} %get-tuple-element.121.rest_10_), channel_id=1, source_target_pairs={{0,8},{4,12},{8,16},{12,20},{16,24},{20,28},{1,9},{5,13},{9,17},{1... | collective-permute-start | bytes 393224 | tf_op jit(solution)/shard_map/ppermute | solution.py:688
  86.5 13.2 %collective-permute-start.29 = (bf16[128,512]{1,0:T(8,128)(2,1)}, bf16[128,512]{1,0:T(8,128)(2,1)S(1)}, u32[]{:S(2)}, u32[]{:S(2)}) collective-permute-start(bf16[128,512]{1,0:T(8,128)(2,1)} %get-tuple-element.121.rest_10_), channel_id=1, source_target_pairs={{0,4},{4,8},{8,12},{12,16},{16,20},{20,24},{24,28},{1,5},{5,9},{9,... | collective-permute-start | bytes 393224 | tf_op jit(solution)/shard_map/ppermute | solution.py:688
  98.4 61.6 %collective-permute-start.35 = (bf16[128,5376]{1,0:T(8,128)(2,1)}, bf16[128,5376]{1,0:T(8,128)(2,1)}, u32[]{:S(2)}, u32[]{:S(2)}) collective-permute-start(bf16[128,5376]{1,0:T(8,128)(2,1)} %get-tuple-element.136), channel_id=1, source_target_pairs={{0,1},{1,0},{2,3},{3,2},{4,5},{5,4},{6,7},{7,6},{8,9},{9,8},{10,11... | collective-permute-start | bytes 4128776 | tf_op jit(solution)/shard_map/ppermute | solution.py:752
  111.9 12.9 %collective-permute-start.32 = (bf16[512,256]{1,0:T(8,128)(2,1)}, bf16[512,256]{1,0:T(8,128)(2,1)S(1)}, u32[]{:S(2)}, u32[]{:S(2)}) collective-permute-start(bf16[512,256]{1,0:T(8,128)(2,1)} %get-tuple-element.128), channel_id=1, source_target_pairs={{8,0},{12,4},{16,8},{20,12},{24,16},{28,20},{9,1},{13,5},{17,9},{2... | collective-permute-start | bytes 786440 | tf_op jit(solution)/shard_map/ppermute | solution.py:698
  113.2 11.6 %collective-permute-start.33 = (bf16[512,256]{1,0:T(8,128)(2,1)}, bf16[512,256]{1,0:T(8,128)(2,1)S(1)}, u32[]{:S(2)}, u32[]{:S(2)}) collective-permute-start(bf16[512,256]{1,0:T(8,128)(2,1)} %get-tuple-element.129), channel_id=1, source_target_pairs={{4,0},{8,4},{12,8},{16,12},{20,16},{24,20},{28,24},{5,1},{9,5},{13... | collective-permute-start | bytes 786440 | tf_op jit(solution)/shard_map/ppermute | solution.py:698
  122.0 14.2 %collective-permute-start.30 = (bf16[512,256]{1,0:T(8,128)(2,1)}, bf16[512,256]{1,0:T(8,128)(2,1)S(1)}, u32[]{:S(2)}, u32[]{:S(2)}) collective-permute-start(bf16[512,256]{1,0:T(8,128)(2,1)} %get-tuple-element.123), channel_id=1, source_target_pairs={{8,0},{12,4},{16,8},{20,12},{24,16},{28,20},{9,1},{13,5},{17,9},{2... | collective-permute-start | bytes 786440 | tf_op jit(solution)/shard_map/ppermute | solution.py:698
  123.3 12.9 %collective-permute-start.31 = (bf16[512,256]{1,0:T(8,128)(2,1)}, bf16[512,256]{1,0:T(8,128)(2,1)}, u32[]{:S(2)}, u32[]{:S(2)}) collective-permute-start(bf16[512,256]{1,0:T(8,128)(2,1)} %get-tuple-element.124), channel_id=1, source_target_pairs={{4,0},{8,4},{12,8},{16,12},{20,16},{24,20},{28,24},{5,1},{9,5},{13... | collective-permute-start | bytes 786440 | tf_op jit(solution)/shard_map/ppermute | solution.py:698
  158.1 63.7 %collective-permute-start.36 = (bf16[128,5376]{1,0:T(8,128)(2,1)}, bf16[128,5376]{1,0:T(8,128)(2,1)}, u32[]{:S(2)}, u32[]{:S(2)}) collective-permute-start(bf16[128,5376]{1,0:T(8,128)(2,1)} %get-tuple-element.133), channel_id=1, source_target_pairs={{0,2},{1,3},{2,0},{3,1},{4,6},{5,7},{6,4},{7,5},{8,10},{9,11},{10,... | collective-permute-start | bytes 4128776 | tf_op jit(solution)/shard_map/ppermute | solution.py:752
  177.0 11.8 %collective-permute-start.1 = (bf16[2,672,128]{2,1,0:T(8,128)(2,1)S(1)}, bf16[2,672,128]{2,1,0:T(8,128)(2,1)S(1)}, u32[]{:S(2)}, u32[]{:S(2)}) collective-permute-start(bf16[2,672,128]{2,1,0:T(8,128)(2,1)S(1)} %get-tuple-element.262), channel_id=1, source_target_pairs={{0,8},{4,12},{8,0},{12,4},{16,24},{20,28},{24,16},{28,20},{1,9},{5... | collective-permute-start | bytes 1032200 | tf_op jit(solution)/shard_map/while/body/ppermute | solution.py:479
  180.0 11.0 %collective-permute-start.2 = (bf16[2,672,128]{2,1,0:T(8,128)(2,1)S(1)}, bf16[2,672,128]{2,1,0:T(8,128)(2,1)S(1)}, u32[]{:S(2)}, u32[]{:S(2)}) collective-permute-start(bf16[2,672,128]{2,1,0:T(8,128)(2,1)S(1)} %get-tuple-element.263), channel_id=1, source_target_pairs={{0,16},{4,20},{8,24},{12,28},{16,0},{20,4},{24,8},{28,12},{1,17},{... | collective-permute-start | bytes 1032200 | tf_op jit(solution)/shard_map/while/body/ppermute | solution.py:479
  181.7 14.5 %collective-permute-start.6 = (bf16[2,672,128]{2,1,0:T(8,128)(2,1)S(1)}, bf16[2,672,128]{2,1,0:T(8,128)(2,1)S(1)}, u32[]{:S(2)}, u32[]{:S(2)}) collective-permute-start(bf16[2,672,128]{2,1,0:T(8,128)(2,1)S(1)} %get-tuple-element.272), channel_id=1, source_target_pairs={{0,8},{4,12},{8,0},{12,4},{16,24},{20,28},{24,16},{28,20},{1,9},{5... | collective-permute-start | bytes 1032200 | tf_op jit(solution)/shard_map/while/body/ppermute | solution.py:479
  183.7 14.6 %collective-permute-start.7 = (bf16[2,672,128]{2,1,0:T(8,128)(2,1)S(1)}, bf16[2,672,128]{2,1,0:T(8,128)(2,1)S(1)}, u32[]{:S(2)}, u32[]{:S(2)}) collective-permute-start(bf16[2,672,128]{2,1,0:T(8,128)(2,1)S(1)} %get-tuple-element.273), channel_id=1, source_target_pairs={{0,16},{4,20},{8,24},{12,28},{16,0},{20,4},{24,8},{28,12},{1,17},{... | collective-permute-start | bytes 1032200 | tf_op jit(solution)/shard_map/while/body/ppermute | solution.py:479
  191.9 10.0 %collective-permute-start.3 = (bf16[1,672,128]{2,1,0:T(8,128)(2,1)S(1)}, bf16[1,672,128]{2,1,0:T(8,128)(2,1)S(1)}, u32[]{:S(2)}, u32[]{:S(2)}) collective-permute-start(bf16[1,672,128]{2,1,0:T(8,128)(2,1)S(1)} %get-tuple-element.266), channel_id=1, source_target_pairs={{0,16},{4,20},{8,24},{12,28},{16,0},{20,4},{24,8},{28,12},{1,17},{... | collective-permute-start | bytes 516104 | tf_op jit(solution)/shard_map/while/body/ppermute | solution.py:479
  192.3 9.6 %collective-permute-start.4 = (bf16[1,672,128]{2,1,0:T(8,128)(2,1)S(1)}, bf16[1,672,128]{2,1,0:T(8,128)(2,1)S(1)}, u32[]{:S(2)}, u32[]{:S(2)}) collective-permute-start(bf16[1,672,128]{2,1,0:T(8,128)(2,1)S(1)} %get-tuple-element.267), channel_id=1, source_target_pairs={{0,8},{4,12},{8,0},{12,4},{16,24},{20,28},{24,16},{28,20},{1,9},{5... | collective-permute-start | bytes 516104 | tf_op jit(solution)/shard_map/while/body/ppermute | solution.py:479
  (35 other events, 219.1 us)

commit v5 on v4

--- a/solution.py
+++ b/solution.py
@@ -338,11 +338,10 @@
     )(info, *dense, queries, grads, *arrays)
 
 
-def finish_body(reach, slots, earlier, info, k_gain, cosine, sine, own, *rest):
+def finish_body(reach, slots, info, k_gain, cosine, sine, own, *rest):
     arrived = rest[:reach]
     raw_keys = rest[reach : reach + slots]
-    before = rest[reach + slots : reach + slots + earlier]
-    outs = rest[reach + slots + earlier :]
+    outs = rest[reach + slots :]
     result = outs[0]
     head_size = k_gain.shape[1]
     rows = raw_keys[0].shape[0]
@@ -353,43 +352,35 @@
             total = total + part[place, :].astype(jnp.float32)
         values = raw_keys[slot][...].astype(jnp.float32)
         turned = rope_back(total[:, :head_size], cosine[place, :], sine[place, :])
-        keys = norm_back(turned, values, inv_rms(values), k_gain[...])
-        result[place, :head_size] = keys.astype(jnp.bfloat16)
+        keys = norm_back(turned, values, inv_rms(values), k_gain[...]).astype(jnp.bfloat16)
+        result[place, :head_size] = keys
         result[place, head_size:] = total[:, head_size:].astype(jnp.bfloat16)
-    if len(outs) > 1:
-        joined, away = outs[1:]
-        for head, part in enumerate((*before, result)):
-            joined[:, 2 * head * head_size : 2 * (head + 1) * head_size] = part[...]
-        for number, slot in enumerate((1, 3)):
-            place = pl.ds(pl.multiple_of(info[slot] * rows, 16), rows)
-            away[number * rows : (number + 1) * rows, :] = joined[place, :]
-
-
-def finish(head, info, k_gain, cosine, sine, own, arrived, raw_keys, before=None):
+        if len(outs) > 1 and slot % 2:
+            low = slot // 2 * rows
+            outs[1][low : low + rows, :head_size] = keys
+            outs[1][low : low + rows, head_size:] = total[:, head_size:].astype(jnp.bfloat16)
+
+
+def finish(head, info, k_gain, cosine, sine, own, arrived, raw_keys, trading=False):
     rows, cols = own.shape
     head_size = k_gain.shape[1]
     slots = len(raw_keys)
     tile = rows // slots
     arrays = [array for array, _ in raw_keys]
-    outs = [jax.ShapeDtypeStruct(own.shape, jnp.bfloat16)]
-    if before is not None:
-        width = cols * (len(before) + 1)
-        outs += [jax.ShapeDtypeStruct((count, width), jnp.bfloat16) for count in (rows, 2 * tile)]
-    before = before or []
+    outs = [jax.ShapeDtypeStruct((count, cols), jnp.bfloat16) for count in (rows, 2 * tile)[: 1 + trading]]
     dense = (k_gain, cosine, sine, own, *arrived)
     results = pl.pallas_call(
-        functools.partial(finish_body, len(arrived), slots, len(before)),
+        functools.partial(finish_body, len(arrived), slots),
         name="finish_kv",
         grid=(1,),
         out_shape=tuple(outs),
         in_specs=[smem_spec()]
         + [full_spec(a) for a in dense]
-        + [pl.BlockSpec((tile, head_size), lambda *_, row=row: (row, head)) for _, row in raw_keys]
-        + [full_spec(a) for a in before],
+        + [pl.BlockSpec((tile, head_size), lambda *_, row=row: (row, head)) for _, row in raw_keys],
         out_specs=tuple(full_spec(o) for o in outs),
         compiler_params=params(63),
         cost_estimate=cost(0, own, *arrived, *outs),
-    )(info, *dense, *arrays, *before)
+    )(info, *dense, *arrays)
     return list(results)
 
 
@@ -557,9 +548,10 @@
     )(w_key, w_value, *kv_grads)
 
 
-def pair_body(places, heads, info, w_key, w_value, joined, arrived, *rest):
-    pieces = rest[: len(places)]
-    away_out, own_out, key_held, value_held, held, own_sems, sems = rest[len(places) :]
+def pair_body(places, heads, info, w_key, w_value, *rest):
+    joined, arrived = rest[:heads], rest[heads : 2 * heads]
+    pieces = rest[2 * heads : 2 * heads + len(places)]
+    away_out, own_out, key_held, value_held, held, own_sems, sems = rest[2 * heads + len(places) :]
     rows, width = own_out.shape
     size = w_key.shape[1] // heads
     half = width // 2
@@ -579,14 +571,17 @@
             + [copy for copy, (offset, _) in zip(copies, places) if offset // split == number]
         )
         start_all(groups[number])
-    own_rows = jnp.concatenate(
-        [joined[pl.ds(pl.multiple_of(info[1 + number] * rows, rows), rows), :] for number in range(2)], axis=0
-    )
+    own_rows = [
+        jnp.concatenate(
+            [part[pl.ds(pl.multiple_of(info[1 + number] * rows, rows), rows), :] for number in range(2)], axis=0
+        )
+        for part in joined
+    ]
     sides = [
-        block[:, (2 * head + side) * size : (2 * head + side + 1) * size]
-        for block in (own_rows, arrived[...])
+        block[:, side * size : (side + 1) * size]
+        for blocks in (own_rows, [part[...] for part in arrived])
         for side in range(2)
-        for head in range(heads)
+        for block in blocks
     ]
     left = jnp.concatenate(sides, axis=1)
     for span, group in zip(spans, groups):
@@ -598,7 +593,7 @@
 
 
 def pair_terms(info, joined, arrived, pieces, w_key, w_value, heads):
-    rows = arrived.shape[0] // 2
+    rows = arrived[0].shape[0] // 2
     width, cols = w_key.shape
     places = [(offset, low) for offset, low, _ in pieces]
     arrays = [piece for _, _, piece in pieces]
@@ -608,7 +603,8 @@
         name="pair_terms",
         grid=(1,),
         out_shape=outs,
-        in_specs=[smem_spec(), any_spec(), any_spec(), full_spec(joined), full_spec(arrived)]
+        in_specs=[smem_spec(), any_spec(), any_spec()]
+        + [full_spec(a) for a in (*joined, *arrived)]
         + [any_spec()] * len(arrays),
         out_specs=tuple(full_spec(o) for o in outs),
         scratch_shapes=[
@@ -620,38 +616,60 @@
         ],
         compiler_params=params(63),
         cost_estimate=cost(16 * rows * width * cols, w_key, w_value, *arrays, *outs),
-    )(info, w_key, w_value, joined, arrived, *arrays)
-
-
-def input_grad_body(sums, rest_count, tokens, gain, *rest):
-    out = rest[-1]
-    values = tokens[...].astype(jnp.float32)
-    parts = []
-    if sums:
-        total = rest[0][...].astype(jnp.float32)
-        for piece in rest[1:sums]:
-            total = total + piece[...].astype(jnp.float32)
-        parts.append(total)
-    parts += [piece[...].astype(jnp.float32) for piece in rest[sums : sums + rest_count]]
-    grads = jnp.concatenate(parts, axis=1) if len(parts) > 1 else parts[0]
-    out[...] = norm_back(grads, values, inv_rms(values), gain[...]).astype(jnp.bfloat16)
-
-
-def input_grad(tokens, gain, sums, others):
+    )(info, w_key, w_value, *joined, *arrived, *arrays)
+
+
+def input_grad_body(count, steps, tokens, gain, *rest):
+    pieces = rest[:count]
+    out, held, piece_held, out_held, sems, out_sems = rest[count:]
+    rows = out_held.shape[0] // steps
+    arrays = [(tokens, held)] + [(piece, piece_held.at[number]) for number, piece in enumerate(pieces)]
+    copies = []
+    for step in range(steps):
+        span = pl.ds(step * rows, rows)
+        copies.append(
+            [
+                pltpu.make_async_copy(source.at[span], target.at[span], sems.at[step, number])
+                for number, (source, target) in enumerate(arrays)
+            ]
+        )
+        start_all(copies[step])
+    results = []
+    for step in range(steps):
+        span = slice(step * rows, (step + 1) * rows)
+        wait_all(copies[step])
+        values = held[span, :].astype(jnp.float32)
+        grads = piece_held[0, span, :].astype(jnp.float32)
+        for number in range(1, count):
+            grads = grads + piece_held[number, span, :].astype(jnp.float32)
+        out_held[span, :] = norm_back(grads, values, inv_rms(values), gain[...]).astype(jnp.bfloat16)
+        span = pl.ds(step * rows, rows)
+        results.append(pltpu.make_async_copy(out_held.at[span], out.at[span], out_sems.at[step]))
+        results[step].start()
+    wait_all(results)
+
+
+def input_grad(tokens, gain, pieces):
     out = jax.ShapeDtypeStruct(tokens.shape, jnp.bfloat16)
-    rows = tokens.shape[0]
-    tile = 32 if rows % 32 == 0 else rows
-    spec = lambda array: pl.BlockSpec((tile, array.shape[1]), lambda step: (step, 0))
+    rows, width = tokens.shape
+    steps = 4 if rows % 64 == 0 else 1
     return pl.pallas_call(
-        functools.partial(input_grad_body, len(sums), len(others)),
+        functools.partial(input_grad_body, len(pieces), steps),
         name="input_grad",
-        grid=(rows // tile,),
+        grid=(1,),
         out_shape=out,
-        in_specs=[spec(tokens), full_spec(gain)] + [spec(a) for a in (*sums, *others)],
-        out_specs=spec(out),
+        in_specs=[any_spec(), full_spec(gain)] + [any_spec()] * len(pieces),
+        out_specs=any_spec(),
+        scratch_shapes=[
+            pltpu.VMEM((rows, width), jnp.bfloat16),
+            pltpu.VMEM((len(pieces), rows, width), jnp.bfloat16),
+            pltpu.VMEM((rows, width), jnp.bfloat16),
+            pltpu.SemaphoreType.DMA((steps, 1 + len(pieces))),
+            pltpu.SemaphoreType.DMA((steps,)),
+        ],
         compiler_params=params(63),
-        cost_estimate=cost(0, tokens, *sums, *others, out),
-    )(tokens, gain, *sums, *others)
+        cost_estimate=cost(0, tokens, *pieces, out),
+    )(tokens, gain, *pieces)
 
 
 def spread_corners(parts):
@@ -739,7 +757,7 @@
     grad_queries = jnp.concatenate(query_parts, axis=1)
     partial_sum = input_terms(kv_grads, w_key, w_value, 0)
     summed_part = lax.psum_scatter(partial_sum, "tp", scatter_dimension=0, tiled=True)
-    grad_x = input_grad(tokens, gain_row, [], [summed_part])
+    grad_x = input_grad(tokens, gain_row, [summed_part])
     left = jnp.concatenate(normed_blocks, axis=0)
     order = (slot_places[:, None] * rows + jnp.arange(rows, dtype=jnp.int32)[None, :]).reshape(-1)
     joined = [g[:, :head_size] for g in kv_grads] + [g[:, head_size:] for g in kv_grads]
@@ -799,20 +817,19 @@
     raw_keys = [(keys_0, 0), (arrived_keys, 0), (keys_2, 0), (arrived_keys, 1)]
     normed = [normed_0, partner_normed_0, normed_2, partner_normed_2]
     weight_info = jnp.concatenate([slot_places, (seq_index & 1)[None]])
-    query_parts, kv_grads = [], []
+    query_parts, kv_grads, arrived = [], [], []
     for head in range(kv_heads):
         outs = attend(head, kv_heads, reach, slot_places, lowest, q_row, cosine, sine, raw_queries, out_grad, blocks)
         query_parts.append(outs[0])
         back = halo_back(outs[2:])
-        before = kv_grads if head == kv_heads - 1 else None
-        results = finish(head, slot_places, k_row, cosine, sine, outs[1], back, raw_keys, before=before)
-        kv_grads = kv_grads + results[:1]
+        own = after(outs[1], arrived)
+        grads, away = finish(head, slot_places, k_row, cosine, sine, own, back, raw_keys, trading=True)
+        kv_grads.append(grads)
+        arrived.append(trade(away, 1))
     grad_queries = jnp.concatenate(query_parts, axis=1)
 
-    joined, away = results[1:]
-    arrived = trade(away, 1)
     info = jnp.stack([seq_index, place, place ^ 2])
-    away_terms, own_terms = pair_terms(info, joined, arrived, pieces, w_key, w_value, kv_heads)
+    away_terms, own_terms = pair_terms(info, kv_grads, arrived, pieces, w_key, w_value, kv_heads)
     other_terms = trade(away_terms, 2)
 
     def weight_step(step, _):
@@ -825,7 +842,8 @@
 
     empty = jnp.zeros((chunk, cols), jnp.float32)
     grad_wk, grad_wv = lax.fori_loop(0, after(once, away_terms), weight_step, (empty, empty))
-    grad_x = input_grad(tokens, gain_row, [after(own_terms, (grad_wk, grad_wv, grad_queries)), other_terms], [])
+    own_terms = after(own_terms, (grad_wk, grad_wv, grad_queries))
+    grad_x = input_grad(tokens, gain_row, [own_terms, other_terms])
     return (grad_x, grad_queries, grad_wk, grad_wv)
 
 

time: 228 us -> 226 us (level)
  waiting for transfers between devices: 97.4 us -> 91.2 us
  starting transfers between devices: 47.2 us -> 49.9 us
    ppermute x4, waiting for transfers between devices: 8.76 us -> 2.98 us  [halo_back(): back.append(lax.ppermute(array, 'seq', pairs))]
    ppermute x19, starting transfers between devices: 18.8 us -> 21.4 us  [swap(): return lax.ppermute(array, 'seq', [(i, i ^ 1 << bit) for i in range(size)])]
    ppermute x8 -> x9, waiting for transfers between devices: 52.2 us -> 49.7 us  [trade(): lax.ppermute(array, 'tp', [(i, i ^ distance) for i in range(lax.axis_size...]
    unnamed x41 -> x43, local copies, waits for them, and re-layouts: 4.88 us -> 4.75 us
    ppermute x8 -> x9, starting transfers between devices: 9.72 us -> 9.73 us  [trade(): lax.ppermute(array, 'tp', [(i, i ^ distance) for i in range(lax.axis_size...]
  transfers between devices with their start and end apart: 37 -> 38, of which waited for: 17 -> 18; matrix products, arithmetic and copies ran while one was open for 4% -> 4% of each run, Pallas kernels for 27% -> 27%
where the time goes in v5:
time: 226 us; the launch traced here: 223 us
  waiting for transfers between devices  91.2 us (40%)
  Pallas kernels  65.1 us (29%)
  starting transfers between devices  49.9 us (22%)
  local copies, waits for them, and re-layouts  10.7 us (5%)
  other arithmetic  4.99 us (2%)
    ppermute x9, waiting for transfers between devices, trade(): lax.ppermute(array, 'tp', [(i, i ^ distance) for i in range(lax.axis_size...  49.7 us
    ppermute x19, waiting for transfers between devices, swap(): return lax.ppermute(array, 'seq', [(i, i ^ 1 << bit) for i in range(size)])  33.1 us
    ppermute x19, starting transfers between devices, swap(): return lax.ppermute(array, 'seq', [(i, i ^ 1 << bit) for i in range(size)])  21.4 us
    pallas_call x2, Pallas kernels, attend(): pl.pallas_call(functools.partial(attend_body, reach, slots), name='attend...  14.9 us
    ppermute x6, starting transfers between devices, halo_of(): sent.append(lax.ppermute(key_value, 'seq', pairs))  13.4 us
    ppermute x9, starting transfers between devices, trade(): lax.ppermute(array, 'tp', [(i, i ^ distance) for i in range(lax.axis_size...  9.73 us
    pallas_call x2, Pallas kernels, weight_terms(): pl.pallas_call(functools.partial(weight_body, len(blocks)), name='weight_...  9.53 us
    pallas_call x1, Pallas kernels, pair_terms(): pl.pallas_call(functools.partial(pair_body, places, heads), name='pair_te...  9.46 us
  transfers between devices with their start and end apart: 38, of which 18 were waited for; matrix products, arithmetic and copies ran while one was open for 4% of the time, Pallas kernels for 27%

profile of v5, /device:TPU:0, one launch (start us, length us, event | category | flops | bytes accessed | tf_op | source)
XLA Modules:
  0.0 223.2 jit_solution(1877301232311214594)
XLA Ops:
  11.0 6.2 %project_block.1 = (bf16[128,512]{1,0:T(8,128)(2,1)}, bf16[128,256]{1,0:T(8,128)(2,1)}, bf16[128,5376]{1,0:T(8,128)(2,1)}) custom-call(s32[2]{0:T(128)} %pad_add_fusion.4.info, f32[1,5376]{1,0:T(1,128)} %broadcast_in_dim.35.gain, f32[1,128]{1,0:T(1,128)} %bitcast.21, f32[512,128]{1,0:T(8,128)} %get-tuple-element.172.cosine, ...), custom_call_target="tpu_custom_call" | custom-call | flops 704643072 | bytes 8454144 | tf_op jit(solution)/shard_map/project_block/pallas_call | solution.py:163
  17.2 3.4 %collective-permute-start.10 = (bf16[128,512]{1,0:T(8,128)(2,1)}, bf16[128,512]{1,0:T(8,128)(2,1)S(1)}, u32[]{:S(2)}, u32[]{:S(2)}) collective-permute-start(bf16[128,512]{1,0:T(8,128)(2,1)} %get-tuple-element.114.rest_8_), channel_id=1, source_target_pairs={{0,8},{4,12},{8,16},{12,20},{16,24},{20,28},{1,9},{5,13},{9,17},{1... | collective-permute-start | bytes 393224 | tf_op jit(solution)/shard_map/ppermute | solution.py:706
  23.4 11.5 %collective-permute-done.12.rest_0_.rest_4_ = bf16[672,512]{1,0:T(8,128)(2,1)} collective-permute-done((bf16[672,512]{1,0:T(8,128)(2,1)S(1)}, bf16[672,512]{1,0:T(8,128)(2,1)}, u32[]{:S(2)}, u32[]{:S(2)}) %collective-permute-start.12) | collective-permute-done | bytes 688160 | tf_op jit(solution)/shard_map/ppermute | solution.py:770
  38.1 13.6 %collective-permute-done.14.rest_1_.rest_5_ = bf16[672,512]{1,0:T(8,128)(2,1)S(1)} collective-permute-done((bf16[672,512]{1,0:T(8,128)(2,1)}, bf16[672,512]{1,0:T(8,128)(2,1)S(1)}, u32[]{:S(2)}, u32[]{:S(2)}) %collective-permute-start.14) | collective-permute-done | bytes 688160 | tf_op jit(solution)/shard_map/ppermute | solution.py:470
  54.8 12.7 %collective-permute-done.11.block = bf16[128,5376]{1,0:T(8,128)(2,1)} collective-permute-done((bf16[128,5376]{1,0:T(8,128)(2,1)}, bf16[128,5376]{1,0:T(8,128)(2,1)}, u32[]{:S(2)}, u32[]{:S(2)}) %collective-permute-start.11) | collective-permute-done | bytes 1376288 | tf_op jit(solution)/shard_map/ppermute | solution.py:770
  72.6 8.3 %project_pair.1 = (bf16[128,512]{1,0:T(8,128)(2,1)}, bf16[128,256]{1,0:T(8,128)(2,1)}, bf16[128,5376]{1,0:T(8,128)(2,1)}, bf16[256,512]{1,0:T(8,128)(2,1)}, bf16[256,256]{1,0:T(8,128)(2,1)}) custom-call(s32[3]{0:T(128)} %pad_add_fusion.2.info, f32[1,5376]{1,0:T(1,128)} %broadcast_in_dim.35.gain, f32[1,128]{1,0:T(1,128)} %bitcast.22, ...), custom_call_target="tpu_custom_call" | custom-call | flops 2113929216 | bytes 14352384 | tf_op jit(solution)/shard_map/project_pair/pallas_call | solution.py:224
  83.0 3.4 %collective-permute-start.27 = (bf16[128,512]{1,0:T(8,128)(2,1)}, bf16[128,512]{1,0:T(8,128)(2,1)S(1)}, u32[]{:S(2)}, u32[]{:S(2)}) collective-permute-start(bf16[128,512]{1,0:T(8,128)(2,1)} %get-tuple-element.123.rest_10_), channel_id=1, source_target_pairs={{0,8},{4,12},{8,16},{12,20},{16,24},{20,28},{1,9},{5,13},{9,17},{1... | collective-permute-start | bytes 393224 | tf_op jit(solution)/shard_map/ppermute | solution.py:706
  87.8 6.6 %collective-permute-done.24.rest_3_.rest_5_ = bf16[256,256]{1,0:T(8,128)(2,1)S(1)} collective-permute-done((bf16[256,256]{1,0:T(8,128)(2,1)}, bf16[256,256]{1,0:T(8,128)(2,1)S(1)}, u32[]{:S(2)}, u32[]{:S(2)}) %collective-permute-start.24) | collective-permute-done | bytes 131104 | tf_op jit(solution)/shard_map/ppermute | solution.py:770
  99.8 3.8 %collective-permute-done.26.rest_1_.rest_3_ = bf16[256,512]{1,0:T(8,128)(2,1)S(1)} collective-permute-done((bf16[256,512]{1,0:T(8,128)(2,1)S(1)}, bf16[256,512]{1,0:T(8,128)(2,1)S(1)}, u32[]{:S(2)}, u32[]{:S(2)}) %collective-permute-start.26) | collective-permute-done | bytes 262176 | tf_op jit(solution)/shard_map/ppermute | solution.py:706
  104.4 7.4 %attend_head.2 = (bf16[512,256]{1,0:T(8,128)(2,1)}, f32[512,256]{1,0:T(8,128)}, bf16[512,256]{1,0:T(8,128)(2,1)}, bf16[512,256]{1,0:T(8,128)(2,1)}) custom-call(s32[4]{0:T(128)} %pad_add_fusion.3.info, s32[1,512]{1,0:T(1,128)} %maximum_subtract_fusion.lowest, f32[1,128]{1,0:T(1,128)} %bitcast.25, f32[512,128]{1,0:T(8,128)} %get-tuple-element.172.cosine, ...), custom_call_target="tpu_custom_call" | custom-call | flops 2013265920 | bytes 2359296 | tf_op jit(solution)/shard_map/attend_head/pallas_call | solution.py:324
  114.4 7.5 %attend_head.3 = (bf16[512,256]{1,0:T(8,128)(2,1)}, f32[512,256]{1,0:T(8,128)}, bf16[512,256]{1,0:T(8,128)(2,1)}, bf16[512,256]{1,0:T(8,128)(2,1)}) custom-call(s32[4]{0:T(128)} %pad_add_fusion.3.info, s32[1,512]{1,0:T(1,128)} %maximum_subtract_fusion.lowest, f32[1,128]{1,0:T(1,128)} %bitcast.26, f32[512,128]{1,0:T(8,128)} %get-tuple-element.172.cosine, ...), custom_call_target="tpu_custom_call" | custom-call | flops 2013265920 | bytes 2359296 | tf_op jit(solution)/shard_map/attend_head/pallas_call | solution.py:324
  128.1 5.0 %collective-permute-done.32.rest_2_ = bf16[256,256]{1,0:T(8,128)(2,1)S(1)} collective-permute-done((bf16[256,256]{1,0:T(8,128)(2,1)}, bf16[256,256]{1,0:T(8,128)(2,1)S(1)}, u32[]{:S(2)}, u32[]{:S(2)}) %collective-permute-start.32) | collective-permute-done | bytes 131104 | tf_op jit(solution)/shard_map/ppermute | solution.py:770
  141.3 3.5 %collective-permute-done.35.rest_3_ = bf16[256,256]{1,0:T(8,128)(2,1)S(1)} collective-permute-done((bf16[256,256]{1,0:T(8,128)(2,1)}, bf16[256,256]{1,0:T(8,128)(2,1)S(1)}, u32[]{:S(2)}, u32[]{:S(2)}) %collective-permute-start.35) | collective-permute-done | bytes 131104 | tf_op jit(solution)/shard_map/ppermute | solution.py:770
  145.5 9.5 %pair_terms.1 = (bf16[128,5376]{1,0:T(8,128)(2,1)}, bf16[128,5376]{1,0:T(8,128)(2,1)}) custom-call(s32[3]{0:T(128)} %pad_add_fusion.2.info, bf16[5376,256]{1,0:T(8,128)(2,1)} %w_key.5, bf16[5376,256]{1,0:T(8,128)(2,1)} %w_value.5, bf16[512,256]{1,0:T(8,128)(2,1)S(1)} %get-tuple-element.289.rest_0_, bf16[512,256]{1,0:T(8,128)(2,1)S(1)} %get-tuple-element.294.rest_1_, ...), custom_call_target="tpu_custom_call" | custom-call | flops 2818572288 | bytes 13762560 | tf_op jit(solution)/shard_map/pair_terms/pallas_call | solution.py:601
  158.6 49.7 %while.12 = (s32[]{:T(128)}, f32[672,256]{1,0:T(8,128)}, f32[672,256]{1,0:T(8,128)}, s32[]{:T(128)}, s32[5]{0:T(128)S(1)}, /*index=5*/bf16[512,256]{1,0:T(8,128)...) while((s32[]{:T(128)}, f32[672,256]{1,0:T(8,128)}, ...), condition=%wide.region_3.4_spmd, body=%wide.region_2.3_spmd.sunk | while | flops 18 | bytes 30278384 | solution.py:844
  158.6 4.8 %weight_terms.2 = (bf16[4,672,256]{2,1,0:T(8,128)(2,1)}, bf16[4,672,256]{2,1,0:T(8,128)(2,1)S(1)}) custom-call(s32[5]{0:T(128)S(1)} %broadcast_add_fusion.2.info, bf16[512,256]{1,0:T(8,128)(2,1)S(1)} %get-tuple-element.319.grads, bf16[128,5376]{1,0:T(8,128)(2,1)} %get-tuple-element.320.rest_0_, bf16[128,5376]{1,0:T(8,128)(2,1)} %get-tuple-element.321.rest_1_, ...), custom_call_target="tpu_custom_call" | custom-call | tf_op jit(solution)/shard_map/while/body/weight_terms/pallas_call | solution.py:412
  164.4 4.8 %weight_terms.3 = (bf16[4,672,256]{2,1,0:T(8,128)(2,1)}, bf16[4,672,256]{2,1,0:T(8,128)(2,1)S(1)}) custom-call(s32[5]{0:T(128)S(1)} %broadcast_add_fusion.2.info, bf16[512,256]{1,0:T(8,128)(2,1)S(1)} %get-tuple-element.324.grads, bf16[128,5376]{1,0:T(8,128)(2,1)} %get-tuple-element.320.rest_0_, bf16[128,5376]{1,0:T(8,128)(2,1)} %get-tuple-element.321.rest_1_, ...), custom_call_target="tpu_custom_call" | custom-call | tf_op jit(solution)/shard_map/while/body/weight_terms/pallas_call | solution.py:412
  174.0 4.7 %collective-permute-start.1 = (bf16[2,672,128]{2,1,0:T(8,128)(2,1)S(1)}, bf16[2,672,128]{2,1,0:T(8,128)(2,1)S(1)}, u32[]{:S(2)}, u32[]{:S(2)}) collective-permute-start(bf16[2,672,128]{2,1,0:T(8,128)(2,1)S(1)} %get-tuple-element.266), channel_id=1, source_target_pairs={{0,8},{4,12},{8,0},{12,4},{16,24},{20,28},{24,16},{28,20},{1,9},{5... | collective-permute-start | bytes 1032200 | tf_op jit(solution)/shard_map/while/body/ppermute | solution.py:470
  178.7 3.4 %collective-permute-start.2 = (bf16[2,672,128]{2,1,0:T(8,128)(2,1)S(1)}, bf16[2,672,128]{2,1,0:T(8,128)(2,1)S(1)}, u32[]{:S(2)}, u32[]{:S(2)}) collective-permute-start(bf16[2,672,128]{2,1,0:T(8,128)(2,1)S(1)} %get-tuple-element.267), channel_id=1, source_target_pairs={{0,16},{4,20},{8,24},{12,28},{16,0},{20,4},{24,8},{28,12},{1,17},{... | collective-permute-start | bytes 1032200 | tf_op jit(solution)/shard_map/while/body/ppermute | solution.py:470
  183.7 3.9 %collective-permute-done.1.rest_2_ = bf16[2,672,128]{2,1,0:T(8,128)(2,1)S(1)} collective-permute-done((bf16[2,672,128]{2,1,0:T(8,128)(2,1)S(1)}, bf16[2,672,128]{2,1,0:T(8,128)(2,1)S(1)}, u32[]{:S(2)}, u32[]{:S(2)}) %collective-permute-start.1) | collective-permute-done | bytes 344096 | tf_op jit(solution)/shard_map/while/body/ppermute | solution.py:470
  194.7 3.5 %collective-permute-done.7.rest_3_ = bf16[2,672,128]{2,1,0:T(8,128)(2,1)S(1)} collective-permute-done((bf16[2,672,128]{2,1,0:T(8,128)(2,1)S(1)}, bf16[2,672,128]{2,1,0:T(8,128)(2,1)S(1)}, u32[]{:S(2)}, u32[]{:S(2)}) %collective-permute-start.7) | collective-permute-done | bytes 344096 | tf_op jit(solution)/shard_map/while/body/ppermute | solution.py:470
  201.8 3.4 %collective-permute-done.8.rest_6_ = bf16[1,672,128]{2,1,0:T(8,128)(2,1)S(1)} collective-permute-done((bf16[1,672,128]{2,1,0:T(8,128)(2,1)S(1)}, bf16[1,672,128]{2,1,0:T(8,128)(2,1)S(1)}, u32[]{:S(2)}, u32[]{:S(2)}) %collective-permute-start.8) | collective-permute-done | bytes 172064 | tf_op jit(solution)/shard_map/while/body/ppermute | solution.py:470
  208.3 10.4 %collective-permute-done.37.rest_1_ = bf16[128,5376]{1,0:T(8,128)(2,1)} collective-permute-done((bf16[128,5376]{1,0:T(8,128)(2,1)}, bf16[128,5376]{1,0:T(8,128)(2,1)}, u32[]{:S(2)}, u32[]{:S(2)}) %collective-permute-start.37) | collective-permute-done | bytes 1376288 | tf_op jit(solution)/shard_map/ppermute | solution.py:770
  218.7 4.3 %input_grad.1 = bf16[128,5376]{1,0:T(8,128)(2,1)} custom-call(bf16[128,5376]{1,0:T(8,128)(2,1)} %tokens.1, f32[1,5376]{1,0:T(1,128)} %broadcast_in_dim.35.gain, bf16[128,5376]{1,0:T(8,128)(2,1)} %get-tuple-element.146.rest_0_, bf16[128,5376]{1,0:T(8,128)(2,1)} %collective-permute-done.37.rest_1_), custom_call_target="tpu_custom_call" | custom-call | bytes 5505024 | tf_op jit(solution)/shard_map/input_grad/pallas_call | solution.py:656
  (139 shorter events, 76.3 us)
Async XLA Ops:
  1.9 33.0 %collective-permute-start.12 = (bf16[672,512]{1,0:T(8,128)(2,1)S(1)}, bf16[672,512]{1,0:T(8,128)(2,1)}, u32[]{:S(2)}, u32[]{:S(2)}) collective-permute-start(bf16[672,512]{1,0:T(8,128)(2,1)S(1)} %pad_maximum_fusion), channel_id=1, source_target_pairs={{0,1},{1,0},{2,3},{3,2},{4,5},{5,4},{6,7},{7,6},{8,9},{9,8},{10,11... | collective-permute-start | bytes 2064392 | tf_op jit(solution)/shard_map/ppermute | solution.py:770
  4.9 62.5 %collective-permute-start.11 = (bf16[128,5376]{1,0:T(8,128)(2,1)}, bf16[128,5376]{1,0:T(8,128)(2,1)}, u32[]{:S(2)}, u32[]{:S(2)}) collective-permute-start(bf16[128,5376]{1,0:T(8,128)(2,1)} %tokens.1), channel_id=1, source_target_pairs={{0,2},{1,3},{2,0},{3,1},{4,6},{5,7},{6,4},{7,5},{8,10},{9,11},{10,... | collective-permute-start | bytes 4128776 | tf_op jit(solution)/shard_map/ppermute | solution.py:770
  34.9 16.8 %collective-permute-start.14 = (bf16[672,512]{1,0:T(8,128)(2,1)}, bf16[672,512]{1,0:T(8,128)(2,1)S(1)}, u32[]{:S(2)}, u32[]{:S(2)}) collective-permute-start(bf16[672,512]{1,0:T(8,128)(2,1)} %collective-permute-done.12.rest_0_.rest_4_), channel_id=1, source_target_pairs={{0,8},{4,12},{8,0},{12,4},{16,24},{20,28},{24,16},{28,20},{1,9},{5... | collective-permute-start | bytes 2064392 | tf_op jit(solution)/shard_map/ppermute | solution.py:470
  36.6 16.6 %collective-permute-start.15 = (bf16[672,512]{1,0:T(8,128)(2,1)}, bf16[672,512]{1,0:T(8,128)(2,1)S(1)}, u32[]{:S(2)}, u32[]{:S(2)}) collective-permute-start(bf16[672,512]{1,0:T(8,128)(2,1)} %collective-permute-done.12.rest_0_.rest_4_), channel_id=1, source_target_pairs={{0,16},{4,20},{8,24},{12,28},{16,0},{20,4},{24,8},{28,12},{1,17},{... | collective-permute-start | bytes 2064392 | tf_op jit(solution)/shard_map/ppermute | solution.py:470
  38.1 29.4 %collective-permute-start.18 = (bf16[672,512]{1,0:T(8,128)(2,1)}, bf16[672,512]{1,0:T(8,128)(2,1)S(1)}, u32[]{:S(2)}, u32[]{:S(2)}) collective-permute-start(bf16[672,512]{1,0:T(8,128)(2,1)} %collective-permute-done.12.rest_0_.rest_4_), channel_id=1, source_target_pairs={{0,4},{4,0},{8,12},{12,8},{16,20},{20,16},{24,28},{28,24},{1,5},{5... | collective-permute-start | bytes 2064392 | tf_op jit(solution)/shard_map/ppermute | solution.py:470
  38.1 49.7 %collective-permute-start.25 = (bf16[128,5376]{1,0:T(8,128)(2,1)}, bf16[128,5376]{1,0:T(8,128)(2,1)}, u32[]{:S(2)}, u32[]{:S(2)}) collective-permute-start(bf16[128,5376]{1,0:T(8,128)(2,1)} %get-tuple-element.121.ready), channel_id=1, source_target_pairs={{0,1},{1,0},{2,3},{3,2},{4,5},{5,4},{6,7},{7,6},{8,9},{9,8},{10,11... | collective-permute-start | bytes 4128776 | tf_op jit(solution)/shard_map/ppermute | solution.py:770
  51.8 16.2 %collective-permute-start.16 = (bf16[672,256]{1,0:T(8,128)(2,1)S(1)}, bf16[672,256]{1,0:T(8,128)(2,1)S(1)}, u32[]{:S(2)}, u32[]{:S(2)}) collective-permute-start(bf16[672,256]{1,0:T(8,128)(2,1)S(1)} %slice.12), channel_id=1, source_target_pairs={{0,16},{4,20},{8,24},{12,28},{16,0},{20,4},{24,8},{28,12},{1,17},{... | collective-permute-start | bytes 1032200 | tf_op jit(solution)/shard_map/ppermute | solution.py:470
  53.2 14.8 %collective-permute-start.17 = (bf16[672,256]{1,0:T(8,128)(2,1)S(1)}, bf16[672,256]{1,0:T(8,128)(2,1)}, u32[]{:S(2)}, u32[]{:S(2)}) collective-permute-start(bf16[672,256]{1,0:T(8,128)(2,1)S(1)} %slice.13), channel_id=1, source_target_pairs={{0,8},{4,12},{8,0},{12,4},{16,24},{20,28},{24,16},{28,20},{1,9},{5... | collective-permute-start | bytes 1032200 | tf_op jit(solution)/shard_map/ppermute | solution.py:470
  81.0 13.4 %collective-permute-start.23 = (bf16[256,512]{1,0:T(8,128)(2,1)}, bf16[256,512]{1,0:T(8,128)(2,1)S(1)}, u32[]{:S(2)}, u32[]{:S(2)}) collective-permute-start(bf16[256,512]{1,0:T(8,128)(2,1)} %get-tuple-element.119), channel_id=1, source_target_pairs={{0,1},{1,0},{2,3},{3,2},{4,5},{5,4},{6,7},{7,6},{8,9},{9,8},{10,11... | collective-permute-start | bytes 786440 | tf_op jit(solution)/shard_map/ppermute | solution.py:770
  81.0 13.4 %collective-permute-start.24 = (bf16[256,256]{1,0:T(8,128)(2,1)}, bf16[256,256]{1,0:T(8,128)(2,1)S(1)}, u32[]{:S(2)}, u32[]{:S(2)}) collective-permute-start(bf16[256,256]{1,0:T(8,128)(2,1)} %get-tuple-element.120), channel_id=1, source_target_pairs={{0,1},{1,0},{2,3},{3,2},{4,5},{5,4},{6,7},{7,6},{8,9},{9,8},{10,11... | collective-permute-start | bytes 393224 | tf_op jit(solution)/shard_map/ppermute | solution.py:770
  83.0 16.7 %collective-permute-start.27 = (bf16[128,512]{1,0:T(8,128)(2,1)}, bf16[128,512]{1,0:T(8,128)(2,1)S(1)}, u32[]{:S(2)}, u32[]{:S(2)}) collective-permute-start(bf16[128,512]{1,0:T(8,128)(2,1)} %get-tuple-element.123.rest_10_), channel_id=1, source_target_pairs={{0,8},{4,12},{8,16},{12,20},{16,24},{20,28},{1,9},{5,13},{9,17},{1... | collective-permute-start | bytes 393224 | tf_op jit(solution)/shard_map/ppermute | solution.py:706
  86.4 13.3 %collective-permute-start.29 = (bf16[128,512]{1,0:T(8,128)(2,1)}, bf16[128,512]{1,0:T(8,128)(2,1)S(1)}, u32[]{:S(2)}, u32[]{:S(2)}) collective-permute-start(bf16[128,512]{1,0:T(8,128)(2,1)} %get-tuple-element.123.rest_10_), channel_id=1, source_target_pairs={{0,4},{4,8},{8,12},{12,16},{16,20},{20,24},{24,28},{1,5},{5,9},{9,... | collective-permute-start | bytes 393224 | tf_op jit(solution)/shard_map/ppermute | solution.py:706
  98.4 58.4 %collective-permute-start.36 = (bf16[128,5376]{1,0:T(8,128)(2,1)}, bf16[128,5376]{1,0:T(8,128)(2,1)}, u32[]{:S(2)}, u32[]{:S(2)}) collective-permute-start(bf16[128,5376]{1,0:T(8,128)(2,1)} %get-tuple-element.141), channel_id=1, source_target_pairs={{0,1},{1,0},{2,3},{3,2},{4,5},{5,4},{6,7},{7,6},{8,9},{9,8},{10,11... | collective-permute-start | bytes 4128776 | tf_op jit(solution)/shard_map/ppermute | solution.py:770
  111.8 12.9 %collective-permute-start.30 = (bf16[512,256]{1,0:T(8,128)(2,1)}, bf16[512,256]{1,0:T(8,128)(2,1)S(1)}, u32[]{:S(2)}, u32[]{:S(2)}) collective-permute-start(bf16[512,256]{1,0:T(8,128)(2,1)} %get-tuple-element.125), channel_id=1, source_target_pairs={{8,0},{12,4},{16,8},{20,12},{24,16},{28,20},{9,1},{13,5},{17,9},{2... | collective-permute-start | bytes 786440 | tf_op jit(solution)/shard_map/ppermute | solution.py:716
  113.1 11.6 %collective-permute-start.31 = (bf16[512,256]{1,0:T(8,128)(2,1)}, bf16[512,256]{1,0:T(8,128)(2,1)S(1)}, u32[]{:S(2)}, u32[]{:S(2)}) collective-permute-start(bf16[512,256]{1,0:T(8,128)(2,1)} %get-tuple-element.126), channel_id=1, source_target_pairs={{4,0},{8,4},{12,8},{16,12},{20,16},{24,20},{28,24},{5,1},{9,5},{13... | collective-permute-start | bytes 786440 | tf_op jit(solution)/shard_map/ppermute | solution.py:716
  121.9 14.2 %collective-permute-start.33 = (bf16[512,256]{1,0:T(8,128)(2,1)}, bf16[512,256]{1,0:T(8,128)(2,1)S(1)}, u32[]{:S(2)}, u32[]{:S(2)}) collective-permute-start(bf16[512,256]{1,0:T(8,128)(2,1)} %get-tuple-element.133), channel_id=1, source_target_pairs={{8,0},{12,4},{16,8},{20,12},{24,16},{28,20},{9,1},{13,5},{17,9},{2... | collective-permute-start | bytes 786440 | tf_op jit(solution)/shard_map/ppermute | solution.py:716
  123.2 12.9 %collective-permute-start.34 = (bf16[512,256]{1,0:T(8,128)(2,1)}, bf16[512,256]{1,0:T(8,128)(2,1)}, u32[]{:S(2)}, u32[]{:S(2)}) collective-permute-start(bf16[512,256]{1,0:T(8,128)(2,1)} %get-tuple-element.134), channel_id=1, source_target_pairs={{4,0},{8,4},{12,8},{16,12},{20,16},{24,20},{28,24},{5,1},{9,5},{13... | collective-permute-start | bytes 786440 | tf_op jit(solution)/shard_map/ppermute | solution.py:716
  154.9 63.8 %collective-permute-start.37 = (bf16[128,5376]{1,0:T(8,128)(2,1)}, bf16[128,5376]{1,0:T(8,128)(2,1)}, u32[]{:S(2)}, u32[]{:S(2)}) collective-permute-start(bf16[128,5376]{1,0:T(8,128)(2,1)} %get-tuple-element.138), channel_id=1, source_target_pairs={{0,2},{1,3},{2,0},{3,1},{4,6},{5,7},{6,4},{7,5},{8,10},{9,11},{10,... | collective-permute-start | bytes 4128776 | tf_op jit(solution)/shard_map/ppermute | solution.py:770
  169.2 12.9 %collective-permute-start.5 = (bf16[4,672,256]{2,1,0:T(8,128)(2,1)}, bf16[4,672,256]{2,1,0:T(8,128)(2,1)S(1)}, u32[]{:S(2)}, u32[]{:S(2)}) collective-permute-start(bf16[4,672,256]{2,1,0:T(8,128)(2,1)} %get-tuple-element.273), channel_id=1, source_target_pairs={{0,4},{4,0},{8,12},{12,8},{16,20},{20,16},{24,28},{28,24},{1,5},{5... | collective-permute-start | bytes 4128776 | tf_op jit(solution)/shard_map/while/body/ppermute | solution.py:470
  174.0 13.6 %collective-permute-start.1 = (bf16[2,672,128]{2,1,0:T(8,128)(2,1)S(1)}, bf16[2,672,128]{2,1,0:T(8,128)(2,1)S(1)}, u32[]{:S(2)}, u32[]{:S(2)}) collective-permute-start(bf16[2,672,128]{2,1,0:T(8,128)(2,1)S(1)} %get-tuple-element.266), channel_id=1, source_target_pairs={{0,8},{4,12},{8,0},{12,4},{16,24},{20,28},{24,16},{28,20},{1,9},{5... | collective-permute-start | bytes 1032200 | tf_op jit(solution)/shard_map/while/body/ppermute | solution.py:470
  178.7 12.3 %collective-permute-start.2 = (bf16[2,672,128]{2,1,0:T(8,128)(2,1)S(1)}, bf16[2,672,128]{2,1,0:T(8,128)(2,1)S(1)}, u32[]{:S(2)}, u32[]{:S(2)}) collective-permute-start(bf16[2,672,128]{2,1,0:T(8,128)(2,1)S(1)} %get-tuple-element.267), channel_id=1, source_target_pairs={{0,16},{4,20},{8,24},{12,28},{16,0},{20,4},{24,8},{28,12},{1,17},{... | collective-permute-start | bytes 1032200 | tf_op jit(solution)/shard_map/while/body/ppermute | solution.py:470
  183.4 11.3 %collective-permute-start.6 = (bf16[2,672,128]{2,1,0:T(8,128)(2,1)S(1)}, bf16[2,672,128]{2,1,0:T(8,128)(2,1)S(1)}, u32[]{:S(2)}, u32[]{:S(2)}) collective-permute-start(bf16[2,672,128]{2,1,0:T(8,128)(2,1)S(1)} %get-tuple-element.276), channel_id=1, source_target_pairs={{0,8},{4,12},{8,0},{12,4},{16,24},{20,28},{24,16},{28,20},{1,9},{5... | collective-permute-start | bytes 1032200 | tf_op jit(solution)/shard_map/while/body/ppermute | solution.py:470
  183.5 14.7 %collective-permute-start.7 = (bf16[2,672,128]{2,1,0:T(8,128)(2,1)S(1)}, bf16[2,672,128]{2,1,0:T(8,128)(2,1)S(1)}, u32[]{:S(2)}, u32[]{:S(2)}) collective-permute-start(bf16[2,672,128]{2,1,0:T(8,128)(2,1)S(1)} %get-tuple-element.277), channel_id=1, source_target_pairs={{0,16},{4,20},{8,24},{12,28},{16,0},{20,4},{24,8},{28,12},{1,17},{... | collective-permute-start | bytes 1032200 | tf_op jit(solution)/shard_map/while/body/ppermute | solution.py:470
  191.8 10.0 %collective-permute-start.3 = (bf16[1,672,128]{2,1,0:T(8,128)(2,1)S(1)}, bf16[1,672,128]{2,1,0:T(8,128)(2,1)S(1)}, u32[]{:S(2)}, u32[]{:S(2)}) collective-permute-start(bf16[1,672,128]{2,1,0:T(8,128)(2,1)S(1)} %get-tuple-element.270), channel_id=1, source_target_pairs={{0,16},{4,20},{8,24},{12,28},{16,0},{20,4},{24,8},{28,12},{1,17},{... | collective-permute-start | bytes 516104 | tf_op jit(solution)/shard_map/while/body/ppermute | solution.py:470
  (37 other events, 230.7 us)

commit v6 on v5

--- a/solution.py
+++ b/solution.py
@@ -171,6 +171,15 @@
         compiler_params=params(63),
         cost_estimate=cost(4 * rows * width * cols, blocks[0], w_key, w_value, *outs),
     )(info, *dense, w_key, w_value, *blocks)
+
+
+def cut_copies(source, target, first, rows, parts, sems, low):
+    size = rows // parts
+    copies = []
+    for part in range(parts):
+        span = pl.ds(pl.multiple_of(first + part * size, 16), size)
+        copies.append(pltpu.make_async_copy(source.at[span, :], target.at[span, :], sems.at[low + part]))
+    return copies
 
 
 def project_pair_body(places, info, gain, k_gain, cosine, sine, w_key, w_value, ready, block, *rest):
@@ -563,11 +572,10 @@
     for number in range(2):
         span = pl.ds(pl.multiple_of(jnp.bitwise_xor(first, number) * half, 128), half)
         spans.append(span)
+        low = jnp.bitwise_xor(first, number) * half
         groups.append(
-            [
-                pltpu.make_async_copy(w_key.at[span, :], key_held.at[span, :], own_sems.at[2 * number]),
-                pltpu.make_async_copy(w_value.at[span, :], value_held.at[span, :], own_sems.at[2 * number + 1]),
-            ]
+            cut_copies(w_key, key_held, low, half, 4, own_sems, 8 * number)
+            + cut_copies(w_value, value_held, low, half, 4, own_sems, 8 * number + 4)
             + [copy for copy, (offset, _) in zip(copies, places) if offset // split == number]
         )
         start_all(groups[number])
@@ -611,7 +619,7 @@
             pltpu.VMEM((width, cols), jnp.bfloat16),
             pltpu.VMEM((width, cols), jnp.bfloat16),
             pltpu.VMEM((width, 2 * cols), jnp.bfloat16),
-            pltpu.SemaphoreType.DMA((4,)),
+            pltpu.SemaphoreType.DMA((16,)),
             pltpu.SemaphoreType.DMA((len(arrays),)),
         ],
         compiler_params=params(63),

time: 226 us -> 226 us (level)
  no operation moved by 1% of the time
where the time goes in v6:
time: 226 us; the launch traced here: 223 us
  waiting for transfers between devices  91.2 us (40%)
  Pallas kernels  64.7 us (29%)
  starting transfers between devices  49.9 us (22%)
  local copies, waits for them, and re-layouts  10.7 us (5%)
  other arithmetic  4.99 us (2%)
    ppermute x9, waiting for transfers between devices, trade(): lax.ppermute(array, 'tp', [(i, i ^ distance) for i in range(lax.axis_size...  49.8 us
    ppermute x19, waiting for transfers between devices, swap(): return lax.ppermute(array, 'seq', [(i, i ^ 1 << bit) for i in range(size)])  33.1 us
    ppermute x19, starting transfers between devices, swap(): return lax.ppermute(array, 'seq', [(i, i ^ 1 << bit) for i in range(size)])  21.4 us
    pallas_call x2, Pallas kernels, attend(): pl.pallas_call(functools.partial(attend_body, reach, slots), name='attend...  14.9 us
    ppermute x6, starting transfers between devices, halo_of(): sent.append(lax.ppermute(key_value, 'seq', pairs))  13.4 us
    ppermute x9, starting transfers between devices, trade(): lax.ppermute(array, 'tp', [(i, i ^ distance) for i in range(lax.axis_size...  9.73 us
    pallas_call x2, Pallas kernels, weight_terms(): pl.pallas_call(functools.partial(weight_body, len(blocks)), name='weight_...  9.53 us
    pallas_call x1, Pallas kernels, pair_terms(): pl.pallas_call(functools.partial(pair_body, places, heads), name='pair_te...  9.02 us
  transfers between devices with their start and end apart: 38, of which 18 were waited for; matrix products, arithmetic and copies ran while one was open for 4% of the time, Pallas kernels for 27%

profile of v6, /device:TPU:0, one launch (start us, length us, event | category | flops | bytes accessed | tf_op | source)
XLA Modules:
  0.0 222.7 jit_solution(15056321690215374997)
XLA Ops:
  11.0 6.2 %project_block.1 = (bf16[128,512]{1,0:T(8,128)(2,1)}, bf16[128,256]{1,0:T(8,128)(2,1)}, bf16[128,5376]{1,0:T(8,128)(2,1)}) custom-call(s32[2]{0:T(128)} %pad_add_fusion.4.info, f32[1,5376]{1,0:T(1,128)} %broadcast_in_dim.35.gain, f32[1,128]{1,0:T(1,128)} %bitcast.21, f32[512,128]{1,0:T(8,128)} %get-tuple-element.172.cosine, ...), custom_call_target="tpu_custom_call" | custom-call | flops 704643072 | bytes 8454144 | tf_op jit(solution)/shard_map/project_block/pallas_call | solution.py:163
  17.2 3.4 %collective-permute-start.10 = (bf16[128,512]{1,0:T(8,128)(2,1)}, bf16[128,512]{1,0:T(8,128)(2,1)S(1)}, u32[]{:S(2)}, u32[]{:S(2)}) collective-permute-start(bf16[128,512]{1,0:T(8,128)(2,1)} %get-tuple-element.114.rest_8_), channel_id=1, source_target_pairs={{0,8},{4,12},{8,16},{12,20},{16,24},{20,28},{1,9},{5,13},{9,17},{1... | collective-permute-start | bytes 393224 | tf_op jit(solution)/shard_map/ppermute | solution.py:714
  23.4 11.5 %collective-permute-done.12.rest_0_.rest_4_ = bf16[672,512]{1,0:T(8,128)(2,1)} collective-permute-done((bf16[672,512]{1,0:T(8,128)(2,1)S(1)}, bf16[672,512]{1,0:T(8,128)(2,1)}, u32[]{:S(2)}, u32[]{:S(2)}) %collective-permute-start.12) | collective-permute-done | bytes 688160 | tf_op jit(solution)/shard_map/ppermute | solution.py:778
  38.1 13.6 %collective-permute-done.14.rest_1_.rest_5_ = bf16[672,512]{1,0:T(8,128)(2,1)S(1)} collective-permute-done((bf16[672,512]{1,0:T(8,128)(2,1)}, bf16[672,512]{1,0:T(8,128)(2,1)S(1)}, u32[]{:S(2)}, u32[]{:S(2)}) %collective-permute-start.14) | collective-permute-done | bytes 688160 | tf_op jit(solution)/shard_map/ppermute | solution.py:479
  54.8 12.7 %collective-permute-done.11.block = bf16[128,5376]{1,0:T(8,128)(2,1)} collective-permute-done((bf16[128,5376]{1,0:T(8,128)(2,1)}, bf16[128,5376]{1,0:T(8,128)(2,1)}, u32[]{:S(2)}, u32[]{:S(2)}) %collective-permute-start.11) | collective-permute-done | bytes 1376288 | tf_op jit(solution)/shard_map/ppermute | solution.py:778
  72.6 8.3 %project_pair.1 = (bf16[128,512]{1,0:T(8,128)(2,1)}, bf16[128,256]{1,0:T(8,128)(2,1)}, bf16[128,5376]{1,0:T(8,128)(2,1)}, bf16[256,512]{1,0:T(8,128)(2,1)}, bf16[256,256]{1,0:T(8,128)(2,1)}) custom-call(s32[3]{0:T(128)} %pad_add_fusion.2.info, f32[1,5376]{1,0:T(1,128)} %broadcast_in_dim.35.gain, f32[1,128]{1,0:T(1,128)} %bitcast.22, ...), custom_call_target="tpu_custom_call" | custom-call | flops 2113929216 | bytes 14352384 | tf_op jit(solution)/shard_map/project_pair/pallas_call | solution.py:233
  83.0 3.4 %collective-permute-start.27 = (bf16[128,512]{1,0:T(8,128)(2,1)}, bf16[128,512]{1,0:T(8,128)(2,1)S(1)}, u32[]{:S(2)}, u32[]{:S(2)}) collective-permute-start(bf16[128,512]{1,0:T(8,128)(2,1)} %get-tuple-element.123.rest_10_), channel_id=1, source_target_pairs={{0,8},{4,12},{8,16},{12,20},{16,24},{20,28},{1,9},{5,13},{9,17},{1... | collective-permute-start | bytes 393224 | tf_op jit(solution)/shard_map/ppermute | solution.py:714
  87.8 6.6 %collective-permute-done.24.rest_3_.rest_5_ = bf16[256,256]{1,0:T(8,128)(2,1)S(1)} collective-permute-done((bf16[256,256]{1,0:T(8,128)(2,1)}, bf16[256,256]{1,0:T(8,128)(2,1)S(1)}, u32[]{:S(2)}, u32[]{:S(2)}) %collective-permute-start.24) | collective-permute-done | bytes 131104 | tf_op jit(solution)/shard_map/ppermute | solution.py:778
  99.8 3.8 %collective-permute-done.26.rest_1_.rest_3_ = bf16[256,512]{1,0:T(8,128)(2,1)S(1)} collective-permute-done((bf16[256,512]{1,0:T(8,128)(2,1)S(1)}, bf16[256,512]{1,0:T(8,128)(2,1)S(1)}, u32[]{:S(2)}, u32[]{:S(2)}) %collective-permute-start.26) | collective-permute-done | bytes 262176 | tf_op jit(solution)/shard_map/ppermute | solution.py:714
  104.4 7.4 %attend_head.2 = (bf16[512,256]{1,0:T(8,128)(2,1)}, f32[512,256]{1,0:T(8,128)}, bf16[512,256]{1,0:T(8,128)(2,1)}, bf16[512,256]{1,0:T(8,128)(2,1)}) custom-call(s32[4]{0:T(128)} %pad_add_fusion.3.info, s32[1,512]{1,0:T(1,128)} %maximum_subtract_fusion.lowest, f32[1,128]{1,0:T(1,128)} %bitcast.25, f32[512,128]{1,0:T(8,128)} %get-tuple-element.172.cosine, ...), custom_call_target="tpu_custom_call" | custom-call | flops 2013265920 | bytes 2359296 | tf_op jit(solution)/shard_map/attend_head/pallas_call | solution.py:333
  114.4 7.5 %attend_head.3 = (bf16[512,256]{1,0:T(8,128)(2,1)}, f32[512,256]{1,0:T(8,128)}, bf16[512,256]{1,0:T(8,128)(2,1)}, bf16[512,256]{1,0:T(8,128)(2,1)}) custom-call(s32[4]{0:T(128)} %pad_add_fusion.3.info, s32[1,512]{1,0:T(1,128)} %maximum_subtract_fusion.lowest, f32[1,128]{1,0:T(1,128)} %bitcast.26, f32[512,128]{1,0:T(8,128)} %get-tuple-element.172.cosine, ...), custom_call_target="tpu_custom_call" | custom-call | flops 2013265920 | bytes 2359296 | tf_op jit(solution)/shard_map/attend_head/pallas_call | solution.py:333
  128.1 5.0 %collective-permute-done.32.rest_2_ = bf16[256,256]{1,0:T(8,128)(2,1)S(1)} collective-permute-done((bf16[256,256]{1,0:T(8,128)(2,1)}, bf16[256,256]{1,0:T(8,128)(2,1)S(1)}, u32[]{:S(2)}, u32[]{:S(2)}) %collective-permute-start.32) | collective-permute-done | bytes 131104 | tf_op jit(solution)/shard_map/ppermute | solution.py:778
  141.3 3.5 %collective-permute-done.35.rest_3_ = bf16[256,256]{1,0:T(8,128)(2,1)S(1)} collective-permute-done((bf16[256,256]{1,0:T(8,128)(2,1)}, bf16[256,256]{1,0:T(8,128)(2,1)S(1)}, u32[]{:S(2)}, u32[]{:S(2)}) %collective-permute-start.35) | collective-permute-done | bytes 131104 | tf_op jit(solution)/shard_map/ppermute | solution.py:778
  145.5 9.0 %pair_terms.1 = (bf16[128,5376]{1,0:T(8,128)(2,1)}, bf16[128,5376]{1,0:T(8,128)(2,1)}) custom-call(s32[3]{0:T(128)} %pad_add_fusion.2.info, bf16[5376,256]{1,0:T(8,128)(2,1)} %w_key.5, bf16[5376,256]{1,0:T(8,128)(2,1)} %w_value.5, bf16[512,256]{1,0:T(8,128)(2,1)S(1)} %get-tuple-element.289.rest_0_, bf16[512,256]{1,0:T(8,128)(2,1)S(1)} %get-tuple-element.294.rest_1_, ...), custom_call_target="tpu_custom_call" | custom-call | flops 2818572288 | bytes 13762560 | tf_op jit(solution)/shard_map/pair_terms/pallas_call | solution.py:609
  158.2 49.7 %while.12 = (s32[]{:T(128)}, f32[672,256]{1,0:T(8,128)}, f32[672,256]{1,0:T(8,128)}, s32[]{:T(128)}, s32[5]{0:T(128)S(1)}, /*index=5*/bf16[512,256]{1,0:T(8,128)...) while((s32[]{:T(128)}, f32[672,256]{1,0:T(8,128)}, ...), condition=%wide.region_3.4_spmd, body=%wide.region_2.3_spmd.sunk | while | flops 18 | bytes 30278384 | solution.py:852
  158.2 4.8 %weight_terms.2 = (bf16[4,672,256]{2,1,0:T(8,128)(2,1)}, bf16[4,672,256]{2,1,0:T(8,128)(2,1)S(1)}) custom-call(s32[5]{0:T(128)S(1)} %broadcast_add_fusion.2.info, bf16[512,256]{1,0:T(8,128)(2,1)S(1)} %get-tuple-element.319.grads, bf16[128,5376]{1,0:T(8,128)(2,1)} %get-tuple-element.320.rest_0_, bf16[128,5376]{1,0:T(8,128)(2,1)} %get-tuple-element.321.rest_1_, ...), custom_call_target="tpu_custom_call" | custom-call | tf_op jit(solution)/shard_map/while/body/weight_terms/pallas_call | solution.py:421
  164.0 4.8 %weight_terms.3 = (bf16[4,672,256]{2,1,0:T(8,128)(2,1)}, bf16[4,672,256]{2,1,0:T(8,128)(2,1)S(1)}) custom-call(s32[5]{0:T(128)S(1)} %broadcast_add_fusion.2.info, bf16[512,256]{1,0:T(8,128)(2,1)S(1)} %get-tuple-element.324.grads, bf16[128,5376]{1,0:T(8,128)(2,1)} %get-tuple-element.320.rest_0_, bf16[128,5376]{1,0:T(8,128)(2,1)} %get-tuple-element.321.rest_1_, ...), custom_call_target="tpu_custom_call" | custom-call | tf_op jit(solution)/shard_map/while/body/weight_terms/pallas_call | solution.py:421
  173.5 4.7 %collective-permute-start.1 = (bf16[2,672,128]{2,1,0:T(8,128)(2,1)S(1)}, bf16[2,672,128]{2,1,0:T(8,128)(2,1)S(1)}, u32[]{:S(2)}, u32[]{:S(2)}) collective-permute-start(bf16[2,672,128]{2,1,0:T(8,128)(2,1)S(1)} %get-tuple-element.266), channel_id=1, source_target_pairs={{0,8},{4,12},{8,0},{12,4},{16,24},{20,28},{24,16},{28,20},{1,9},{5... | collective-permute-start | bytes 1032200 | tf_op jit(solution)/shard_map/while/body/ppermute | solution.py:479
  178.2 3.4 %collective-permute-start.2 = (bf16[2,672,128]{2,1,0:T(8,128)(2,1)S(1)}, bf16[2,672,128]{2,1,0:T(8,128)(2,1)S(1)}, u32[]{:S(2)}, u32[]{:S(2)}) collective-permute-start(bf16[2,672,128]{2,1,0:T(8,128)(2,1)S(1)} %get-tuple-element.267), channel_id=1, source_target_pairs={{0,16},{4,20},{8,24},{12,28},{16,0},{20,4},{24,8},{28,12},{1,17},{... | collective-permute-start | bytes 1032200 | tf_op jit(solution)/shard_map/while/body/ppermute | solution.py:479
  183.2 3.9 %collective-permute-done.1.rest_2_ = bf16[2,672,128]{2,1,0:T(8,128)(2,1)S(1)} collective-permute-done((bf16[2,672,128]{2,1,0:T(8,128)(2,1)S(1)}, bf16[2,672,128]{2,1,0:T(8,128)(2,1)S(1)}, u32[]{:S(2)}, u32[]{:S(2)}) %collective-permute-start.1) | collective-permute-done | bytes 344096 | tf_op jit(solution)/shard_map/while/body/ppermute | solution.py:479
  194.3 3.5 %collective-permute-done.7.rest_3_ = bf16[2,672,128]{2,1,0:T(8,128)(2,1)S(1)} collective-permute-done((bf16[2,672,128]{2,1,0:T(8,128)(2,1)S(1)}, bf16[2,672,128]{2,1,0:T(8,128)(2,1)S(1)}, u32[]{:S(2)}, u32[]{:S(2)}) %collective-permute-start.7) | collective-permute-done | bytes 344096 | tf_op jit(solution)/shard_map/while/body/ppermute | solution.py:479
  201.4 3.4 %collective-permute-done.8.rest_6_ = bf16[1,672,128]{2,1,0:T(8,128)(2,1)S(1)} collective-permute-done((bf16[1,672,128]{2,1,0:T(8,128)(2,1)S(1)}, bf16[1,672,128]{2,1,0:T(8,128)(2,1)S(1)}, u32[]{:S(2)}, u32[]{:S(2)}) %collective-permute-start.8) | collective-permute-done | bytes 172064 | tf_op jit(solution)/shard_map/while/body/ppermute | solution.py:479
  207.9 10.4 %collective-permute-done.37.rest_1_ = bf16[128,5376]{1,0:T(8,128)(2,1)} collective-permute-done((bf16[128,5376]{1,0:T(8,128)(2,1)}, bf16[128,5376]{1,0:T(8,128)(2,1)}, u32[]{:S(2)}, u32[]{:S(2)}) %collective-permute-start.37) | collective-permute-done | bytes 1376288 | tf_op jit(solution)/shard_map/ppermute | solution.py:778
  218.3 4.3 %input_grad.1 = bf16[128,5376]{1,0:T(8,128)(2,1)} custom-call(bf16[128,5376]{1,0:T(8,128)(2,1)} %tokens.1, f32[1,5376]{1,0:T(1,128)} %broadcast_in_dim.35.gain, bf16[128,5376]{1,0:T(8,128)(2,1)} %get-tuple-element.146.rest_0_, bf16[128,5376]{1,0:T(8,128)(2,1)} %collective-permute-done.37.rest_1_), custom_call_target="tpu_custom_call" | custom-call | bytes 5505024 | tf_op jit(solution)/shard_map/input_grad/pallas_call | solution.py:664
  (139 shorter events, 76.3 us)
Async XLA Ops:
  1.9 33.0 %collective-permute-start.12 = (bf16[672,512]{1,0:T(8,128)(2,1)S(1)}, bf16[672,512]{1,0:T(8,128)(2,1)}, u32[]{:S(2)}, u32[]{:S(2)}) collective-permute-start(bf16[672,512]{1,0:T(8,128)(2,1)S(1)} %pad_maximum_fusion), channel_id=1, source_target_pairs={{0,1},{1,0},{2,3},{3,2},{4,5},{5,4},{6,7},{7,6},{8,9},{9,8},{10,11... | collective-permute-start | bytes 2064392 | tf_op jit(solution)/shard_map/ppermute | solution.py:778
  4.9 62.5 %collective-permute-start.11 = (bf16[128,5376]{1,0:T(8,128)(2,1)}, bf16[128,5376]{1,0:T(8,128)(2,1)}, u32[]{:S(2)}, u32[]{:S(2)}) collective-permute-start(bf16[128,5376]{1,0:T(8,128)(2,1)} %tokens.1), channel_id=1, source_target_pairs={{0,2},{1,3},{2,0},{3,1},{4,6},{5,7},{6,4},{7,5},{8,10},{9,11},{10,... | collective-permute-start | bytes 4128776 | tf_op jit(solution)/shard_map/ppermute | solution.py:778
  34.9 16.8 %collective-permute-start.14 = (bf16[672,512]{1,0:T(8,128)(2,1)}, bf16[672,512]{1,0:T(8,128)(2,1)S(1)}, u32[]{:S(2)}, u32[]{:S(2)}) collective-permute-start(bf16[672,512]{1,0:T(8,128)(2,1)} %collective-permute-done.12.rest_0_.rest_4_), channel_id=1, source_target_pairs={{0,8},{4,12},{8,0},{12,4},{16,24},{20,28},{24,16},{28,20},{1,9},{5... | collective-permute-start | bytes 2064392 | tf_op jit(solution)/shard_map/ppermute | solution.py:479
  36.6 16.6 %collective-permute-start.15 = (bf16[672,512]{1,0:T(8,128)(2,1)}, bf16[672,512]{1,0:T(8,128)(2,1)S(1)}, u32[]{:S(2)}, u32[]{:S(2)}) collective-permute-start(bf16[672,512]{1,0:T(8,128)(2,1)} %collective-permute-done.12.rest_0_.rest_4_), channel_id=1, source_target_pairs={{0,16},{4,20},{8,24},{12,28},{16,0},{20,4},{24,8},{28,12},{1,17},{... | collective-permute-start | bytes 2064392 | tf_op jit(solution)/shard_map/ppermute | solution.py:479
  38.1 29.4 %collective-permute-start.18 = (bf16[672,512]{1,0:T(8,128)(2,1)}, bf16[672,512]{1,0:T(8,128)(2,1)S(1)}, u32[]{:S(2)}, u32[]{:S(2)}) collective-permute-start(bf16[672,512]{1,0:T(8,128)(2,1)} %collective-permute-done.12.rest_0_.rest_4_), channel_id=1, source_target_pairs={{0,4},{4,0},{8,12},{12,8},{16,20},{20,16},{24,28},{28,24},{1,5},{5... | collective-permute-start | bytes 2064392 | tf_op jit(solution)/shard_map/ppermute | solution.py:479
  38.1 49.7 %collective-permute-start.25 = (bf16[128,5376]{1,0:T(8,128)(2,1)}, bf16[128,5376]{1,0:T(8,128)(2,1)}, u32[]{:S(2)}, u32[]{:S(2)}) collective-permute-start(bf16[128,5376]{1,0:T(8,128)(2,1)} %get-tuple-element.121.ready), channel_id=1, source_target_pairs={{0,1},{1,0},{2,3},{3,2},{4,5},{5,4},{6,7},{7,6},{8,9},{9,8},{10,11... | collective-permute-start | bytes 4128776 | tf_op jit(solution)/shard_map/ppermute | solution.py:778
  51.8 16.2 %collective-permute-start.16 = (bf16[672,256]{1,0:T(8,128)(2,1)S(1)}, bf16[672,256]{1,0:T(8,128)(2,1)S(1)}, u32[]{:S(2)}, u32[]{:S(2)}) collective-permute-start(bf16[672,256]{1,0:T(8,128)(2,1)S(1)} %slice.12), channel_id=1, source_target_pairs={{0,16},{4,20},{8,24},{12,28},{16,0},{20,4},{24,8},{28,12},{1,17},{... | collective-permute-start | bytes 1032200 | tf_op jit(solution)/shard_map/ppermute | solution.py:479
  53.2 14.8 %collective-permute-start.17 = (bf16[672,256]{1,0:T(8,128)(2,1)S(1)}, bf16[672,256]{1,0:T(8,128)(2,1)}, u32[]{:S(2)}, u32[]{:S(2)}) collective-permute-start(bf16[672,256]{1,0:T(8,128)(2,1)S(1)} %slice.13), channel_id=1, source_target_pairs={{0,8},{4,12},{8,0},{12,4},{16,24},{20,28},{24,16},{28,20},{1,9},{5... | collective-permute-start | bytes 1032200 | tf_op jit(solution)/shard_map/ppermute | solution.py:479
  81.0 13.4 %collective-permute-start.23 = (bf16[256,512]{1,0:T(8,128)(2,1)}, bf16[256,512]{1,0:T(8,128)(2,1)S(1)}, u32[]{:S(2)}, u32[]{:S(2)}) collective-permute-start(bf16[256,512]{1,0:T(8,128)(2,1)} %get-tuple-element.119), channel_id=1, source_target_pairs={{0,1},{1,0},{2,3},{3,2},{4,5},{5,4},{6,7},{7,6},{8,9},{9,8},{10,11... | collective-permute-start | bytes 786440 | tf_op jit(solution)/shard_map/ppermute | solution.py:778
  81.0 13.4 %collective-permute-start.24 = (bf16[256,256]{1,0:T(8,128)(2,1)}, bf16[256,256]{1,0:T(8,128)(2,1)S(1)}, u32[]{:S(2)}, u32[]{:S(2)}) collective-permute-start(bf16[256,256]{1,0:T(8,128)(2,1)} %get-tuple-element.120), channel_id=1, source_target_pairs={{0,1},{1,0},{2,3},{3,2},{4,5},{5,4},{6,7},{7,6},{8,9},{9,8},{10,11... | collective-permute-start | bytes 393224 | tf_op jit(solution)/shard_map/ppermute | solution.py:778
  83.0 16.7 %collective-permute-start.27 = (bf16[128,512]{1,0:T(8,128)(2,1)}, bf16[128,512]{1,0:T(8,128)(2,1)S(1)}, u32[]{:S(2)}, u32[]{:S(2)}) collective-permute-start(bf16[128,512]{1,0:T(8,128)(2,1)} %get-tuple-element.123.rest_10_), channel_id=1, source_target_pairs={{0,8},{4,12},{8,16},{12,20},{16,24},{20,28},{1,9},{5,13},{9,17},{1... | collective-permute-start | bytes 393224 | tf_op jit(solution)/shard_map/ppermute | solution.py:714
  86.4 13.3 %collective-permute-start.29 = (bf16[128,512]{1,0:T(8,128)(2,1)}, bf16[128,512]{1,0:T(8,128)(2,1)S(1)}, u32[]{:S(2)}, u32[]{:S(2)}) collective-permute-start(bf16[128,512]{1,0:T(8,128)(2,1)} %get-tuple-element.123.rest_10_), channel_id=1, source_target_pairs={{0,4},{4,8},{8,12},{12,16},{16,20},{20,24},{24,28},{1,5},{5,9},{9,... | collective-permute-start | bytes 393224 | tf_op jit(solution)/shard_map/ppermute | solution.py:714
  98.4 58.0 %collective-permute-start.36 = (bf16[128,5376]{1,0:T(8,128)(2,1)}, bf16[128,5376]{1,0:T(8,128)(2,1)}, u32[]{:S(2)}, u32[]{:S(2)}) collective-permute-start(bf16[128,5376]{1,0:T(8,128)(2,1)} %get-tuple-element.141), channel_id=1, source_target_pairs={{0,1},{1,0},{2,3},{3,2},{4,5},{5,4},{6,7},{7,6},{8,9},{9,8},{10,11... | collective-permute-start | bytes 4128776 | tf_op jit(solution)/shard_map/ppermute | solution.py:778
  111.8 12.9 %collective-permute-start.30 = (bf16[512,256]{1,0:T(8,128)(2,1)}, bf16[512,256]{1,0:T(8,128)(2,1)S(1)}, u32[]{:S(2)}, u32[]{:S(2)}) collective-permute-start(bf16[512,256]{1,0:T(8,128)(2,1)} %get-tuple-element.125), channel_id=1, source_target_pairs={{8,0},{12,4},{16,8},{20,12},{24,16},{28,20},{9,1},{13,5},{17,9},{2... | collective-permute-start | bytes 786440 | tf_op jit(solution)/shard_map/ppermute | solution.py:724
  113.1 11.6 %collective-permute-start.31 = (bf16[512,256]{1,0:T(8,128)(2,1)}, bf16[512,256]{1,0:T(8,128)(2,1)S(1)}, u32[]{:S(2)}, u32[]{:S(2)}) collective-permute-start(bf16[512,256]{1,0:T(8,128)(2,1)} %get-tuple-element.126), channel_id=1, source_target_pairs={{4,0},{8,4},{12,8},{16,12},{20,16},{24,20},{28,24},{5,1},{9,5},{13... | collective-permute-start | bytes 786440 | tf_op jit(solution)/shard_map/ppermute | solution.py:724
  121.9 14.2 %collective-permute-start.33 = (bf16[512,256]{1,0:T(8,128)(2,1)}, bf16[512,256]{1,0:T(8,128)(2,1)S(1)}, u32[]{:S(2)}, u32[]{:S(2)}) collective-permute-start(bf16[512,256]{1,0:T(8,128)(2,1)} %get-tuple-element.133), channel_id=1, source_target_pairs={{8,0},{12,4},{16,8},{20,12},{24,16},{28,20},{9,1},{13,5},{17,9},{2... | collective-permute-start | bytes 786440 | tf_op jit(solution)/shard_map/ppermute | solution.py:724
  123.2 12.9 %collective-permute-start.34 = (bf16[512,256]{1,0:T(8,128)(2,1)}, bf16[512,256]{1,0:T(8,128)(2,1)}, u32[]{:S(2)}, u32[]{:S(2)}) collective-permute-start(bf16[512,256]{1,0:T(8,128)(2,1)} %get-tuple-element.134), channel_id=1, source_target_pairs={{4,0},{8,4},{12,8},{16,12},{20,16},{24,20},{28,24},{5,1},{9,5},{13... | collective-permute-start | bytes 786440 | tf_op jit(solution)/shard_map/ppermute | solution.py:724
  154.5 63.8 %collective-permute-start.37 = (bf16[128,5376]{1,0:T(8,128)(2,1)}, bf16[128,5376]{1,0:T(8,128)(2,1)}, u32[]{:S(2)}, u32[]{:S(2)}) collective-permute-start(bf16[128,5376]{1,0:T(8,128)(2,1)} %get-tuple-element.138), channel_id=1, source_target_pairs={{0,2},{1,3},{2,0},{3,1},{4,6},{5,7},{6,4},{7,5},{8,10},{9,11},{10,... | collective-permute-start | bytes 4128776 | tf_op jit(solution)/shard_map/ppermute | solution.py:778
  168.8 12.9 %collective-permute-start.5 = (bf16[4,672,256]{2,1,0:T(8,128)(2,1)}, bf16[4,672,256]{2,1,0:T(8,128)(2,1)S(1)}, u32[]{:S(2)}, u32[]{:S(2)}) collective-permute-start(bf16[4,672,256]{2,1,0:T(8,128)(2,1)} %get-tuple-element.273), channel_id=1, source_target_pairs={{0,4},{4,0},{8,12},{12,8},{16,20},{20,16},{24,28},{28,24},{1,5},{5... | collective-permute-start | bytes 4128776 | tf_op jit(solution)/shard_map/while/body/ppermute | solution.py:479
  173.5 13.6 %collective-permute-start.1 = (bf16[2,672,128]{2,1,0:T(8,128)(2,1)S(1)}, bf16[2,672,128]{2,1,0:T(8,128)(2,1)S(1)}, u32[]{:S(2)}, u32[]{:S(2)}) collective-permute-start(bf16[2,672,128]{2,1,0:T(8,128)(2,1)S(1)} %get-tuple-element.266), channel_id=1, source_target_pairs={{0,8},{4,12},{8,0},{12,4},{16,24},{20,28},{24,16},{28,20},{1,9},{5... | collective-permute-start | bytes 1032200 | tf_op jit(solution)/shard_map/while/body/ppermute | solution.py:479
  178.2 12.3 %collective-permute-start.2 = (bf16[2,672,128]{2,1,0:T(8,128)(2,1)S(1)}, bf16[2,672,128]{2,1,0:T(8,128)(2,1)S(1)}, u32[]{:S(2)}, u32[]{:S(2)}) collective-permute-start(bf16[2,672,128]{2,1,0:T(8,128)(2,1)S(1)} %get-tuple-element.267), channel_id=1, source_target_pairs={{0,16},{4,20},{8,24},{12,28},{16,0},{20,4},{24,8},{28,12},{1,17},{... | collective-permute-start | bytes 1032200 | tf_op jit(solution)/shard_map/while/body/ppermute | solution.py:479
  183.0 11.3 %collective-permute-start.6 = (bf16[2,672,128]{2,1,0:T(8,128)(2,1)S(1)}, bf16[2,672,128]{2,1,0:T(8,128)(2,1)S(1)}, u32[]{:S(2)}, u32[]{:S(2)}) collective-permute-start(bf16[2,672,128]{2,1,0:T(8,128)(2,1)S(1)} %get-tuple-element.276), channel_id=1, source_target_pairs={{0,8},{4,12},{8,0},{12,4},{16,24},{20,28},{24,16},{28,20},{1,9},{5... | collective-permute-start | bytes 1032200 | tf_op jit(solution)/shard_map/while/body/ppermute | solution.py:479
  183.1 14.7 %collective-permute-start.7 = (bf16[2,672,128]{2,1,0:T(8,128)(2,1)S(1)}, bf16[2,672,128]{2,1,0:T(8,128)(2,1)S(1)}, u32[]{:S(2)}, u32[]{:S(2)}) collective-permute-start(bf16[2,672,128]{2,1,0:T(8,128)(2,1)S(1)} %get-tuple-element.277), channel_id=1, source_target_pairs={{0,16},{4,20},{8,24},{12,28},{16,0},{20,4},{24,8},{28,12},{1,17},{... | collective-permute-start | bytes 1032200 | tf_op jit(solution)/shard_map/while/body/ppermute | solution.py:479
  191.4 10.0 %collective-permute-start.3 = (bf16[1,672,128]{2,1,0:T(8,128)(2,1)S(1)}, bf16[1,672,128]{2,1,0:T(8,128)(2,1)S(1)}, u32[]{:S(2)}, u32[]{:S(2)}) collective-permute-start(bf16[1,672,128]{2,1,0:T(8,128)(2,1)S(1)} %get-tuple-element.270), channel_id=1, source_target_pairs={{0,16},{4,20},{8,24},{12,28},{16,0},{20,4},{24,8},{28,12},{1,17},{... | collective-permute-start | bytes 516104 | tf_op jit(solution)/shard_map/while/body/ppermute | solution.py:479
  (37 other events, 230.7 us)

commit v7 on v6

--- a/solution.py
+++ b/solution.py
@@ -574,8 +574,8 @@
         spans.append(span)
         low = jnp.bitwise_xor(first, number) * half
         groups.append(
-            cut_copies(w_key, key_held, low, half, 4, own_sems, 8 * number)
-            + cut_copies(w_value, value_held, low, half, 4, own_sems, 8 * number + 4)
+            cut_copies(w_key, key_held, low, half, 8, own_sems, 16 * number)
+            + cut_copies(w_value, value_held, low, half, 8, own_sems, 16 * number + 8)
             + [copy for copy, (offset, _) in zip(copies, places) if offset // split == number]
         )
         start_all(groups[number])
@@ -619,7 +619,7 @@
             pltpu.VMEM((width, cols), jnp.bfloat16),
             pltpu.VMEM((width, cols), jnp.bfloat16),
             pltpu.VMEM((width, 2 * cols), jnp.bfloat16),
-            pltpu.SemaphoreType.DMA((16,)),
+            pltpu.SemaphoreType.DMA((32,)),
             pltpu.SemaphoreType.DMA((len(arrays),)),
         ],
         compiler_params=params(63),

time: 226 us -> 227 us (level)
  no operation moved by 1% of the time
where the time goes in v7:
time: 227 us; the launch traced here: 223 us
  waiting for transfers between devices  91.1 us (40%)
  Pallas kernels  65.4 us (29%)
  starting transfers between devices  49.9 us (22%)
  local copies, waits for them, and re-layouts  10.7 us (5%)
  other arithmetic  4.99 us (2%)
    ppermute x9, waiting for transfers between devices, trade(): lax.ppermute(array, 'tp', [(i, i ^ distance) for i in range(lax.axis_size...  49.7 us
    ppermute x19, waiting for transfers between devices, swap(): return lax.ppermute(array, 'seq', [(i, i ^ 1 << bit) for i in range(size)])  33.1 us
    ppermute x19, starting transfers between devices, swap(): return lax.ppermute(array, 'seq', [(i, i ^ 1 << bit) for i in range(size)])  21.4 us
    pallas_call x2, Pallas kernels, attend(): pl.pallas_call(functools.partial(attend_body, reach, slots), name='attend...  14.9 us
    ppermute x6, starting transfers between devices, halo_of(): sent.append(lax.ppermute(key_value, 'seq', pairs))  13.4 us
    ppermute x9, starting transfers between devices, trade(): lax.ppermute(array, 'tp', [(i, i ^ distance) for i in range(lax.axis_size...  9.73 us
    pallas_call x1, Pallas kernels, pair_terms(): pl.pallas_call(functools.partial(pair_body, places, heads), name='pair_te...  9.67 us
    pallas_call x2, Pallas kernels, weight_terms(): pl.pallas_call(functools.partial(weight_body, len(blocks)), name='weight_...  9.53 us
  transfers between devices with their start and end apart: 38, of which 18 were waited for; matrix products, arithmetic and copies ran while one was open for 4% of the time, Pallas kernels for 27%

profile of v7, /device:TPU:0, one launch (start us, length us, event | category | flops | bytes accessed | tf_op | source)
XLA Modules:
  0.0 223.4 jit_solution(16117238140866083895)
XLA Ops:
  11.0 6.2 %project_block.1 = (bf16[128,512]{1,0:T(8,128)(2,1)}, bf16[128,256]{1,0:T(8,128)(2,1)}, bf16[128,5376]{1,0:T(8,128)(2,1)}) custom-call(s32[2]{0:T(128)} %pad_add_fusion.4.info, f32[1,5376]{1,0:T(1,128)} %broadcast_in_dim.35.gain, f32[1,128]{1,0:T(1,128)} %bitcast.21, f32[512,128]{1,0:T(8,128)} %get-tuple-element.172.cosine, ...), custom_call_target="tpu_custom_call" | custom-call | flops 704643072 | bytes 8454144 | tf_op jit(solution)/shard_map/project_block/pallas_call | solution.py:163
  17.2 3.4 %collective-permute-start.10 = (bf16[128,512]{1,0:T(8,128)(2,1)}, bf16[128,512]{1,0:T(8,128)(2,1)S(1)}, u32[]{:S(2)}, u32[]{:S(2)}) collective-permute-start(bf16[128,512]{1,0:T(8,128)(2,1)} %get-tuple-element.114.rest_8_), channel_id=1, source_target_pairs={{0,8},{4,12},{8,16},{12,20},{16,24},{20,28},{1,9},{5,13},{9,17},{1... | collective-permute-start | bytes 393224 | tf_op jit(solution)/shard_map/ppermute | solution.py:714
  23.4 11.5 %collective-permute-done.12.rest_0_.rest_4_ = bf16[672,512]{1,0:T(8,128)(2,1)} collective-permute-done((bf16[672,512]{1,0:T(8,128)(2,1)S(1)}, bf16[672,512]{1,0:T(8,128)(2,1)}, u32[]{:S(2)}, u32[]{:S(2)}) %collective-permute-start.12) | collective-permute-done | bytes 688160 | tf_op jit(solution)/shard_map/ppermute | solution.py:778
  38.1 13.6 %collective-permute-done.14.rest_1_.rest_5_ = bf16[672,512]{1,0:T(8,128)(2,1)S(1)} collective-permute-done((bf16[672,512]{1,0:T(8,128)(2,1)}, bf16[672,512]{1,0:T(8,128)(2,1)S(1)}, u32[]{:S(2)}, u32[]{:S(2)}) %collective-permute-start.14) | collective-permute-done | bytes 688160 | tf_op jit(solution)/shard_map/ppermute | solution.py:479
  54.8 12.7 %collective-permute-done.11.block = bf16[128,5376]{1,0:T(8,128)(2,1)} collective-permute-done((bf16[128,5376]{1,0:T(8,128)(2,1)}, bf16[128,5376]{1,0:T(8,128)(2,1)}, u32[]{:S(2)}, u32[]{:S(2)}) %collective-permute-start.11) | collective-permute-done | bytes 1376288 | tf_op jit(solution)/shard_map/ppermute | solution.py:778
  72.6 8.3 %project_pair.1 = (bf16[128,512]{1,0:T(8,128)(2,1)}, bf16[128,256]{1,0:T(8,128)(2,1)}, bf16[128,5376]{1,0:T(8,128)(2,1)}, bf16[256,512]{1,0:T(8,128)(2,1)}, bf16[256,256]{1,0:T(8,128)(2,1)}) custom-call(s32[3]{0:T(128)} %pad_add_fusion.2.info, f32[1,5376]{1,0:T(1,128)} %broadcast_in_dim.35.gain, f32[1,128]{1,0:T(1,128)} %bitcast.22, ...), custom_call_target="tpu_custom_call" | custom-call | flops 2113929216 | bytes 14352384 | tf_op jit(solution)/shard_map/project_pair/pallas_call | solution.py:233
  83.0 3.4 %collective-permute-start.27 = (bf16[128,512]{1,0:T(8,128)(2,1)}, bf16[128,512]{1,0:T(8,128)(2,1)S(1)}, u32[]{:S(2)}, u32[]{:S(2)}) collective-permute-start(bf16[128,512]{1,0:T(8,128)(2,1)} %get-tuple-element.123.rest_10_), channel_id=1, source_target_pairs={{0,8},{4,12},{8,16},{12,20},{16,24},{20,28},{1,9},{5,13},{9,17},{1... | collective-permute-start | bytes 393224 | tf_op jit(solution)/shard_map/ppermute | solution.py:714
  87.8 6.6 %collective-permute-done.24.rest_3_.rest_5_ = bf16[256,256]{1,0:T(8,128)(2,1)S(1)} collective-permute-done((bf16[256,256]{1,0:T(8,128)(2,1)}, bf16[256,256]{1,0:T(8,128)(2,1)S(1)}, u32[]{:S(2)}, u32[]{:S(2)}) %collective-permute-start.24) | collective-permute-done | bytes 131104 | tf_op jit(solution)/shard_map/ppermute | solution.py:778
  99.8 3.8 %collective-permute-done.26.rest_1_.rest_3_ = bf16[256,512]{1,0:T(8,128)(2,1)S(1)} collective-permute-done((bf16[256,512]{1,0:T(8,128)(2,1)S(1)}, bf16[256,512]{1,0:T(8,128)(2,1)S(1)}, u32[]{:S(2)}, u32[]{:S(2)}) %collective-permute-start.26) | collective-permute-done | bytes 262176 | tf_op jit(solution)/shard_map/ppermute | solution.py:714
  104.4 7.4 %attend_head.2 = (bf16[512,256]{1,0:T(8,128)(2,1)}, f32[512,256]{1,0:T(8,128)}, bf16[512,256]{1,0:T(8,128)(2,1)}, bf16[512,256]{1,0:T(8,128)(2,1)}) custom-call(s32[4]{0:T(128)} %pad_add_fusion.3.info, s32[1,512]{1,0:T(1,128)} %maximum_subtract_fusion.lowest, f32[1,128]{1,0:T(1,128)} %bitcast.25, f32[512,128]{1,0:T(8,128)} %get-tuple-element.172.cosine, ...), custom_call_target="tpu_custom_call" | custom-call | flops 2013265920 | bytes 2359296 | tf_op jit(solution)/shard_map/attend_head/pallas_call | solution.py:333
  114.4 7.5 %attend_head.3 = (bf16[512,256]{1,0:T(8,128)(2,1)}, f32[512,256]{1,0:T(8,128)}, bf16[512,256]{1,0:T(8,128)(2,1)}, bf16[512,256]{1,0:T(8,128)(2,1)}) custom-call(s32[4]{0:T(128)} %pad_add_fusion.3.info, s32[1,512]{1,0:T(1,128)} %maximum_subtract_fusion.lowest, f32[1,128]{1,0:T(1,128)} %bitcast.26, f32[512,128]{1,0:T(8,128)} %get-tuple-element.172.cosine, ...), custom_call_target="tpu_custom_call" | custom-call | flops 2013265920 | bytes 2359296 | tf_op jit(solution)/shard_map/attend_head/pallas_call | solution.py:333
  128.1 5.0 %collective-permute-done.32.rest_2_ = bf16[256,256]{1,0:T(8,128)(2,1)S(1)} collective-permute-done((bf16[256,256]{1,0:T(8,128)(2,1)}, bf16[256,256]{1,0:T(8,128)(2,1)S(1)}, u32[]{:S(2)}, u32[]{:S(2)}) %collective-permute-start.32) | collective-permute-done | bytes 131104 | tf_op jit(solution)/shard_map/ppermute | solution.py:778
  141.3 3.5 %collective-permute-done.35.rest_3_ = bf16[256,256]{1,0:T(8,128)(2,1)S(1)} collective-permute-done((bf16[256,256]{1,0:T(8,128)(2,1)}, bf16[256,256]{1,0:T(8,128)(2,1)S(1)}, u32[]{:S(2)}, u32[]{:S(2)}) %collective-permute-start.35) | collective-permute-done | bytes 131104 | tf_op jit(solution)/shard_map/ppermute | solution.py:778
  145.5 9.7 %pair_terms.1 = (bf16[128,5376]{1,0:T(8,128)(2,1)}, bf16[128,5376]{1,0:T(8,128)(2,1)}) custom-call(s32[3]{0:T(128)} %pad_add_fusion.2.info, bf16[5376,256]{1,0:T(8,128)(2,1)} %w_key.5, bf16[5376,256]{1,0:T(8,128)(2,1)} %w_value.5, bf16[512,256]{1,0:T(8,128)(2,1)S(1)} %get-tuple-element.289.rest_0_, bf16[512,256]{1,0:T(8,128)(2,1)S(1)} %get-tuple-element.294.rest_1_, ...), custom_call_target="tpu_custom_call" | custom-call | flops 2818572288 | bytes 13762560 | tf_op jit(solution)/shard_map/pair_terms/pallas_call | solution.py:609
  158.8 49.7 %while.12 = (s32[]{:T(128)}, f32[672,256]{1,0:T(8,128)}, f32[672,256]{1,0:T(8,128)}, s32[]{:T(128)}, s32[5]{0:T(128)S(1)}, /*index=5*/bf16[512,256]{1,0:T(8,128)...) while((s32[]{:T(128)}, f32[672,256]{1,0:T(8,128)}, ...), condition=%wide.region_3.4_spmd, body=%wide.region_2.3_spmd.sunk | while | flops 18 | bytes 30278384 | solution.py:852
  158.8 4.8 %weight_terms.2 = (bf16[4,672,256]{2,1,0:T(8,128)(2,1)}, bf16[4,672,256]{2,1,0:T(8,128)(2,1)S(1)}) custom-call(s32[5]{0:T(128)S(1)} %broadcast_add_fusion.2.info, bf16[512,256]{1,0:T(8,128)(2,1)S(1)} %get-tuple-element.319.grads, bf16[128,5376]{1,0:T(8,128)(2,1)} %get-tuple-element.320.rest_0_, bf16[128,5376]{1,0:T(8,128)(2,1)} %get-tuple-element.321.rest_1_, ...), custom_call_target="tpu_custom_call" | custom-call | tf_op jit(solution)/shard_map/while/body/weight_terms/pallas_call | solution.py:421
  164.7 4.8 %weight_terms.3 = (bf16[4,672,256]{2,1,0:T(8,128)(2,1)}, bf16[4,672,256]{2,1,0:T(8,128)(2,1)S(1)}) custom-call(s32[5]{0:T(128)S(1)} %broadcast_add_fusion.2.info, bf16[512,256]{1,0:T(8,128)(2,1)S(1)} %get-tuple-element.324.grads, bf16[128,5376]{1,0:T(8,128)(2,1)} %get-tuple-element.320.rest_0_, bf16[128,5376]{1,0:T(8,128)(2,1)} %get-tuple-element.321.rest_1_, ...), custom_call_target="tpu_custom_call" | custom-call | tf_op jit(solution)/shard_map/while/body/weight_terms/pallas_call | solution.py:421
  174.2 4.7 %collective-permute-start.1 = (bf16[2,672,128]{2,1,0:T(8,128)(2,1)S(1)}, bf16[2,672,128]{2,1,0:T(8,128)(2,1)S(1)}, u32[]{:S(2)}, u32[]{:S(2)}) collective-permute-start(bf16[2,672,128]{2,1,0:T(8,128)(2,1)S(1)} %get-tuple-element.266), channel_id=1, source_target_pairs={{0,8},{4,12},{8,0},{12,4},{16,24},{20,28},{24,16},{28,20},{1,9},{5... | collective-permute-start | bytes 1032200 | tf_op jit(solution)/shard_map/while/body/ppermute | solution.py:479
  178.9 3.4 %collective-permute-start.2 = (bf16[2,672,128]{2,1,0:T(8,128)(2,1)S(1)}, bf16[2,672,128]{2,1,0:T(8,128)(2,1)S(1)}, u32[]{:S(2)}, u32[]{:S(2)}) collective-permute-start(bf16[2,672,128]{2,1,0:T(8,128)(2,1)S(1)} %get-tuple-element.267), channel_id=1, source_target_pairs={{0,16},{4,20},{8,24},{12,28},{16,0},{20,4},{24,8},{28,12},{1,17},{... | collective-permute-start | bytes 1032200 | tf_op jit(solution)/shard_map/while/body/ppermute | solution.py:479
  183.9 3.9 %collective-permute-done.1.rest_2_ = bf16[2,672,128]{2,1,0:T(8,128)(2,1)S(1)} collective-permute-done((bf16[2,672,128]{2,1,0:T(8,128)(2,1)S(1)}, bf16[2,672,128]{2,1,0:T(8,128)(2,1)S(1)}, u32[]{:S(2)}, u32[]{:S(2)}) %collective-permute-start.1) | collective-permute-done | bytes 344096 | tf_op jit(solution)/shard_map/while/body/ppermute | solution.py:479
  195.0 3.6 %collective-permute-done.7.rest_3_ = bf16[2,672,128]{2,1,0:T(8,128)(2,1)S(1)} collective-permute-done((bf16[2,672,128]{2,1,0:T(8,128)(2,1)S(1)}, bf16[2,672,128]{2,1,0:T(8,128)(2,1)S(1)}, u32[]{:S(2)}, u32[]{:S(2)}) %collective-permute-start.7) | collective-permute-done | bytes 344096 | tf_op jit(solution)/shard_map/while/body/ppermute | solution.py:479
  202.1 3.4 %collective-permute-done.8.rest_6_ = bf16[1,672,128]{2,1,0:T(8,128)(2,1)S(1)} collective-permute-done((bf16[1,672,128]{2,1,0:T(8,128)(2,1)S(1)}, bf16[1,672,128]{2,1,0:T(8,128)(2,1)S(1)}, u32[]{:S(2)}, u32[]{:S(2)}) %collective-permute-start.8) | collective-permute-done | bytes 172064 | tf_op jit(solution)/shard_map/while/body/ppermute | solution.py:479
  208.5 10.4 %collective-permute-done.37.rest_1_ = bf16[128,5376]{1,0:T(8,128)(2,1)} collective-permute-done((bf16[128,5376]{1,0:T(8,128)(2,1)}, bf16[128,5376]{1,0:T(8,128)(2,1)}, u32[]{:S(2)}, u32[]{:S(2)}) %collective-permute-start.37) | collective-permute-done | bytes 1376288 | tf_op jit(solution)/shard_map/ppermute | solution.py:778
  218.9 4.3 %input_grad.1 = bf16[128,5376]{1,0:T(8,128)(2,1)} custom-call(bf16[128,5376]{1,0:T(8,128)(2,1)} %tokens.1, f32[1,5376]{1,0:T(1,128)} %broadcast_in_dim.35.gain, bf16[128,5376]{1,0:T(8,128)(2,1)} %get-tuple-element.146.rest_0_, bf16[128,5376]{1,0:T(8,128)(2,1)} %collective-permute-done.37.rest_1_), custom_call_target="tpu_custom_call" | custom-call | bytes 5505024 | tf_op jit(solution)/shard_map/input_grad/pallas_call | solution.py:664
  (139 shorter events, 76.3 us)
Async XLA Ops:
  1.9 33.0 %collective-permute-start.12 = (bf16[672,512]{1,0:T(8,128)(2,1)S(1)}, bf16[672,512]{1,0:T(8,128)(2,1)}, u32[]{:S(2)}, u32[]{:S(2)}) collective-permute-start(bf16[672,512]{1,0:T(8,128)(2,1)S(1)} %pad_maximum_fusion), channel_id=1, source_target_pairs={{0,1},{1,0},{2,3},{3,2},{4,5},{5,4},{6,7},{7,6},{8,9},{9,8},{10,11... | collective-permute-start | bytes 2064392 | tf_op jit(solution)/shard_map/ppermute | solution.py:778
  4.9 62.5 %collective-permute-start.11 = (bf16[128,5376]{1,0:T(8,128)(2,1)}, bf16[128,5376]{1,0:T(8,128)(2,1)}, u32[]{:S(2)}, u32[]{:S(2)}) collective-permute-start(bf16[128,5376]{1,0:T(8,128)(2,1)} %tokens.1), channel_id=1, source_target_pairs={{0,2},{1,3},{2,0},{3,1},{4,6},{5,7},{6,4},{7,5},{8,10},{9,11},{10,... | collective-permute-start | bytes 4128776 | tf_op jit(solution)/shard_map/ppermute | solution.py:778
  34.9 16.8 %collective-permute-start.14 = (bf16[672,512]{1,0:T(8,128)(2,1)}, bf16[672,512]{1,0:T(8,128)(2,1)S(1)}, u32[]{:S(2)}, u32[]{:S(2)}) collective-permute-start(bf16[672,512]{1,0:T(8,128)(2,1)} %collective-permute-done.12.rest_0_.rest_4_), channel_id=1, source_target_pairs={{0,8},{4,12},{8,0},{12,4},{16,24},{20,28},{24,16},{28,20},{1,9},{5... | collective-permute-start | bytes 2064392 | tf_op jit(solution)/shard_map/ppermute | solution.py:479
  36.6 16.6 %collective-permute-start.15 = (bf16[672,512]{1,0:T(8,128)(2,1)}, bf16[672,512]{1,0:T(8,128)(2,1)S(1)}, u32[]{:S(2)}, u32[]{:S(2)}) collective-permute-start(bf16[672,512]{1,0:T(8,128)(2,1)} %collective-permute-done.12.rest_0_.rest_4_), channel_id=1, source_target_pairs={{0,16},{4,20},{8,24},{12,28},{16,0},{20,4},{24,8},{28,12},{1,17},{... | collective-permute-start | bytes 2064392 | tf_op jit(solution)/shard_map/ppermute | solution.py:479
  38.1 29.4 %collective-permute-start.18 = (bf16[672,512]{1,0:T(8,128)(2,1)}, bf16[672,512]{1,0:T(8,128)(2,1)S(1)}, u32[]{:S(2)}, u32[]{:S(2)}) collective-permute-start(bf16[672,512]{1,0:T(8,128)(2,1)} %collective-permute-done.12.rest_0_.rest_4_), channel_id=1, source_target_pairs={{0,4},{4,0},{8,12},{12,8},{16,20},{20,16},{24,28},{28,24},{1,5},{5... | collective-permute-start | bytes 2064392 | tf_op jit(solution)/shard_map/ppermute | solution.py:479
  38.1 49.7 %collective-permute-start.25 = (bf16[128,5376]{1,0:T(8,128)(2,1)}, bf16[128,5376]{1,0:T(8,128)(2,1)}, u32[]{:S(2)}, u32[]{:S(2)}) collective-permute-start(bf16[128,5376]{1,0:T(8,128)(2,1)} %get-tuple-element.121.ready), channel_id=1, source_target_pairs={{0,1},{1,0},{2,3},{3,2},{4,5},{5,4},{6,7},{7,6},{8,9},{9,8},{10,11... | collective-permute-start | bytes 4128776 | tf_op jit(solution)/shard_map/ppermute | solution.py:778
  51.8 16.2 %collective-permute-start.16 = (bf16[672,256]{1,0:T(8,128)(2,1)S(1)}, bf16[672,256]{1,0:T(8,128)(2,1)S(1)}, u32[]{:S(2)}, u32[]{:S(2)}) collective-permute-start(bf16[672,256]{1,0:T(8,128)(2,1)S(1)} %slice.12), channel_id=1, source_target_pairs={{0,16},{4,20},{8,24},{12,28},{16,0},{20,4},{24,8},{28,12},{1,17},{... | collective-permute-start | bytes 1032200 | tf_op jit(solution)/shard_map/ppermute | solution.py:479
  53.2 14.8 %collective-permute-start.17 = (bf16[672,256]{1,0:T(8,128)(2,1)S(1)}, bf16[672,256]{1,0:T(8,128)(2,1)}, u32[]{:S(2)}, u32[]{:S(2)}) collective-permute-start(bf16[672,256]{1,0:T(8,128)(2,1)S(1)} %slice.13), channel_id=1, source_target_pairs={{0,8},{4,12},{8,0},{12,4},{16,24},{20,28},{24,16},{28,20},{1,9},{5... | collective-permute-start | bytes 1032200 | tf_op jit(solution)/shard_map/ppermute | solution.py:479
  81.0 13.4 %collective-permute-start.23 = (bf16[256,512]{1,0:T(8,128)(2,1)}, bf16[256,512]{1,0:T(8,128)(2,1)S(1)}, u32[]{:S(2)}, u32[]{:S(2)}) collective-permute-start(bf16[256,512]{1,0:T(8,128)(2,1)} %get-tuple-element.119), channel_id=1, source_target_pairs={{0,1},{1,0},{2,3},{3,2},{4,5},{5,4},{6,7},{7,6},{8,9},{9,8},{10,11... | collective-permute-start | bytes 786440 | tf_op jit(solution)/shard_map/ppermute | solution.py:778
  81.0 13.4 %collective-permute-start.24 = (bf16[256,256]{1,0:T(8,128)(2,1)}, bf16[256,256]{1,0:T(8,128)(2,1)S(1)}, u32[]{:S(2)}, u32[]{:S(2)}) collective-permute-start(bf16[256,256]{1,0:T(8,128)(2,1)} %get-tuple-element.120), channel_id=1, source_target_pairs={{0,1},{1,0},{2,3},{3,2},{4,5},{5,4},{6,7},{7,6},{8,9},{9,8},{10,11... | collective-permute-start | bytes 393224 | tf_op jit(solution)/shard_map/ppermute | solution.py:778
  83.0 16.7 %collective-permute-start.27 = (bf16[128,512]{1,0:T(8,128)(2,1)}, bf16[128,512]{1,0:T(8,128)(2,1)S(1)}, u32[]{:S(2)}, u32[]{:S(2)}) collective-permute-start(bf16[128,512]{1,0:T(8,128)(2,1)} %get-tuple-element.123.rest_10_), channel_id=1, source_target_pairs={{0,8},{4,12},{8,16},{12,20},{16,24},{20,28},{1,9},{5,13},{9,17},{1... | collective-permute-start | bytes 393224 | tf_op jit(solution)/shard_map/ppermute | solution.py:714
  86.4 13.3 %collective-permute-start.29 = (bf16[128,512]{1,0:T(8,128)(2,1)}, bf16[128,512]{1,0:T(8,128)(2,1)S(1)}, u32[]{:S(2)}, u32[]{:S(2)}) collective-permute-start(bf16[128,512]{1,0:T(8,128)(2,1)} %get-tuple-element.123.rest_10_), channel_id=1, source_target_pairs={{0,4},{4,8},{8,12},{12,16},{16,20},{20,24},{24,28},{1,5},{5,9},{9,... | collective-permute-start | bytes 393224 | tf_op jit(solution)/shard_map/ppermute | solution.py:714
  98.4 58.6 %collective-permute-start.36 = (bf16[128,5376]{1,0:T(8,128)(2,1)}, bf16[128,5376]{1,0:T(8,128)(2,1)}, u32[]{:S(2)}, u32[]{:S(2)}) collective-permute-start(bf16[128,5376]{1,0:T(8,128)(2,1)} %get-tuple-element.141), channel_id=1, source_target_pairs={{0,1},{1,0},{2,3},{3,2},{4,5},{5,4},{6,7},{7,6},{8,9},{9,8},{10,11... | collective-permute-start | bytes 4128776 | tf_op jit(solution)/shard_map/ppermute | solution.py:778
  111.8 12.9 %collective-permute-start.30 = (bf16[512,256]{1,0:T(8,128)(2,1)}, bf16[512,256]{1,0:T(8,128)(2,1)S(1)}, u32[]{:S(2)}, u32[]{:S(2)}) collective-permute-start(bf16[512,256]{1,0:T(8,128)(2,1)} %get-tuple-element.125), channel_id=1, source_target_pairs={{8,0},{12,4},{16,8},{20,12},{24,16},{28,20},{9,1},{13,5},{17,9},{2... | collective-permute-start | bytes 786440 | tf_op jit(solution)/shard_map/ppermute | solution.py:724
  113.1 11.6 %collective-permute-start.31 = (bf16[512,256]{1,0:T(8,128)(2,1)}, bf16[512,256]{1,0:T(8,128)(2,1)S(1)}, u32[]{:S(2)}, u32[]{:S(2)}) collective-permute-start(bf16[512,256]{1,0:T(8,128)(2,1)} %get-tuple-element.126), channel_id=1, source_target_pairs={{4,0},{8,4},{12,8},{16,12},{20,16},{24,20},{28,24},{5,1},{9,5},{13... | collective-permute-start | bytes 786440 | tf_op jit(solution)/shard_map/ppermute | solution.py:724
  121.9 14.2 %collective-permute-start.33 = (bf16[512,256]{1,0:T(8,128)(2,1)}, bf16[512,256]{1,0:T(8,128)(2,1)S(1)}, u32[]{:S(2)}, u32[]{:S(2)}) collective-permute-start(bf16[512,256]{1,0:T(8,128)(2,1)} %get-tuple-element.133), channel_id=1, source_target_pairs={{8,0},{12,4},{16,8},{20,12},{24,16},{28,20},{9,1},{13,5},{17,9},{2... | collective-permute-start | bytes 786440 | tf_op jit(solution)/shard_map/ppermute | solution.py:724
  123.2 12.9 %collective-permute-start.34 = (bf16[512,256]{1,0:T(8,128)(2,1)}, bf16[512,256]{1,0:T(8,128)(2,1)}, u32[]{:S(2)}, u32[]{:S(2)}) collective-permute-start(bf16[512,256]{1,0:T(8,128)(2,1)} %get-tuple-element.134), channel_id=1, source_target_pairs={{4,0},{8,4},{12,8},{16,12},{20,16},{24,20},{28,24},{5,1},{9,5},{13... | collective-permute-start | bytes 786440 | tf_op jit(solution)/shard_map/ppermute | solution.py:724
  155.1 63.8 %collective-permute-start.37 = (bf16[128,5376]{1,0:T(8,128)(2,1)}, bf16[128,5376]{1,0:T(8,128)(2,1)}, u32[]{:S(2)}, u32[]{:S(2)}) collective-permute-start(bf16[128,5376]{1,0:T(8,128)(2,1)} %get-tuple-element.138), channel_id=1, source_target_pairs={{0,2},{1,3},{2,0},{3,1},{4,6},{5,7},{6,4},{7,5},{8,10},{9,11},{10,... | collective-permute-start | bytes 4128776 | tf_op jit(solution)/shard_map/ppermute | solution.py:778
  169.4 12.9 %collective-permute-start.5 = (bf16[4,672,256]{2,1,0:T(8,128)(2,1)}, bf16[4,672,256]{2,1,0:T(8,128)(2,1)S(1)}, u32[]{:S(2)}, u32[]{:S(2)}) collective-permute-start(bf16[4,672,256]{2,1,0:T(8,128)(2,1)} %get-tuple-element.273), channel_id=1, source_target_pairs={{0,4},{4,0},{8,12},{12,8},{16,20},{20,16},{24,28},{28,24},{1,5},{5... | collective-permute-start | bytes 4128776 | tf_op jit(solution)/shard_map/while/body/ppermute | solution.py:479
  174.2 13.6 %collective-permute-start.1 = (bf16[2,672,128]{2,1,0:T(8,128)(2,1)S(1)}, bf16[2,672,128]{2,1,0:T(8,128)(2,1)S(1)}, u32[]{:S(2)}, u32[]{:S(2)}) collective-permute-start(bf16[2,672,128]{2,1,0:T(8,128)(2,1)S(1)} %get-tuple-element.266), channel_id=1, source_target_pairs={{0,8},{4,12},{8,0},{12,4},{16,24},{20,28},{24,16},{28,20},{1,9},{5... | collective-permute-start | bytes 1032200 | tf_op jit(solution)/shard_map/while/body/ppermute | solution.py:479
  178.9 12.3 %collective-permute-start.2 = (bf16[2,672,128]{2,1,0:T(8,128)(2,1)S(1)}, bf16[2,672,128]{2,1,0:T(8,128)(2,1)S(1)}, u32[]{:S(2)}, u32[]{:S(2)}) collective-permute-start(bf16[2,672,128]{2,1,0:T(8,128)(2,1)S(1)} %get-tuple-element.267), channel_id=1, source_target_pairs={{0,16},{4,20},{8,24},{12,28},{16,0},{20,4},{24,8},{28,12},{1,17},{... | collective-permute-start | bytes 1032200 | tf_op jit(solution)/shard_map/while/body/ppermute | solution.py:479
  183.6 11.3 %collective-permute-start.6 = (bf16[2,672,128]{2,1,0:T(8,128)(2,1)S(1)}, bf16[2,672,128]{2,1,0:T(8,128)(2,1)S(1)}, u32[]{:S(2)}, u32[]{:S(2)}) collective-permute-start(bf16[2,672,128]{2,1,0:T(8,128)(2,1)S(1)} %get-tuple-element.276), channel_id=1, source_target_pairs={{0,8},{4,12},{8,0},{12,4},{16,24},{20,28},{24,16},{28,20},{1,9},{5... | collective-permute-start | bytes 1032200 | tf_op jit(solution)/shard_map/while/body/ppermute | solution.py:479
  183.8 14.7 %collective-permute-start.7 = (bf16[2,672,128]{2,1,0:T(8,128)(2,1)S(1)}, bf16[2,672,128]{2,1,0:T(8,128)(2,1)S(1)}, u32[]{:S(2)}, u32[]{:S(2)}) collective-permute-start(bf16[2,672,128]{2,1,0:T(8,128)(2,1)S(1)} %get-tuple-element.277), channel_id=1, source_target_pairs={{0,16},{4,20},{8,24},{12,28},{16,0},{20,4},{24,8},{28,12},{1,17},{... | collective-permute-start | bytes 1032200 | tf_op jit(solution)/shard_map/while/body/ppermute | solution.py:479
  192.0 10.0 %collective-permute-start.3 = (bf16[1,672,128]{2,1,0:T(8,128)(2,1)S(1)}, bf16[1,672,128]{2,1,0:T(8,128)(2,1)S(1)}, u32[]{:S(2)}, u32[]{:S(2)}) collective-permute-start(bf16[1,672,128]{2,1,0:T(8,128)(2,1)S(1)} %get-tuple-element.270), channel_id=1, source_target_pairs={{0,16},{4,20},{8,24},{12,28},{16,0},{20,4},{24,8},{28,12},{1,17},{... | collective-permute-start | bytes 516104 | tf_op jit(solution)/shard_map/while/body/ppermute | solution.py:479
  (37 other events, 230.7 us)
